TPU v7x, 512 devices: a whole 4x8x8 slice. The times are simulated.
512 devices in a mesh: dp: 32 (over z_lo, y), fac: 16 (over x, z_hi, core).
Axes of the slice: x: 4, y: 8, z: 8 (z_hi: 2, z_lo: 4; z = z_hi * 4 + z_lo), core: 2. Of those that a mesh axis runs over, the one named last changes fastest.
Arguments:
- activations: bfloat16 [2048, 5120], P('fac', 'dp'), may hold values from -6 to 6
- output_grads: bfloat16 [2048, 13824], P('fac', 'dp'), may hold values from -6 to 6
- input_prior: float32 [5120, 5120], P('fac', 'dp'), as said below
- gradient_prior: float32 [13824, 13824], P('fac', 'dp'), as said below
- input_inverse: bfloat16 [5120, 5120], P('fac', 'dp'), as said below
- gradient_inverse: bfloat16 [13824, 13824], P('fac', 'dp'), as said below
Outputs:
- input_factor: float32 [5120, 5120], P('fac', 'dp')
- gradient_factor: float32 [13824, 13824], P('fac', 'dp')
- preconditioned: bfloat16 [5120, 13824], P('fac', 'dp')
Inputs may be any that keep to these rules, and one draw needn't show every extreme that they name: `input_prior`: symmetric. `gradient_prior`: symmetric. `input_inverse`: symmetric. `gradient_inverse`: symmetric.
All inputs are finite; a program needn't handle non-finite values.
Results may differ from a plain program's by a relative error of at most 0.0057.
Values may be sent and summed in bfloat16 or wider, within the bound.
No kernel may reach another device: no remote copies, remote signals or barrier semaphores. Data moves between devices by JAX's collectives and lax.ppermute only.
A program may use at most 64 MiB of HBM per device.

v0:
```python
import jax
import jax.numpy as jnp
from jax import lax
from jax.sharding import PartitionSpec as P

decay_rate = 0.95


def local(activations, output_grads, input_prior, gradient_prior, input_inverse, gradient_inverse):
    fac_count = lax.axis_size("fac")
    slice_rows = activations.shape[0] // lax.axis_size("dp")
    input_columns, gradient_columns = (
        lax.all_gather(activations, "fac", axis=0, tiled=True),
        lax.all_gather(output_grads, "fac", axis=0, tiled=True),
    )
    tokens = input_columns.shape[0]
    input_parts, gradient_parts = (
        lax.all_to_all(
            lax.all_to_all(activations, "dp", split_axis=0, concat_axis=1, tiled=True),
            "fac",
            split_axis=1,
            concat_axis=0,
            tiled=True,
        ),
        lax.all_to_all(
            lax.all_to_all(output_grads, "dp", split_axis=0, concat_axis=1, tiled=True),
            "fac",
            split_axis=1,
            concat_axis=0,
            tiled=True,
        ),
    )
    input_parts = input_parts.reshape(fac_count, slice_rows, input_parts.shape[1])
    gradient_parts = gradient_parts.reshape(fac_count, slice_rows, gradient_parts.shape[1])
    input_gathered, gradient_gathered = (
        lax.all_gather(input_parts, "dp", axis=1, tiled=True),
        lax.all_gather(gradient_parts, "dp", axis=1, tiled=True),
    )
    input_panel = input_gathered.reshape(tokens, input_gathered.shape[2])
    gradient_panel = gradient_gathered.reshape(tokens, gradient_gathered.shape[2])
    weight_new = (1.0 - decay_rate) / tokens
    input_factor = decay_rate * input_prior + weight_new * jnp.einsum(
        "tp,tq->pq", input_panel, input_columns, preferred_element_type=jnp.float32
    )
    gradient_factor = decay_rate * gradient_prior + weight_new * jnp.einsum(
        "tp,tq->pq", gradient_panel, gradient_columns, preferred_element_type=jnp.float32
    )
    left_partial = jnp.einsum(
        "tk,sk->ts", input_columns, input_inverse, preferred_element_type=jnp.float32
    )
    left_side = lax.psum(left_partial, "dp").astype(jnp.bfloat16)
    right_rows = lax.psum_scatter(
        jnp.dot(gradient_panel, gradient_inverse, preferred_element_type=jnp.float32),
        "fac",
        scatter_dimension=0,
        tiled=True,
    ).astype(jnp.bfloat16)
    product = jnp.einsum(
        "ts,tq->sq",
        left_side,
        lax.all_gather(right_rows, "fac", axis=0, tiled=True),
        preferred_element_type=jnp.float32,
    )
    preconditioned = (product / tokens).astype(jnp.bfloat16)
    return (input_factor, gradient_factor, preconditioned)


def solution(mesh):
    placed = (
        P("fac", "dp"),
        P("fac", "dp"),
        P("fac", "dp"),
        P("fac", "dp"),
        P("fac", "dp"),
        P("fac", "dp"),
    )
    return jax.shard_map(
        local,
        mesh=mesh,
        in_specs=placed,
        out_specs=(P("fac", "dp"), P("fac", "dp"), P("fac", "dp")),
        check_vma=False,
    )
```

profile of v0, /device:TPU:1, one launch (start us, length us, event | category | flops | bytes accessed | tf_op | source)
XLA Modules:
  0.0 622.5 jit_solution(6988160393048392964)
XLA Ops:
  7.2 0.0 all-gather.7.cloned.1.call-start
  7.2 1.1 copy.20
  8.3 22.6 %all_to_all.64 = bf16[32,4,432]{2,1,0:T(4,128)(2,1)S(1)} all-to-all(bf16[32,4,432]{2,1,0:T(4,128)(2,1)S(1)} %all_to_all.54), channel_id=1, replica_groups=mesh['dp'=32,'fac'=16] {'dp'}, dimensions={0} | all-to-all | bytes 221184 | tf_op jit(solution)/shard_map/all_to_all | solution.py:26
  31.0 0.1 all_to_all.57
  31.2 21.9 %all_to_all.65 = bf16[4,16,864]{2,0,1:T(4,128)(2,1)S(1)} all-to-all(bf16[4,16,864]{2,0,1:T(4,128)(2,1)S(1)} %copy.22), channel_id=1, replica_groups=mesh['dp'=32,'fac'=16] {'fac'}, dimensions={1} | all-to-all | bytes 221184 | tf_op jit(solution)/shard_map/all_to_all | solution.py:25
  53.1 0.7 copy.23
  53.7 0.0 reduce-scatter.2.cloned.1.call-start
  53.8 129.9 %all-gather.7.cloned.1.call-done = bf16[16,128,864]{2,0,1:T(8,128)(2,1)} async-done(((bf16[16,4,864]{2,0,1:T(8,128)(2,1)}), bf16[16,128,864]{2,0,1:T(8,128)(2,1)}) %all-gather.7.cloned.1.call-update) | async-done | bytes 3538960 | tf_op jit(solution)/shard_map/all_gather | solution.py:37
  183.7 7.1 %copy.24 = bf16[16,128,864]{1,0,2:T(8,128)(2,1)} copy(bf16[16,128,864]{2,0,1:T(8,128)(2,1)} %all-gather.7.cloned.1.call-done) | data formatting | bytes 7077888 | tf_op jit(solution)/shard_map/all_gather | solution.py:37
  190.8 5.8 fusion
  196.6 0.0 all-gather.5.cloned.1.call-start
  196.7 0.7 copy-done.4
  197.4 0.1 copy.15
  197.5 14.4 %all_to_all.66 = bf16[32,4,160]{2,1,0:T(4,128)(2,1)S(1)} all-to-all(bf16[32,4,160]{2,1,0:T(4,128)(2,1)S(1)} %all_to_all.48), channel_id=1, replica_groups=mesh['dp'=32,'fac'=16] {'dp'}, dimensions={0} | all-to-all | bytes 81920 | tf_op jit(solution)/shard_map/all_to_all | solution.py:19
  212.0 0.1 all_to_all.51
  212.1 38.8 %all_to_all.67 = bf16[4,16,320]{2,0,1:T(4,128)(2,1)S(1)} all-to-all(bf16[4,16,320]{2,0,1:T(4,128)(2,1)S(1)} %copy.17), channel_id=1, replica_groups=mesh['dp'=32,'fac'=16] {'fac'}, dimensions={1} | all-to-all | bytes 81920 | tf_op jit(solution)/shard_map/all_to_all | solution.py:18
  250.9 0.6 copy.18
  251.6 0.0 all-gather.9.cloned.1.call-start
  251.6 0.5 all-gather.9.cloned.1.call-update
  252.2 0.0 all-gather.11.cloned.1.call-start
  252.2 38.6 %all_gather.16 = bf16[2048,160]{0,1:T(8,128)(2,1)S(1)} all-gather(bf16[128,160]{0,1:T(8,128)(2,1)S(1)} %copy-done.4), channel_id=1, replica_groups=mesh['dp'=32,'fac'=16] {'fac'}, dimensions={0}, use_global_device_ids=true | all-gather | bytes 696320 | tf_op jit(solution)/shard_map/all_gather | solution.py:13
  290.8 0.8 copy-done.1
  291.7 0.6 fusion.25
  292.2 33.3 %reduce-scatter.2.cloned.1.call-done = f32[128,432]{0,1:T(8,128)} async-done(((f32[2048,432]{0,1:T(8,128)}), f32[128,432]{0,1:T(8,128)}) %reduce-scatter.2.cloned.1.call-update) | async-done | bytes 221200 | tf_op jit(solution)/shard_map/reduce_scatter | solution.py:52
  325.6 1.6 convert_element_type.10
  327.2 162.8 %all-reduce.1 = bf16[2048,320]{0,1:T(8,128)(2,1)} all-reduce(f32[2048,320]{0,1:T(8,128)S(1)} %fusion.25), channel_id=1, replica_groups=mesh['dp'=32,'fac'=16] {'dp'}, use_global_device_ids=true, to_apply=%region_0.0 | all-reduce | flops 655360 | bytes 3932160 | tf_op jit(solution)/shard_map/psum | solution.py:51
  490.0 2.7 copy.19
  492.6 1.4 fusion.22
  494.0 52.4 %all-gather.9.cloned.1.call-done = bf16[2048,432]{0,1:T(8,128)(2,1)} async-done(((bf16[128,432]{0,1:T(8,128)(2,1)}), bf16[2048,432]{0,1:T(8,128)(2,1)}) %all-gather.9.cloned.1.call-update) | async-done | bytes 1769488 | tf_op jit(solution)/shard_map/all_gather | solution.py:14
  546.4 6.2 multiply_add_fusion
  552.6 60.2 %all-gather.11.cloned.1.call-done = bf16[2048,432]{0,1:T(8,128)(2,1)} async-done(((bf16[128,432]{0,1:T(8,128)(2,1)}), bf16[2048,432]{0,1:T(8,128)(2,1)}) %all-gather.11.cloned.1.call-update) | async-done | bytes 1769488 | tf_op jit(solution)/shard_map/all_gather | solution.py:61
  612.9 3.1 fusion.16
  (23 shorter events, 0.3 us)
Async XLA Ops:
  7.2 183.7 %copy-start = (bf16[864,432]{0,1:T(8,128)(2,1)S(1)}, bf16[864,432]{0,1:T(8,128)(2,1)}, u32[]{:S(2)}) copy-start(bf16[864,432]{0,1:T(8,128)(2,1)} %param.11) | copy-start | bytes 2239492
  7.2 176.6 %all-gather.7.cloned.1.call-start = ((), (), s32[]{:S(2)}) async-start(), calls=%async_computation.6 | async-start | bytes 3784704 | tf_op jit(solution)/shard_map/all_gather | solution.py:37
  53.7 271.8 %reduce-scatter.2.cloned.1.call-start = ((), (), s32[]{:S(2)}) async-start(), calls=%async_computation.8 | async-start | bytes 3760128 | tf_op jit(solution)/shard_map/reduce_scatter | solution.py:52
  196.6 0.8 copy-start.4
  196.6 95.1 %copy-start.5 = (bf16[320,160]{0,1:T(8,128)(2,1)S(1)}, bf16[320,160]{0,1:T(8,128)(2,1)}, u32[]{:S(2)}) copy-start(bf16[320,160]{0,1:T(8,128)(2,1)} %param.10) | copy-start | bytes 307204
  196.6 293.3 %all-gather.5.cloned.1.call-start = ((), (), s32[]{:S(2)}) async-start(), calls=%async_computation.5 | async-start | bytes 1622016 | tf_op jit(solution)/shard_map/all_gather | solution.py:36
  251.6 294.9 %all-gather.9.cloned.1.call-start = ((), (), s32[]{:S(2)}) async-start(), calls=%async_computation.7 | async-start | bytes 1880064 | tf_op jit(solution)/shard_map/all_gather | solution.py:14
  252.2 360.7 %all-gather.11.cloned.1.call-start = ((), (), s32[]{:S(2)}) async-start(), calls=%async_computation.9 | async-start | bytes 1880064 | tf_op jit(solution)/shard_map/all_gather | solution.py:61
  290.8 0.8 copy-start.1
  489.9 2.7 copy-start.2
  489.9 2.7 copy-start.6
  494.0 118.9 %copy-start.3 = (bf16[2048,320]{0,1:T(8,128)(2,1)S(1)}, bf16[2048,320]{0,1:T(8,128)(2,1)}, u32[]{:S(2)}) copy-start(bf16[2048,320]{0,1:T(8,128)(2,1)} %all-reduce.1) | copy-start | bytes 3932164
Sparse Core Ops, SparseCore 0:
  53.9 129.8 all-gather.6
  196.7 128.7 reduce-scatter.1
  328.4 132.6 all-gather.4
  464.5 81.8 all-gather.8
  550.5 62.3 all-gather.10
where the time goes:
time: 623 us; the launch traced here: 622 us
  blocking collectives  299 us (48%)
  waiting for transfers between devices  277 us (44%)
  matrix products  16.9 us (3%)
  local copies, waits for them, and re-layouts  14.2 us (2%)
  between operations  13.9 us (2%)
    psum x1, blocking collectives, local(): left_side = lax.psum(left_partial, 'dp').astype(jnp.bfloat16)  163 us
    all_gather x1, waiting for transfers between devices, local(): lax.all_gather(gradient_parts, 'dp', axis=1, tiled=True)  130 us
    all_gather x1, waiting for transfers between devices, local(): lax.all_gather(right_rows, 'fac', axis=0, tiled=True)  60.2 us
    all_gather x1, waiting for transfers between devices, local(): lax.all_gather(output_grads, 'fac', axis=0, tiled=True)  52.4 us
    all_to_all x1, blocking collectives, local(): lax.all_to_all(lax.all_to_all(activations, 'dp', split_axis=0, concat_axi...  38.8 us
    all_gather x1, blocking collectives, local(): lax.all_gather(activations, 'fac', axis=0, tiled=True)  38.6 us
    reduce_scatter x1, waiting for transfers between devices, local(): lax.psum_scatter(jnp.dot(gradient_panel, gradient_inverse, preferred_elem...  33.3 us
    all_to_all x1, blocking collectives, local(): lax.all_to_all(output_grads, 'dp', split_axis=0, concat_axis=1, tiled=True)  22.6 us
  transfers between devices with their start and end apart: 5, of which 4 were waited for; matrix products, arithmetic and copies ran while one was open for 2% of the time, Pallas kernels for 0%

commit v1 on v0

v1 whole, which is shorter than its diff:
```python
import functools
import jax
import jax.numpy as jnp
from jax import lax
from jax.experimental import pallas as pl
from jax.experimental.pallas import tpu as pltpu
from jax.sharding import Mesh, PartitionSpec as P

decay_rate = 0.95
VMEM = pl.BlockSpec(memory_space=pltpu.VMEM)
f32, bf16 = jnp.float32, jnp.bfloat16
shape = jax.ShapeDtypeStruct
AXES = ("zg", "p", "y", "xh", "xl", "w", "core")
SIZES = (2, 2, 8, 2, 2, 2, 2)
X = ("xh", "xl")
PANELS = 4
RING = 8


def device(zg, p, y, xh, xl, w, core):
    n = 0
    for size, at in zip(SIZES, (zg, p, y, xh, xl, w, core)):
        n = n * size + at
    return n


def coordinates():
    for n in range(512):
        out = []
        for size in SIZES[::-1]:
            out.append(n % size)
            n //= size
        yield out[::-1]


def panel_perm(flip):
    return [
        (
            device(zg, p, y, xh, xl, w, core),
            device(xh ^ flip, xl, PANELS * w + y % PANELS, zg, p, y // PANELS, core),
        )
        for zg, p, y, xh, xl, w, core in coordinates()
    ]


def piece_perm():
    return [
        (
            device(zg, p, y, xh, xl, w, core),
            device(xh, p, PANELS * w + y % PANELS, zg, xl, y // PANELS, core),
        )
        for zg, p, y, xh, xl, w, core in coordinates()
    ]


def column_perm():
    return [
        (
            device(zg, p, y, xh, xl, w, core),
            device(zg, p, y, xh, xl, w, core) if xl == p else device(zg, 1 - p, y, xh, 1 - xl, w, core),
        )
        for zg, p, y, xh, xl, w, core in coordinates()
    ]


def swap(x, axis):
    return lax.ppermute(x, axis, [(0, 1), (1, 0)])


def shift(x, axis, size, by):
    return lax.ppermute(x, axis, [(i, (i + by) % size) for i in range(size)])


def after(x, *others):
    return lax.optimization_barrier((x, *others))[0]


def dot(a, b, dims):
    return lax.dot_general(a, b, (dims, ((), ())), preferred_element_type=f32)


def call(kernel, out, flops, *args, scratch=()):
    size = sum(a.size * a.dtype.itemsize for a in (*args, *jax.tree.leaves(out)))
    return pl.pallas_call(
        kernel,
        out_shape=out,
        in_specs=[VMEM] * len(args),
        out_specs=jax.tree.map(lambda _: VMEM, out),
        scratch_shapes=list(scratch),
        compiler_params=pltpu.CompilerParams(vmem_limit_bytes=24 * 1024 * 1024),
        cost_estimate=pl.CostEstimate(flops=flops, bytes_accessed=size, transcendentals=0),
    )(*args)


def packed_shape(da, dg, h):
    return dg + da // 2, -(-dg * h // 128) * 128


def small_at(da, dg, h):
    lane = -(-da * h // 128) * 128
    return [
        (slice(i * da // 2, (i + 1) * da // 2), slice(dg, dg + da // 2), slice(i * lane, i * lane + da * h))
        for i in range(2)
    ]


def pack_kernel(small, big, out):
    da, dg = small.shape[0], big.shape[0]
    h = big.shape[1] // dg
    out[...] = jnp.zeros_like(out)
    out[:dg, : big.shape[1]] = big[...]
    for rows, to, lanes in small_at(da, dg, h):
        out[to, lanes] = small[rows, :]


def sides_kernel(da, dg, h, *refs):
    ring, inverses = refs[: RING + 1], refs[RING + 1 : RING + 5]
    rows, own, s1, s2, s3, acc = refs[RING + 5 :]
    core, zg, p, y = (lax.axis_index(a) for a in ("core", "zg", "p", "y"))
    x = 2 * lax.axis_index("xh") + lax.axis_index("xl")
    width, n = own.shape[1:]
    for offset, ref in zip((0, -1, 1, -2, 2, -3, 3), ring):
        at = lax.rem(y + offset + RING, RING)
        for slot in range(2):
            rows[at, lax.bitwise_xor(zg, slot)] = ref[slot]
    for slot in range(2):
        rows[lax.rem(y + 4, RING), lax.bitwise_xor(zg, slot)] = ring[RING - 1 + slot][...]
    big = [ref[:dg, : dg * h] for ref in inverses]
    small = [
        jnp.concatenate([ref[at, lanes] for _, at, lanes in small_at(da, dg, h)], 0) for ref in inverses
    ]
    for w in range(2):

        def panel(first, lo, hi):
            return jnp.concatenate(
                [
                    jnp.concatenate([rows[PANELS * w + first + m, xh, lo:hi, :] for m in range(h)], 0)
                    for xh in range(2)
                ],
                1,
            )

        for lo, hi, blocks in ((0, da, small), (da, width, big)):
            mine, other = panel(core * h, lo, hi), panel((1 - core) * h, lo, hi)
            for q in range(2):
                total = dot(blocks[2 * q], mine, ((1,), (0,))) + dot(blocks[2 * q + 1], other, ((1,), (0,)))
                for xh in range(2):
                    acc[2 * xh + lax.bitwise_xor(p, q), w, lo:hi, :] = total[:, xh * n : (xh + 1) * n]
    own[...] = acc[x]
    for ahead, ref in enumerate((s1, s2, s3)):
        ref[...] = acc[lax.rem(x + ahead + 1, 4)].astype(ref.dtype)


def first_sum_kernel(da, own, r1, r2, r3, keep, send):
    w = lax.axis_index("w")
    dg = own.shape[1] - da
    keep[...] = ((own[...] + r1[...].astype(f32)) + r2[...].astype(f32)) + r3[...].astype(f32)
    for t in range(2):
        send[t * dg : (t + 1) * dg, :] = keep[t, da:, :].astype(send.dtype)
    send[2 * dg :, :] = keep[1 - w, :da, :].astype(send.dtype)


def second_sum_kernel(da, keep, got, left, right):
    w = lax.axis_index("w")
    dg = right.shape[1]
    for t in range(2):
        right[t] = (keep[t, da:, :] + got[t * dg : (t + 1) * dg, :].astype(f32)).astype(right.dtype)
    left[...] = (keep[w, :da, :] + got[2 * dg :, :].astype(f32)).astype(left.dtype)


def factor_kernel(da, dg, h, weight, rows, cols, ip, gp, i_own, g_own, keep, send):
    core, p, w = (lax.axis_index(a) for a in ("core", "p", "w"))
    keep[...] = jnp.zeros_like(keep)
    send[...] = jnp.zeros_like(send)

    def panel(k, lo, hi):
        return jnp.concatenate([rows[PANELS * t + k, xh, lo:hi, :] for xh in range(2) for t in range(2)], 1)

    def columns(xl, lo, hi):
        return jnp.concatenate(
            [cols[2 * xh + xl, lax.bitwise_xor(w, t), lo:hi, :] for xh in range(2) for t in range(2)], 1
        )

    for lo, hi, prior, own in ((0, da, ip, i_own), (da, da + dg, gp, g_own)):
        n = hi - lo
        here, there = columns(p, lo, hi), columns(1 - p, lo, hi)
        for m in range(h):
            at = slice(m * n, (m + 1) * n)
            parts = [
                weight * dot(c, panel(first * h + m, lo, hi), ((1,), (1,)))
                for first in (core, 1 - core)
                for c in (here, there)
            ]
            own[:, at] = decay_rate * prior[:, at] + parts[0]
            for ref, part in ((keep, parts[1]), (send.at[0], parts[2]), (send.at[1], parts[3])):
                if lo:
                    ref[:dg, at] = part.astype(ref.dtype)
                else:
                    for src, to, lanes in small_at(da, dg, h):
                        lane = slice(lanes.start + m * n, lanes.start + (m + 1) * n)
                        ref[to, lane] = part[src, :].astype(ref.dtype)


def factor_sum_kernel(da, dg, h, i_own, g_own, got, last, i_out, g_out):
    def total(at, lanes):
        return got[0, at, lanes].astype(f32) + last[at, lanes].astype(f32)

    g_out[...] = g_own[...] + total(slice(0, dg), slice(0, dg * h))
    for src, at, lanes in small_at(da, dg, h):
        i_out[src, :] = i_own[src, :] + total(at, lanes)


def product_kernel(h, scale, left, right, r1, r2, r3, own, keep, send, held):
    core, p = lax.axis_index("core"), lax.axis_index("p")
    x = 2 * lax.axis_index("xh") + lax.axis_index("xl")
    n = left.shape[1]
    for behind, ref in enumerate((right, r1, r2, r3)):
        held[lax.rem(x - behind + 4, 4)] = ref[...]

    def columns(xl):
        return jnp.concatenate([held[2 * xh + xl, t] for xh in range(2) for t in range(2)], 1)

    here, there = columns(p), columns(1 - p)
    for first, outs in ((1 - core, (send.at[0], send.at[1])), (core, (own, keep))):
        for m in range(h):
            panel = jnp.concatenate([left[PANELS * b + first * h + m] for b in range(4)], 1)
            for c, ref in zip((here, there), outs):
                ref[m * n : (m + 1) * n, :] = (dot(panel, c, ((1,), (1,))) * scale).astype(ref.dtype)


def local(activations, output_grads, input_prior, gradient_prior, input_inverse, gradient_inverse):
    da, dg = activations.shape[1], output_grads.shape[1]
    width, block = da + dg, activations.shape[0]
    h = input_prior.shape[0] // da
    tokens = block * 16
    work = 2 * tokens * h * (da * da + dg * dg)
    pair = (2, width, block)
    pack = packed_shape(da, dg, h)

    x = jnp.concatenate([activations.T, output_grads.T], 0)
    u = jnp.stack([lax.ppermute(x, AXES, panel_perm(j)) for j in range(2)])
    up, down = [u], [u]
    for _ in range(3):
        up.append(shift(up[-1], "y", RING, 1))
        down.append(shift(down[-1], "y", RING, -1))
    ring = [u, up[1], down[1], up[2], down[2], up[3], down[3]]
    ring += [shift(up[3][0], "y", RING, 1), shift(down[3][1], "y", RING, -1)]

    inverse = call(
        pack_kernel, shape(pack, bf16), 0, after(input_inverse.T, x), gradient_inverse.T
    )
    inverse = after(inverse, u)
    inverse_z = swap(inverse, "p")
    inverses = [inverse, swap(inverse, "core"), inverse_z, swap(inverse_z, "core")]

    col = lax.ppermute(after(x, u), AXES, column_perm())
    cols = lax.all_gather(jnp.stack([col, swap(col, "w")]), X, axis=0, tiled=False)

    rows, own, *ahead = call(
        functools.partial(sides_kernel, da, dg, h),
        (shape((RING, *pair), bf16), shape(pair, f32)) + (shape(pair, bf16),) * 3,
        work, *ring, *inverses,
        scratch=[pltpu.VMEM((4, *pair), f32)],
    )
    got = [shift(part, X, 4, i + 1) for i, part in enumerate(ahead)]
    keep, send = call(
        functools.partial(first_sum_kernel, da),
        (shape(pair, f32), shape((2 * dg + da, block), bf16)),
        0, own, *got,
    )
    left, right = call(
        functools.partial(second_sum_kernel, da),
        (shape((da, block), bf16), shape((2, dg, block), bf16)),
        0, keep, swap(send, "w"),
    )
    piece = lax.ppermute(left, AXES, piece_perm())
    rights = [shift(right, X, 4, i + 1) for i in range(3)]

    i_own, g_own, f_keep, f_send = call(
        functools.partial(factor_kernel, da, dg, h, (1.0 - decay_rate) / tokens),
        (shape((da, da * h), f32), shape((dg, dg * h), f32), shape(pack, f32), shape((2, *pack), bf16)),
        work, rows, cols, input_prior.T, gradient_prior.T,
    )
    f_got = swap(f_send, "core")
    f_mid = after((f_keep + f_got[1].astype(f32)).astype(bf16), left)
    f_last = swap(f_mid, "p")
    input_factor, gradient_factor = call(
        functools.partial(factor_sum_kernel, da, dg, h),
        (shape((da, da * h), f32), shape((dg, dg * h), f32)),
        0, i_own, g_own, f_got, f_last,
    )

    pieces = jnp.broadcast_to(after(piece, f_mid), (16, *piece.shape))
    lefts = lax.all_to_all(pieces, ("zg", "y"), 0, 0, tiled=True)
    lefts = after(lefts, f_last)
    p_own, p_keep, p_send = call(
        functools.partial(product_kernel, h, 1.0 / tokens),
        (shape((da * h, dg), f32), shape((da * h, dg), f32), shape((2, da * h, dg), bf16)),
        2 * tokens * h * da * dg, lefts, right, *rights,
        scratch=[pltpu.VMEM((4, 2, dg, block), bf16)],
    )
    p_got = swap(p_send, "core")
    p_last = swap((p_keep + p_got[1].astype(f32)).astype(bf16), "p")
    preconditioned = (p_own + p_got[0].astype(f32) + p_last.astype(f32)).astype(bf16)
    return input_factor.T, gradient_factor.T, preconditioned


def solution(mesh):
    split = Mesh(mesh.devices.reshape(SIZES), AXES)
    placed = P(("xh", "xl", "w", "core"), ("zg", "p", "y"))
    return jax.shard_map(
        local,
        mesh=split,
        in_specs=(placed,) * 6,
        out_specs=(placed,) * 3,
        check_vma=False,
    )
```

time: 623 us -> 259 us (0.42)
  blocking collectives: 299 us -> 0 us
  waiting for transfers between devices: 277 us -> 62.6 us
  starting transfers between devices: 0.2 us -> 151 us
  matrix products: 16.9 us -> 0 us
  Pallas kernels: 0 us -> 9.66 us
    all_gather x4 -> x1, waiting for transfers between devices: 243 us -> 0.01 us  [local(): lax.all_gather(jnp.stack([col, swap(col, 'w')]), X, axis=0, tiled=False)]
    psum x1 -> x0, blocking collectives: 163 us -> none  [local(): left_side = lax.psum(left_partial, 'dp').astype(jnp.bfloat16)]
    ppermute x0 -> x27, starting transfers between devices: none -> 134 us  [the longest x9 62 us: swap(): return lax.ppermute(x, axis, [(0, 1), (1, 0)])]
    all_to_all x4 -> x0, blocking collectives: 97.8 us -> none  [the longest x1 38.8 us: local(): lax.all_to_all(lax.all_to_all(activations, 'dp', split_axis=0, concat_axi...]
    ppermute x0 -> x27, waiting for transfers between devices: none -> 62.5 us  [the longest x9 36.2 us: swap(): return lax.ppermute(x, axis, [(0, 1), (1, 0)])]
    all_gather x1 -> x0, blocking collectives: 38.6 us -> none  [local(): lax.all_gather(activations, 'fac', axis=0, tiled=True)]
    reduce_scatter x1 -> x0, waiting for transfers between devices: 33.3 us -> none  [local(): lax.psum_scatter(jnp.dot(gradient_panel, gradient_inverse, preferred_elem...]
    dot_general x5 -> x0, matrix products: 16.9 us -> none  [the longest x1 6.2 us: local(): jnp.einsum('tp,tq->pq', gradient_panel, gradient_columns, preferred_eleme...]
  transfers between devices with their start and end apart: 5 -> 29, of which waited for: 4 -> 12; matrix products, arithmetic and copies ran while one was open for 2% -> 1% of each run, Pallas kernels for 0% -> 2%
where the time goes in v1:
time: 259 us; the launch traced here: 256 us
  starting transfers between devices  151 us (58%)
  waiting for transfers between devices  62.6 us (24%)
  local copies, waits for them, and re-layouts  14.7 us (6%)
  between operations  14.5 us (6%)
  Pallas kernels  9.66 us (4%)
  other arithmetic  3.76 us (1%)
    ppermute x9, starting transfers between devices, swap(): return lax.ppermute(x, axis, [(0, 1), (1, 0)])  62 us
    ppermute x14, starting transfers between devices, shift(): return lax.ppermute(x, axis, [(i, (i + by) % size) for i in range(size)])  61.2 us
    ppermute x9, waiting for transfers between devices, swap(): return lax.ppermute(x, axis, [(0, 1), (1, 0)])  36.2 us
    ppermute x14, waiting for transfers between devices, shift(): return lax.ppermute(x, axis, [(i, (i + by) % size) for i in range(size)])  22 us
    all_to_all x1, starting transfers between devices, local(): lefts = lax.all_to_all(pieces, ('zg', 'y'), 0, 0, tiled=True)  16.9 us
    unnamed x42, local copies, waits for them, and re-layouts  13.7 us
    pallas_call x7, Pallas kernels, call(): pl.pallas_call(kernel, out_shape=out, in_specs=[VMEM] * len(args), out_sp...  9.66 us
    ppermute x2, starting transfers between devices, local(): u = jnp.stack([lax.ppermute(x, AXES, panel_perm(j)) for j in range(2)])  9.47 us
  transfers between devices with their start and end apart: 29, of which 12 were waited for; matrix products, arithmetic and copies ran while one was open for 1% of the time, Pallas kernels for 2%

profile of v1, /device:TPU:1, one launch (start us, length us, event | category | flops | bytes accessed | tf_op | source)
XLA Modules:
  0.0 256.1 jit_solution(8750074528669403399)
XLA Ops:
  8.8 8.8 %collective-permute-start.1 = (bf16[592,128]{1,0:T(8,128)(2,1)S(1)}, bf16[592,128]{1,0:T(8,128)(2,1)S(1)}, u32[]{:S(2)}, u32[]{:S(2)}) collective-permute-start(bf16[592,128]{1,0:T(8,128)(2,1)S(1)} %pad_maximum_fusion.2), channel_id=1, source_target_pairs={{0,256},{1,257},{2,320},{3,321},{4,384},{5,385},{6,448},{7,449},{8... | collective-permute-start | bytes 454664 | tf_op jit(solution)/shard_map/ppermute | solution.py:241
  17.6 4.3 %collective-permute-done.1 = bf16[592,128]{1,0:T(8,128)(2,1)S(1)} collective-permute-done((bf16[592,128]{1,0:T(8,128)(2,1)S(1)}, bf16[592,128]{1,0:T(8,128)(2,1)S(1)}, u32[]{:S(2)}, u32[]{:S(2)}) %collective-permute-start.1) | collective-permute-done | bytes 151584 | tf_op jit(solution)/shard_map/ppermute | solution.py:241
  22.7 30.4 %collective-permute-start.14 = (bf16[592,128]{1,0:T(8,128)(2,1)S(1)}, bf16[592,128]{1,0:T(8,128)(2,1)S(1)}, u32[]{:S(2)}, u32[]{:S(2)}) collective-permute-start(bf16[592,128]{1,0:T(8,128)(2,1)S(1)} %collective-permute-done.13), channel_id=1, source_target_pairs={{0,2},{2,0},{1,3},{3,1},{4,6},{6,4},{5,7},{7,5},{8,10},{10,8},{9,1... | collective-permute-start | bytes 454664 | tf_op jit(solution)/shard_map/ppermute | solution.py:67
  55.2 5.2 %collective-permute-start.11 = (bf16[512,896]{1,0:T(8,128)(2,1)S(1)}, bf16[512,896]{1,0:T(8,128)(2,1)S(1)}, u32[]{:S(2)}, u32[]{:S(2)}) collective-permute-start(bf16[512,896]{1,0:T(8,128)(2,1)S(1)} %shard_map.85.refs_9_), channel_id=1, source_target_pairs={{0,128},{128,0},{1,129},{129,1},{2,130},{130,2},{3,131},{131,3},{4... | collective-permute-start | bytes 2752520 | tf_op jit(solution)/shard_map/ppermute | solution.py:67
  61.2 6.7 %collective-permute-start.2 = (bf16[2,592,128]{2,1,0:T(8,128)(2,1)S(1)}, bf16[2,592,128]{2,1,0:T(8,128)(2,1)S(1)}, u32[]{:S(2)}, u32[]{:S(2)}) collective-permute-start(bf16[2,592,128]{2,1,0:T(8,128)(2,1)S(1)} %pad_maximum_fusion.refs_0_), channel_id=1, source_target_pairs={{0,16},{16,32},{32,48},{48,64},{64,80},{80,96},{96,112},{112,0},{1... | collective-permute-start | bytes 909320 | tf_op jit(solution)/shard_map/ppermute | solution.py:71
  71.6 15.2 %collective-permute-start.4 = (bf16[2,592,128]{2,1,0:T(8,128)(2,1)S(1)}, bf16[2,592,128]{2,1,0:T(8,128)(2,1)S(1)}, u32[]{:S(2)}, u32[]{:S(2)}) collective-permute-start(bf16[2,592,128]{2,1,0:T(8,128)(2,1)S(1)} %collective-permute-done.2.refs_1_), channel_id=1, source_target_pairs={{0,16},{16,32},{32,48},{48,64},{64,80},{80,96},{96,112},{112,0},{1... | collective-permute-start | bytes 909320 | tf_op jit(solution)/shard_map/ppermute | solution.py:71
  90.6 4.1 %collective-permute-start.6 = (bf16[2,592,128]{2,1,0:T(8,128)(2,1)S(1)}, bf16[2,592,128]{2,1,0:T(8,128)(2,1)S(1)}, u32[]{:S(2)}, u32[]{:S(2)}) collective-permute-start(bf16[2,592,128]{2,1,0:T(8,128)(2,1)S(1)} %collective-permute-done.4.refs_3_), channel_id=1, source_target_pairs={{0,16},{16,32},{32,48},{48,64},{64,80},{80,96},{96,112},{112,0},{1... | collective-permute-start | bytes 909320 | tf_op jit(solution)/shard_map/ppermute | solution.py:71
  94.7 6.4 %collective-permute-start.10 = (bf16[512,896]{1,0:T(8,128)(2,1)S(1)}, bf16[512,896]{1,0:T(8,128)(2,1)S(1)}, u32[]{:S(2)}, u32[]{:S(2)}) collective-permute-start(bf16[512,896]{1,0:T(8,128)(2,1)S(1)} %shard_map.85.refs_9_), channel_id=1, source_target_pairs={{0,1},{1,0},{2,3},{3,2},{4,5},{5,4},{6,7},{7,6},{8,9},{9,8},{10,11... | collective-permute-start | bytes 2752520 | tf_op jit(solution)/shard_map/ppermute | solution.py:67
  103.0 2.4 collective-permute-start.7
  105.4 3.6 %collective-permute-start.8 = (bf16[592,128]{1,0:T(8,128)(2,1)S(1)}, bf16[592,128]{1,0:T(8,128)(2,1)S(1)}, u32[]{:S(2)}, u32[]{:S(2)}) collective-permute-start(bf16[592,128]{1,0:T(8,128)(2,1)S(1)} %slice_bitcast_fusion.4), channel_id=1, source_target_pairs={{0,16},{16,32},{32,48},{48,64},{64,80},{80,96},{96,112},{112,0},{1... | collective-permute-start | bytes 454664 | tf_op jit(solution)/shard_map/ppermute | solution.py:71
  109.1 5.1 %collective-permute-done.7.refs_6_ = bf16[2,592,128]{2,1,0:T(8,128)(2,1)S(1)} collective-permute-done((bf16[2,592,128]{2,1,0:T(8,128)(2,1)S(1)}, bf16[2,592,128]{2,1,0:T(8,128)(2,1)S(1)}, u32[]{:S(2)}, u32[]{:S(2)}) %collective-permute-start.7) | collective-permute-done | bytes 303136 | tf_op jit(solution)/shard_map/ppermute | solution.py:71
  114.3 2.5 collective-permute-start.9
  116.8 3.7 %collective-permute-done.9.refs_8_ = bf16[592,128]{1,0:T(8,128)(2,1)S(1)} collective-permute-done((bf16[592,128]{1,0:T(8,128)(2,1)S(1)}, bf16[592,128]{1,0:T(8,128)(2,1)S(1)}, u32[]{:S(2)}, u32[]{:S(2)}) %collective-permute-start.9) | collective-permute-done | bytes 151584 | tf_op jit(solution)/shard_map/ppermute | solution.py:71
  120.6 2.7 %shard_map.86 = (bf16[8,2,592,128]{3,2,1,0:T(8,128)(2,1)S(1)}, f32[2,592,128]{2,1,0:T(8,128)S(1)}, bf16[2,592,128]{2,1,0:T(8,128)(2,1)S(1)}, bf16[2,592,128]{2,1,0:T(8,128)(2,1)S(1)}, bf16[2,592,128]{2,1,0:T(8,128)(2,1)S(1)}) custom-call(bf16[2,592,128]{2,1,0:T(8,128)(2,1)S(1)} %pad_maximum_fusion.refs_0_, ...), custom_call_target="tpu_custom_call" | custom-call | flops 1738539008 | bytes 10035200 | tf_op jit(solution)/shard_map/pallas_call | solution.py:84
  133.0 2.6 %shard_map.87 = (f32[160,320]{1,0:T(8,128)S(1)}, f32[432,864]{1,0:T(8,128)S(1)}, f32[512,896]{1,0:T(8,128)S(1)}, bf16[2,512,896]{2,1,0:T(8,128)(2,1)S(1)}) custom-call(bf16[8,2,592,128]{3,2,1,0:T(8,128)(2,1)S(1)} %copy-done.20, bf16[4,2,592,128]{3,2,1,0:T(8,128)(2,1)S(1)} %bitcast.35, f32[160,320]{1,0:T(8,128)S(1)} %bitcast.36, f32[432,864]{1,0:T(8,128)S(1)} %bitcast.34), custom_call_target="tpu_custom_call" | custom-call | flops 1738539008 | bytes 10702848 | tf_op jit(solution)/shard_map/pallas_call | solution.py:84
  135.7 3.9 %collective-permute-start.15 = (bf16[2,512,896]{2,1,0:T(8,128)(2,1)S(1)}, bf16[2,512,896]{2,1,0:T(8,128)(2,1)S(1)}, u32[]{:S(2)}, u32[]{:S(2)}) collective-permute-start(bf16[2,512,896]{2,1,0:T(8,128)(2,1)S(1)} %get-tuple-element.33), channel_id=1, source_target_pairs={{0,1},{1,0},{2,3},{3,2},{4,5},{5,4},{6,7},{7,6},{8,9},{9,8},{10,11... | collective-permute-start | bytes 5505032 | tf_op jit(solution)/shard_map/ppermute | solution.py:67
  139.5 4.8 %collective-permute-start.16 = (bf16[2,592,128]{2,1,0:T(8,128)(2,1)S(1)}, bf16[2,592,128]{2,1,0:T(8,128)(2,1)S(1)}, u32[]{:S(2)}, u32[]{:S(2)}) collective-permute-start(bf16[2,592,128]{2,1,0:T(8,128)(2,1)S(1)} %copy-done.15), channel_id=1, source_target_pairs={{0,4},{4,8},{8,12},{12,0},{1,5},{5,9},{9,13},{13,1},{2,6},{6,10},{... | collective-permute-start | bytes 909320 | tf_op jit(solution)/shard_map/ppermute | solution.py:71
  144.4 1.9 collective-permute-start.17
  146.3 4.3 %collective-permute-start.18 = (bf16[2,592,128]{2,1,0:T(8,128)(2,1)S(1)}, bf16[2,592,128]{2,1,0:T(8,128)(2,1)S(1)}, u32[]{:S(2)}, u32[]{:S(2)}) collective-permute-start(bf16[2,592,128]{2,1,0:T(8,128)(2,1)S(1)} %copy-done.11), channel_id=1, source_target_pairs={{0,12},{4,0},{8,4},{12,8},{1,13},{5,1},{9,5},{13,9},{2,14},{6,2},{... | collective-permute-start | bytes 909320 | tf_op jit(solution)/shard_map/ppermute | solution.py:71
  150.6 7.3 %collective-permute-done.16.r1 = bf16[2,592,128]{2,1,0:T(8,128)(2,1)S(1)} collective-permute-done((bf16[2,592,128]{2,1,0:T(8,128)(2,1)S(1)}, bf16[2,592,128]{2,1,0:T(8,128)(2,1)S(1)}, u32[]{:S(2)}, u32[]{:S(2)}) %collective-permute-start.16) | collective-permute-done | bytes 303136 | tf_op jit(solution)/shard_map/ppermute | solution.py:71
  157.9 2.2 collective-permute-done.18.r3
  160.4 6.3 %collective-permute-start.19 = (bf16[1024,128]{1,0:T(8,128)(2,1)S(1)}, bf16[1024,128]{1,0:T(8,128)(2,1)S(1)}, u32[]{:S(2)}, u32[]{:S(2)}) collective-permute-start(bf16[1024,128]{1,0:T(8,128)(2,1)S(1)} %get-tuple-element.40), channel_id=1, source_target_pairs={{0,2},{2,0},{1,3},{3,1},{4,6},{6,4},{5,7},{7,5},{8,10},{10,8},{9,1... | collective-permute-start | bytes 786440 | tf_op jit(solution)/shard_map/ppermute | solution.py:67
  166.6 11.5 %collective-permute-done.19.got = bf16[1024,128]{1,0:T(8,128)(2,1)S(1)} collective-permute-done((bf16[1024,128]{1,0:T(8,128)(2,1)S(1)}, bf16[1024,128]{1,0:T(8,128)(2,1)S(1)}, u32[]{:S(2)}, u32[]{:S(2)}) %collective-permute-start.19) | collective-permute-done | bytes 262176 | tf_op jit(solution)/shard_map/ppermute | solution.py:67
  181.0 16.9 %all-to-all-start = ((bf16[16,160,128]{2,1,0:T(8,128)(2,1)}), bf16[16,160,128]{2,1,0:T(8,128)(2,1)}, u32[]{:S(2)}, u32[]{:S(2)}) async-start(bf16[16,160,128]{2,1,0:T(8,128)(2,1)} %broadcast_in_dim.3), calls=%async_computation | async-start | bytes 1310720 | tf_op jit(solution)/shard_map/all_to_all | solution.py:294
  197.9 2.3 collective-permute-start.20
  200.2 5.2 %collective-permute-start.22 = (bf16[2,432,128]{2,1,0:T(8,128)(2,1)}, bf16[2,432,128]{2,1,0:T(8,128)(2,1)}, u32[]{:S(2)}, u32[]{:S(2)}) collective-permute-start(bf16[2,432,128]{2,1,0:T(8,128)(2,1)} %copy-done.17), channel_id=1, source_target_pairs={{0,4},{4,8},{8,12},{12,0},{1,5},{5,9},{9,13},{13,1},{2,6},{6,10},{... | collective-permute-start | bytes 663560 | tf_op jit(solution)/shard_map/ppermute | solution.py:71
  205.4 3.3 %collective-permute-start.23 = (bf16[2,432,128]{2,1,0:T(8,128)(2,1)}, bf16[2,432,128]{2,1,0:T(8,128)(2,1)}, u32[]{:S(2)}, u32[]{:S(2)}) collective-permute-start(bf16[2,432,128]{2,1,0:T(8,128)(2,1)} %copy-done.17), channel_id=1, source_target_pairs={{0,8},{4,12},{8,0},{12,4},{1,9},{5,13},{9,1},{13,5},{2,10},{6,14},... | collective-permute-start | bytes 663560 | tf_op jit(solution)/shard_map/ppermute | solution.py:71
  208.7 3.3 %collective-permute-start.24 = (bf16[2,432,128]{2,1,0:T(8,128)(2,1)}, bf16[2,432,128]{2,1,0:T(8,128)(2,1)}, u32[]{:S(2)}, u32[]{:S(2)}) collective-permute-start(bf16[2,432,128]{2,1,0:T(8,128)(2,1)} %copy-done.17), channel_id=1, source_target_pairs={{0,12},{4,0},{8,4},{12,8},{1,13},{5,1},{9,5},{13,9},{2,14},{6,2},{... | collective-permute-start | bytes 663560 | tf_op jit(solution)/shard_map/ppermute | solution.py:71
  211.9 15.5 %collective-permute-done.20.last = bf16[512,896]{1,0:T(8,128)(2,1)S(1)} collective-permute-done((bf16[512,896]{1,0:T(8,128)(2,1)}, bf16[512,896]{1,0:T(8,128)(2,1)S(1)}, u32[]{:S(2)}, u32[]{:S(2)}) %collective-permute-start.20) | collective-permute-done | bytes 917536 | tf_op jit(solution)/shard_map/ppermute | solution.py:67
  229.4 2.6 shard_map.91
  232.0 3.8 %collective-permute-start.25 = (bf16[2,320,432]{2,1,0:T(8,128)(2,1)S(1)}, bf16[2,320,432]{2,1,0:T(8,128)(2,1)S(1)}, u32[]{:S(2)}, u32[]{:S(2)}) collective-permute-start(bf16[2,320,432]{2,1,0:T(8,128)(2,1)S(1)} %get-tuple-element.49), channel_id=1, source_target_pairs={{0,1},{1,0},{2,3},{3,2},{4,5},{5,4},{6,7},{7,6},{8,9},{9,8},{10,11... | collective-permute-start | bytes 1658888 | tf_op jit(solution)/shard_map/ppermute | solution.py:67
  241.0 7.4 %collective-permute-done.26 = bf16[320,432]{1,0:T(8,128)(2,1)S(1)} collective-permute-done((bf16[320,432]{1,0:T(8,128)(2,1)S(1)}, bf16[320,432]{1,0:T(8,128)(2,1)S(1)}, u32[]{:S(2)}, u32[]{:S(2)}) %collective-permute-start.26) | collective-permute-done | bytes 276512 | tf_op jit(solution)/shard_map/ppermute | solution.py:67
  (85 shorter events, 35.4 us)
Async XLA Ops:
  7.2 120.5 %all-gather.3.cloned.1.call-start = ((), (), s32[]{:S(2)}) async-start(), calls=%async_computation.1 | async-start | bytes 1515520 | tf_op jit(solution)/shard_map/all_gather | solution.py:257
  8.1 9.5 %collective-permute-start = (bf16[592,128]{1,0:T(8,128)(2,1)S(1)}, bf16[592,128]{1,0:T(8,128)(2,1)S(1)}, u32[]{:S(2)}, u32[]{:S(2)}) collective-permute-start(bf16[592,128]{1,0:T(8,128)(2,1)S(1)} %pad_maximum_fusion.2), channel_id=1, source_target_pairs={{0,0},{1,1},{2,64},{3,65},{4,128},{5,129},{6,192},{7,193},{8,256},... | collective-permute-start | bytes 454664 | tf_op jit(solution)/shard_map/ppermute | solution.py:241
  8.8 13.1 %collective-permute-start.1 = (bf16[592,128]{1,0:T(8,128)(2,1)S(1)}, bf16[592,128]{1,0:T(8,128)(2,1)S(1)}, u32[]{:S(2)}, u32[]{:S(2)}) collective-permute-start(bf16[592,128]{1,0:T(8,128)(2,1)S(1)} %pad_maximum_fusion.2), channel_id=1, source_target_pairs={{0,256},{1,257},{2,320},{3,321},{4,384},{5,385},{6,448},{7,449},{8... | collective-permute-start | bytes 454664 | tf_op jit(solution)/shard_map/ppermute | solution.py:241
  22.0 0.7 collective-permute-start.13
  22.7 37.7 %collective-permute-start.14 = (bf16[592,128]{1,0:T(8,128)(2,1)S(1)}, bf16[592,128]{1,0:T(8,128)(2,1)S(1)}, u32[]{:S(2)}, u32[]{:S(2)}) collective-permute-start(bf16[592,128]{1,0:T(8,128)(2,1)S(1)} %collective-permute-done.13), channel_id=1, source_target_pairs={{0,2},{2,0},{1,3},{3,1},{4,6},{6,4},{5,7},{7,5},{8,10},{10,8},{9,1... | collective-permute-start | bytes 454664 | tf_op jit(solution)/shard_map/ppermute | solution.py:67
  55.2 45.9 %collective-permute-start.11 = (bf16[512,896]{1,0:T(8,128)(2,1)S(1)}, bf16[512,896]{1,0:T(8,128)(2,1)S(1)}, u32[]{:S(2)}, u32[]{:S(2)}) collective-permute-start(bf16[512,896]{1,0:T(8,128)(2,1)S(1)} %shard_map.85.refs_9_), channel_id=1, source_target_pairs={{0,128},{128,0},{1,129},{129,1},{2,130},{130,2},{3,131},{131,3},{4... | collective-permute-start | bytes 2752520 | tf_op jit(solution)/shard_map/ppermute | solution.py:67
  61.2 10.4 %collective-permute-start.2 = (bf16[2,592,128]{2,1,0:T(8,128)(2,1)S(1)}, bf16[2,592,128]{2,1,0:T(8,128)(2,1)S(1)}, u32[]{:S(2)}, u32[]{:S(2)}) collective-permute-start(bf16[2,592,128]{2,1,0:T(8,128)(2,1)S(1)} %pad_maximum_fusion.refs_0_), channel_id=1, source_target_pairs={{0,16},{16,32},{32,48},{48,64},{64,80},{80,96},{96,112},{112,0},{1... | collective-permute-start | bytes 909320 | tf_op jit(solution)/shard_map/ppermute | solution.py:71
  67.9 19.7 %collective-permute-start.3 = (bf16[2,592,128]{2,1,0:T(8,128)(2,1)S(1)}, bf16[2,592,128]{2,1,0:T(8,128)(2,1)S(1)}, u32[]{:S(2)}, u32[]{:S(2)}) collective-permute-start(bf16[2,592,128]{2,1,0:T(8,128)(2,1)S(1)} %pad_maximum_fusion.refs_0_), channel_id=1, source_target_pairs={{0,112},{16,0},{32,16},{48,32},{64,48},{80,64},{96,80},{112,96},{1... | collective-permute-start | bytes 909320 | tf_op jit(solution)/shard_map/ppermute | solution.py:71
  71.6 18.9 %collective-permute-start.4 = (bf16[2,592,128]{2,1,0:T(8,128)(2,1)S(1)}, bf16[2,592,128]{2,1,0:T(8,128)(2,1)S(1)}, u32[]{:S(2)}, u32[]{:S(2)}) collective-permute-start(bf16[2,592,128]{2,1,0:T(8,128)(2,1)S(1)} %collective-permute-done.2.refs_1_), channel_id=1, source_target_pairs={{0,16},{16,32},{32,48},{48,64},{64,80},{80,96},{96,112},{112,0},{1... | collective-permute-start | bytes 909320 | tf_op jit(solution)/shard_map/ppermute | solution.py:71
  87.6 15.4 %collective-permute-start.5 = (bf16[2,592,128]{2,1,0:T(8,128)(2,1)S(1)}, bf16[2,592,128]{2,1,0:T(8,128)(2,1)S(1)}, u32[]{:S(2)}, u32[]{:S(2)}) collective-permute-start(bf16[2,592,128]{2,1,0:T(8,128)(2,1)S(1)} %collective-permute-done.3.refs_2_), channel_id=1, source_target_pairs={{0,112},{16,0},{32,16},{48,32},{64,48},{80,64},{96,80},{112,96},{1... | collective-permute-start | bytes 909320 | tf_op jit(solution)/shard_map/ppermute | solution.py:71
  90.6 14.8 %collective-permute-start.6 = (bf16[2,592,128]{2,1,0:T(8,128)(2,1)S(1)}, bf16[2,592,128]{2,1,0:T(8,128)(2,1)S(1)}, u32[]{:S(2)}, u32[]{:S(2)}) collective-permute-start(bf16[2,592,128]{2,1,0:T(8,128)(2,1)S(1)} %collective-permute-done.4.refs_3_), channel_id=1, source_target_pairs={{0,16},{16,32},{32,48},{48,64},{64,80},{80,96},{96,112},{112,0},{1... | collective-permute-start | bytes 909320 | tf_op jit(solution)/shard_map/ppermute | solution.py:71
  94.7 22.1 %collective-permute-start.10 = (bf16[512,896]{1,0:T(8,128)(2,1)S(1)}, bf16[512,896]{1,0:T(8,128)(2,1)S(1)}, u32[]{:S(2)}, u32[]{:S(2)}) collective-permute-start(bf16[512,896]{1,0:T(8,128)(2,1)S(1)} %shard_map.85.refs_9_), channel_id=1, source_target_pairs={{0,1},{1,0},{2,3},{3,2},{4,5},{5,4},{6,7},{7,6},{8,9},{9,8},{10,11... | collective-permute-start | bytes 2752520 | tf_op jit(solution)/shard_map/ppermute | solution.py:67
  101.1 19.5 %collective-permute-start.12 = (bf16[512,896]{1,0:T(8,128)(2,1)S(1)}, bf16[512,896]{1,0:T(8,128)(2,1)S(1)}, u32[]{:S(2)}, u32[]{:S(2)}) collective-permute-start(bf16[512,896]{1,0:T(8,128)(2,1)S(1)} %collective-permute-done.11.refs_11_), channel_id=1, source_target_pairs={{0,1},{1,0},{2,3},{3,2},{4,5},{5,4},{6,7},{7,6},{8,9},{9,8},{10,11... | collective-permute-start | bytes 2752520 | tf_op jit(solution)/shard_map/ppermute | solution.py:67
  103.0 11.2 %collective-permute-start.7 = (bf16[2,592,128]{2,1,0:T(8,128)(2,1)S(1)}, bf16[2,592,128]{2,1,0:T(8,128)(2,1)S(1)}, u32[]{:S(2)}, u32[]{:S(2)}) collective-permute-start(bf16[2,592,128]{2,1,0:T(8,128)(2,1)S(1)} %collective-permute-done.5.refs_4_), channel_id=1, source_target_pairs={{0,112},{16,0},{32,16},{48,32},{64,48},{80,64},{96,80},{112,96},{1... | collective-permute-start | bytes 909320 | tf_op jit(solution)/shard_map/ppermute | solution.py:71
  105.4 11.4 %collective-permute-start.8 = (bf16[592,128]{1,0:T(8,128)(2,1)S(1)}, bf16[592,128]{1,0:T(8,128)(2,1)S(1)}, u32[]{:S(2)}, u32[]{:S(2)}) collective-permute-start(bf16[592,128]{1,0:T(8,128)(2,1)S(1)} %slice_bitcast_fusion.4), channel_id=1, source_target_pairs={{0,16},{16,32},{32,48},{48,64},{64,80},{80,96},{96,112},{112,0},{1... | collective-permute-start | bytes 454664 | tf_op jit(solution)/shard_map/ppermute | solution.py:71
  114.3 6.3 %collective-permute-start.9 = (bf16[592,128]{1,0:T(8,128)(2,1)S(1)}, bf16[592,128]{1,0:T(8,128)(2,1)S(1)}, u32[]{:S(2)}, u32[]{:S(2)}) collective-permute-start(bf16[592,128]{1,0:T(8,128)(2,1)S(1)} %slice_bitcast_fusion.3), channel_id=1, source_target_pairs={{0,112},{16,0},{32,16},{48,32},{64,48},{80,64},{96,80},{112,96},{1... | collective-permute-start | bytes 454664 | tf_op jit(solution)/shard_map/ppermute | solution.py:71
  133.0 13.3 %copy-start.11 = (bf16[2,592,128]{2,1,0:T(8,128)(2,1)S(1)}, bf16[2,592,128]{2,1,0:T(8,128)(2,1)}, u32[]{:S(2)}) copy-start(bf16[2,592,128]{2,1,0:T(8,128)(2,1)} %copy-done.10) | copy-start | bytes 909316
  133.0 27.1 %copy-start.4 = (f32[2,592,128]{2,1,0:T(8,128)S(1)}, f32[2,592,128]{2,1,0:T(8,128)}, u32[]{:S(2)}) copy-start(f32[2,592,128]{2,1,0:T(8,128)} %copy-done.3) | copy-start | bytes 1818628
  135.6 44.4 %copy-start.5 = (f32[160,320]{1,0:T(8,128)}, f32[160,320]{1,0:T(8,128)S(1)}, u32[]{:S(2)}) copy-start(f32[160,320]{1,0:T(8,128)S(1)} %get-tuple-element.31.i_own) | copy-start | bytes 614404
  135.7 43.3 %collective-permute-start.15 = (bf16[2,512,896]{2,1,0:T(8,128)(2,1)S(1)}, bf16[2,512,896]{2,1,0:T(8,128)(2,1)S(1)}, u32[]{:S(2)}, u32[]{:S(2)}) collective-permute-start(bf16[2,512,896]{2,1,0:T(8,128)(2,1)S(1)} %get-tuple-element.33), channel_id=1, source_target_pairs={{0,1},{1,0},{2,3},{3,2},{4,5},{5,4},{6,7},{7,6},{8,9},{9,8},{10,11... | collective-permute-start | bytes 5505032 | tf_op jit(solution)/shard_map/ppermute | solution.py:67
  139.5 18.4 %collective-permute-start.16 = (bf16[2,592,128]{2,1,0:T(8,128)(2,1)S(1)}, bf16[2,592,128]{2,1,0:T(8,128)(2,1)S(1)}, u32[]{:S(2)}, u32[]{:S(2)}) collective-permute-start(bf16[2,592,128]{2,1,0:T(8,128)(2,1)S(1)} %copy-done.15), channel_id=1, source_target_pairs={{0,4},{4,8},{8,12},{12,0},{1,5},{5,9},{9,13},{13,1},{2,6},{6,10},{... | collective-permute-start | bytes 909320 | tf_op jit(solution)/shard_map/ppermute | solution.py:71
  144.4 13.6 %collective-permute-start.17 = (bf16[2,592,128]{2,1,0:T(8,128)(2,1)S(1)}, bf16[2,592,128]{2,1,0:T(8,128)(2,1)S(1)}, u32[]{:S(2)}, u32[]{:S(2)}) collective-permute-start(bf16[2,592,128]{2,1,0:T(8,128)(2,1)S(1)} %copy-done.13), channel_id=1, source_target_pairs={{0,8},{4,12},{8,0},{12,4},{1,9},{5,13},{9,1},{13,5},{2,10},{6,14},... | collective-permute-start | bytes 909320 | tf_op jit(solution)/shard_map/ppermute | solution.py:71
  146.3 13.8 %collective-permute-start.18 = (bf16[2,592,128]{2,1,0:T(8,128)(2,1)S(1)}, bf16[2,592,128]{2,1,0:T(8,128)(2,1)S(1)}, u32[]{:S(2)}, u32[]{:S(2)}) collective-permute-start(bf16[2,592,128]{2,1,0:T(8,128)(2,1)S(1)} %copy-done.11), channel_id=1, source_target_pairs={{0,12},{4,0},{8,4},{12,8},{1,13},{5,1},{9,5},{13,9},{2,14},{6,2},{... | collective-permute-start | bytes 909320 | tf_op jit(solution)/shard_map/ppermute | solution.py:71
  160.4 17.8 %collective-permute-start.19 = (bf16[1024,128]{1,0:T(8,128)(2,1)S(1)}, bf16[1024,128]{1,0:T(8,128)(2,1)S(1)}, u32[]{:S(2)}, u32[]{:S(2)}) collective-permute-start(bf16[1024,128]{1,0:T(8,128)(2,1)S(1)} %get-tuple-element.40), channel_id=1, source_target_pairs={{0,2},{2,0},{1,3},{3,1},{4,6},{6,4},{5,7},{7,5},{8,10},{10,8},{9,1... | collective-permute-start | bytes 786440 | tf_op jit(solution)/shard_map/ppermute | solution.py:67
  178.2 1.8 collective-permute-start.21
  181.0 47.4 %all-to-all-start = ((bf16[16,160,128]{2,1,0:T(8,128)(2,1)}), bf16[16,160,128]{2,1,0:T(8,128)(2,1)}, u32[]{:S(2)}, u32[]{:S(2)}) async-start(bf16[16,160,128]{2,1,0:T(8,128)(2,1)} %broadcast_in_dim.3), calls=%async_computation | async-start | bytes 1310720 | tf_op jit(solution)/shard_map/all_to_all | solution.py:294
  197.9 29.6 %collective-permute-start.20 = (bf16[512,896]{1,0:T(8,128)(2,1)}, bf16[512,896]{1,0:T(8,128)(2,1)S(1)}, u32[]{:S(2)}, u32[]{:S(2)}) collective-permute-start(bf16[512,896]{1,0:T(8,128)(2,1)} %fusion), channel_id=1, source_target_pairs={{0,128},{128,0},{1,129},{129,1},{2,130},{130,2},{3,131},{131,3},{4... | collective-permute-start | bytes 2752520 | tf_op jit(solution)/shard_map/ppermute | solution.py:67
  200.2 28.2 %collective-permute-start.22 = (bf16[2,432,128]{2,1,0:T(8,128)(2,1)}, bf16[2,432,128]{2,1,0:T(8,128)(2,1)}, u32[]{:S(2)}, u32[]{:S(2)}) collective-permute-start(bf16[2,432,128]{2,1,0:T(8,128)(2,1)} %copy-done.17), channel_id=1, source_target_pairs={{0,4},{4,8},{8,12},{12,0},{1,5},{5,9},{9,13},{13,1},{2,6},{6,10},{... | collective-permute-start | bytes 663560 | tf_op jit(solution)/shard_map/ppermute | solution.py:71
  205.4 23.0 %collective-permute-start.23 = (bf16[2,432,128]{2,1,0:T(8,128)(2,1)}, bf16[2,432,128]{2,1,0:T(8,128)(2,1)}, u32[]{:S(2)}, u32[]{:S(2)}) collective-permute-start(bf16[2,432,128]{2,1,0:T(8,128)(2,1)} %copy-done.17), channel_id=1, source_target_pairs={{0,8},{4,12},{8,0},{12,4},{1,9},{5,13},{9,1},{13,5},{2,10},{6,14},... | collective-permute-start | bytes 663560 | tf_op jit(solution)/shard_map/ppermute | solution.py:71
  208.7 19.7 %collective-permute-start.24 = (bf16[2,432,128]{2,1,0:T(8,128)(2,1)}, bf16[2,432,128]{2,1,0:T(8,128)(2,1)}, u32[]{:S(2)}, u32[]{:S(2)}) collective-permute-start(bf16[2,432,128]{2,1,0:T(8,128)(2,1)} %copy-done.17), channel_id=1, source_target_pairs={{0,12},{4,0},{8,4},{12,8},{1,13},{5,1},{9,5},{13,9},{2,14},{6,2},{... | collective-permute-start | bytes 663560 | tf_op jit(solution)/shard_map/ppermute | solution.py:71
  232.0 5.5 %collective-permute-start.25 = (bf16[2,320,432]{2,1,0:T(8,128)(2,1)S(1)}, bf16[2,320,432]{2,1,0:T(8,128)(2,1)S(1)}, u32[]{:S(2)}, u32[]{:S(2)}) collective-permute-start(bf16[2,320,432]{2,1,0:T(8,128)(2,1)S(1)} %get-tuple-element.49), channel_id=1, source_target_pairs={{0,1},{1,0},{2,3},{3,2},{4,5},{5,4},{6,7},{7,6},{8,9},{9,8},{10,11... | collective-permute-start | bytes 1658888 | tf_op jit(solution)/shard_map/ppermute | solution.py:67
  237.6 10.8 %collective-permute-start.26 = (bf16[320,432]{1,0:T(8,128)(2,1)S(1)}, bf16[320,432]{1,0:T(8,128)(2,1)S(1)}, u32[]{:S(2)}, u32[]{:S(2)}) collective-permute-start(bf16[320,432]{1,0:T(8,128)(2,1)S(1)} %fusion.1), channel_id=1, source_target_pairs={{0,128},{128,0},{1,129},{129,1},{2,130},{130,2},{3,131},{131,3},{4... | collective-permute-start | bytes 829448 | tf_op jit(solution)/shard_map/ppermute | solution.py:67
  (18 other events, 55.7 us)
Sparse Core Ops, SparseCore 0:
  61.3 41.4 all-gather.2

commit v2 on v1

--- a/solution.py
+++ b/solution.py
@@ -37,7 +37,7 @@
     return [
         (
             device(zg, p, y, xh, xl, w, core),
-            device(xh ^ flip, xl, PANELS * w + y % PANELS, zg, p, y // PANELS, core),
+            device(xh ^ flip, w, PANELS * (xl ^ zg) + y % PANELS, zg, p, y // PANELS, core),
         )
         for zg, p, y, xh, xl, w, core in coordinates()
     ]
@@ -47,7 +47,7 @@
     return [
         (
             device(zg, p, y, xh, xl, w, core),
-            device(xh, p, PANELS * w + y % PANELS, zg, xl, y // PANELS, core),
+            device(xh, p, PANELS * (xl ^ zg) + y % PANELS, zg, w, y // PANELS, core),
         )
         for zg, p, y, xh, xl, w, core in coordinates()
     ]
@@ -57,7 +57,7 @@
     return [
         (
             device(zg, p, y, xh, xl, w, core),
-            device(zg, p, y, xh, xl, w, core) if xl == p else device(zg, 1 - p, y, xh, 1 - xl, w, core),
+            device(zg, w, y, xh, xl, p, core),
         )
         for zg, p, y, xh, xl, w, core in coordinates()
     ]
@@ -87,7 +87,7 @@
         in_specs=[VMEM] * len(args),
         out_specs=jax.tree.map(lambda _: VMEM, out),
         scratch_shapes=list(scratch),
-        compiler_params=pltpu.CompilerParams(vmem_limit_bytes=24 * 1024 * 1024),
+        compiler_params=pltpu.CompilerParams(vmem_limit_bytes=16 * 1024 * 1024),
         cost_estimate=pl.CostEstimate(flops=flops, bytes_accessed=size, transcendentals=0),
     )(*args)
 
@@ -115,26 +115,31 @@
 
 def sides_kernel(da, dg, h, *refs):
     ring, inverses = refs[: RING + 1], refs[RING + 1 : RING + 5]
-    rows, own, s1, s2, s3, acc = refs[RING + 5 :]
+    rows, own, send, acc = refs[RING + 5 :]
     core, zg, p, y = (lax.axis_index(a) for a in ("core", "zg", "p", "y"))
-    x = 2 * lax.axis_index("xh") + lax.axis_index("xl")
+    group = lax.axis_index("xh")
+    x = 2 * group + lax.axis_index("xl")
     width, n = own.shape[1:]
+
+    def place(offset):
+        return lax.bitwise_xor(lax.rem(y + offset + RING, RING), PANELS * group)
+
     for offset, ref in zip((0, -1, 1, -2, 2, -3, 3), ring):
-        at = lax.rem(y + offset + RING, RING)
+        at = place(offset)
         for slot in range(2):
             rows[at, lax.bitwise_xor(zg, slot)] = ref[slot]
     for slot in range(2):
-        rows[lax.rem(y + 4, RING), lax.bitwise_xor(zg, slot)] = ring[RING - 1 + slot][...]
+        rows[place(4), lax.bitwise_xor(zg, slot)] = ring[RING - 1 + slot][...]
     big = [ref[:dg, : dg * h] for ref in inverses]
     small = [
         jnp.concatenate([ref[at, lanes] for _, at, lanes in small_at(da, dg, h)], 0) for ref in inverses
     ]
-    for w in range(2):
+    for xl in range(2):
 
         def panel(first, lo, hi):
             return jnp.concatenate(
                 [
-                    jnp.concatenate([rows[PANELS * w + first + m, xh, lo:hi, :] for m in range(h)], 0)
+                    jnp.concatenate([rows[PANELS * xl + first + m, xh, lo:hi, :] for m in range(h)], 0)
                     for xh in range(2)
                 ],
                 1,
@@ -145,16 +150,19 @@
             for q in range(2):
                 total = dot(blocks[2 * q], mine, ((1,), (0,))) + dot(blocks[2 * q + 1], other, ((1,), (0,)))
                 for xh in range(2):
-                    acc[2 * xh + lax.bitwise_xor(p, q), w, lo:hi, :] = total[:, xh * n : (xh + 1) * n]
+                    acc[2 * xh + xl, lax.bitwise_xor(p, q), lo:hi, :] = total[:, xh * n : (xh + 1) * n]
     own[...] = acc[x]
-    for ahead, ref in enumerate((s1, s2, s3)):
-        ref[...] = acc[lax.rem(x + ahead + 1, 4)].astype(ref.dtype)
-
-
-def first_sum_kernel(da, own, r1, r2, r3, keep, send):
+    send[...] = acc[...].astype(send.dtype)
+
+
+def first_sum_kernel(da, own, got, keep, send):
     w = lax.axis_index("w")
+    x = 2 * lax.axis_index("xh") + lax.axis_index("xl")
     dg = own.shape[1] - da
-    keep[...] = ((own[...] + r1[...].astype(f32)) + r2[...].astype(f32)) + r3[...].astype(f32)
+    total = own[...]
+    for i in range(1, 4):
+        total = total + got[lax.rem(x + i, 4)].astype(f32)
+    keep[...] = total
     for t in range(2):
         send[t * dg : (t + 1) * dg, :] = keep[t, da:, :].astype(send.dtype)
     send[2 * dg :, :] = keep[1 - w, :da, :].astype(send.dtype)
@@ -168,18 +176,19 @@
     left[...] = (keep[w, :da, :] + got[2 * dg :, :].astype(f32)).astype(left.dtype)
 
 
-def factor_kernel(da, dg, h, weight, rows, cols, ip, gp, i_own, g_own, keep, send):
+def factor_kernel(da, dg, h, weight, rows, c0, c1, c2, c3, ip, gp, i_own, g_own, keep, send, held):
     core, p, w = (lax.axis_index(a) for a in ("core", "p", "w"))
+    x = 2 * lax.axis_index("xh") + lax.axis_index("xl")
+    for behind, ref in enumerate((c0, c1, c2, c3)):
+        held[lax.rem(x - behind + 4, 4)] = ref[...]
     keep[...] = jnp.zeros_like(keep)
     send[...] = jnp.zeros_like(send)
 
     def panel(k, lo, hi):
-        return jnp.concatenate([rows[PANELS * t + k, xh, lo:hi, :] for xh in range(2) for t in range(2)], 1)
-
-    def columns(xl, lo, hi):
-        return jnp.concatenate(
-            [cols[2 * xh + xl, lax.bitwise_xor(w, t), lo:hi, :] for xh in range(2) for t in range(2)], 1
-        )
+        return jnp.concatenate([rows[PANELS * xl + k, xh, lo:hi, :] for xh in range(2) for xl in range(2)], 1)
+
+    def columns(q, lo, hi):
+        return jnp.concatenate([held[token, lax.bitwise_xor(q, w), lo:hi, :] for token in range(4)], 1)
 
     for lo, hi, prior, own in ((0, da, ip, i_own), (da, da + dg, gp, g_own)):
         n = hi - lo
@@ -211,21 +220,26 @@
 
 
 def product_kernel(h, scale, left, right, r1, r2, r3, own, keep, send, held):
-    core, p = lax.axis_index("core"), lax.axis_index("p")
-    x = 2 * lax.axis_index("xh") + lax.axis_index("xl")
+    core, p, group = lax.axis_index("core"), lax.axis_index("p"), lax.axis_index("xh")
+    x = 2 * group + lax.axis_index("xl")
     n = left.shape[1]
     for behind, ref in enumerate((right, r1, r2, r3)):
         held[lax.rem(x - behind + 4, 4)] = ref[...]
 
-    def columns(xl):
-        return jnp.concatenate([held[2 * xh + xl, t] for xh in range(2) for t in range(2)], 1)
+    def columns(q):
+        return jnp.concatenate([held[token, q] for token in range(4)], 1)
+
+    def panel(k):
+        return jnp.concatenate(
+            [left[2 * PANELS * xh + PANELS * lax.bitwise_xor(xl, group) + k] for xh in range(2) for xl in range(2)], 1
+        )
 
     here, there = columns(p), columns(1 - p)
     for first, outs in ((1 - core, (send.at[0], send.at[1])), (core, (own, keep))):
         for m in range(h):
-            panel = jnp.concatenate([left[PANELS * b + first * h + m] for b in range(4)], 1)
+            part = panel(first * h + m)
             for c, ref in zip((here, there), outs):
-                ref[m * n : (m + 1) * n, :] = (dot(panel, c, ((1,), (1,))) * scale).astype(ref.dtype)
+                ref[m * n : (m + 1) * n, :] = (dot(part, c, ((1,), (1,))) * scale).astype(ref.dtype)
 
 
 def local(activations, output_grads, input_prior, gradient_prior, input_inverse, gradient_inverse):
@@ -238,7 +252,16 @@
     pack = packed_shape(da, dg, h)
 
     x = jnp.concatenate([activations.T, output_grads.T], 0)
-    u = jnp.stack([lax.ppermute(x, AXES, panel_perm(j)) for j in range(2)])
+    inverse = call(pack_kernel, shape(pack, bf16), 0, after(input_inverse.T, x), gradient_inverse.T)
+    first, second, col, inverse_c = lax.optimization_barrier(
+        (
+            lax.ppermute(x, AXES, panel_perm(0)),
+            lax.ppermute(x, AXES, panel_perm(1)),
+            lax.ppermute(x, AXES, column_perm()),
+            swap(inverse, "core"),
+        )
+    )
+    u = jnp.stack([first, second])
     up, down = [u], [u]
     for _ in range(3):
         up.append(shift(up[-1], "y", RING, 1))
@@ -246,43 +269,41 @@
     ring = [u, up[1], down[1], up[2], down[2], up[3], down[3]]
     ring += [shift(up[3][0], "y", RING, 1), shift(down[3][1], "y", RING, -1)]
 
-    inverse = call(
-        pack_kernel, shape(pack, bf16), 0, after(input_inverse.T, x), gradient_inverse.T
-    )
-    inverse = after(inverse, u)
-    inverse_z = swap(inverse, "p")
-    inverses = [inverse, swap(inverse, "core"), inverse_z, swap(inverse_z, "core")]
-
-    col = lax.ppermute(after(x, u), AXES, column_perm())
-    cols = lax.all_gather(jnp.stack([col, swap(col, "w")]), X, axis=0, tiled=False)
-
-    rows, own, *ahead = call(
+    inverse_z = swap(after(inverse, up[1], down[1]), "p")
+    inverse_zc = swap(after(inverse_z, up[3], down[3]), "core")
+
+    rows, own, send = call(
         functools.partial(sides_kernel, da, dg, h),
-        (shape((RING, *pair), bf16), shape(pair, f32)) + (shape(pair, bf16),) * 3,
-        work, *ring, *inverses,
+        (shape((RING, *pair), bf16), shape(pair, f32), shape((4, *pair), bf16)),
+        work, *ring, inverse, inverse_c, inverse_z, inverse_zc,
         scratch=[pltpu.VMEM((4, *pair), f32)],
     )
-    got = [shift(part, X, 4, i + 1) for i, part in enumerate(ahead)]
+    col = jnp.stack([col, swap(after(col, send), "w")])
+    got = lax.all_to_all(send, X, 0, 0, tiled=True)
     keep, send = call(
         functools.partial(first_sum_kernel, da),
         (shape(pair, f32), shape((2 * dg + da, block), bf16)),
-        0, own, *got,
-    )
+        0, own, got,
+    )
+    col = after(col, send)
+    cols = [shift(col, X, 4, i + 1) for i in range(3)]
     left, right = call(
         functools.partial(second_sum_kernel, da),
         (shape((da, block), bf16), shape((2, dg, block), bf16)),
         0, keep, swap(send, "w"),
     )
-    piece = lax.ppermute(left, AXES, piece_perm())
-    rights = [shift(right, X, 4, i + 1) for i in range(3)]
-
     i_own, g_own, f_keep, f_send = call(
         functools.partial(factor_kernel, da, dg, h, (1.0 - decay_rate) / tokens),
         (shape((da, da * h), f32), shape((dg, dg * h), f32), shape(pack, f32), shape((2, *pack), bf16)),
-        work, rows, cols, input_prior.T, gradient_prior.T,
-    )
+        work, after(rows, left), col, *cols, input_prior.T, gradient_prior.T,
+        scratch=[pltpu.VMEM((4, *pair), bf16)],
+    )
+    piece = lax.ppermute(left, AXES, piece_perm())
+    rights = [shift(right, X, 4, i + 1) for i in range(3)]
+
     f_got = swap(f_send, "core")
-    f_mid = after((f_keep + f_got[1].astype(f32)).astype(bf16), left)
+    f_mid = (f_keep + f_got[1].astype(f32)).astype(bf16)
+    lefts = lax.all_to_all(jnp.broadcast_to(after(piece, *rights[:2]), (16, *piece.shape)), ("zg", "y"), 0, 0, tiled=True)
     f_last = swap(f_mid, "p")
     input_factor, gradient_factor = call(
         functools.partial(factor_sum_kernel, da, dg, h),
@@ -290,16 +311,13 @@
         0, i_own, g_own, f_got, f_last,
     )
 
-    pieces = jnp.broadcast_to(after(piece, f_mid), (16, *piece.shape))
-    lefts = lax.all_to_all(pieces, ("zg", "y"), 0, 0, tiled=True)
-    lefts = after(lefts, f_last)
     p_own, p_keep, p_send = call(
         functools.partial(product_kernel, h, 1.0 / tokens),
         (shape((da * h, dg), f32), shape((da * h, dg), f32), shape((2, da * h, dg), bf16)),
         2 * tokens * h * da * dg, lefts, right, *rights,
         scratch=[pltpu.VMEM((4, 2, dg, block), bf16)],
     )
-    p_got = swap(p_send, "core")
+    p_got = after(swap(p_send, "core"), f_last)
     p_last = swap((p_keep + p_got[1].astype(f32)).astype(bf16), "p")
     preconditioned = (p_own + p_got[0].astype(f32) + p_last.astype(f32)).astype(bf16)
     return input_factor.T, gradient_factor.T, preconditioned

time: 259 us -> 236 us (0.911)
  starting transfers between devices: 151 us -> 134 us
  between operations: 14.5 us -> 1.06 us
  Pallas kernels: 9.66 us -> 13.1 us
    ppermute x9, waiting for transfers between devices: 36.2 us -> 23.9 us  [swap(): return lax.ppermute(x, axis, [(0, 1), (1, 0)])]
    ppermute x14, starting transfers between devices: 61.2 us -> 50.5 us  [shift(): return lax.ppermute(x, axis, [(i, (i + by) % size) for i in range(size)])]
    ppermute x3, waiting for transfers between devices: 4.32 us -> 8.87 us  [the longest x1 8.86 us: local(): lax.ppermute(x, AXES, panel_perm(1))]
    ppermute x14, waiting for transfers between devices: 22 us -> 26.6 us  [shift(): return lax.ppermute(x, axis, [(i, (i + by) % size) for i in range(size)])]
    pallas_call x7, Pallas kernels: 9.66 us -> 13.1 us  [call(): pl.pallas_call(kernel, out_shape=out, in_specs=[VMEM] * len(args), out_sp...]
    ppermute x9, starting transfers between devices: 62 us -> 58.7 us  [swap(): return lax.ppermute(x, axis, [(0, 1), (1, 0)])]
    all_to_all x1 -> x2, waiting for transfers between devices: 0.01 us -> 3.24 us  [the longest x1 2.06 us: local(): lax.all_to_all(jnp.broadcast_to(after(piece, *rights[:2]), (16, *piece.sh...]
    all_to_all x1 -> x2, starting transfers between devices: 16.9 us -> 15.1 us  [the longest x1 7.82 us: local(): got = lax.all_to_all(send, X, 0, 0, tiled=True)]
  transfers between devices with their start and end apart: 29 -> 29, of which waited for: 12 -> 17; matrix products, arithmetic and copies ran while one was open for 1% -> 2% of each run, Pallas kernels for 2% -> 2%
where the time goes in v2:
time: 236 us; the launch traced here: 231 us
  starting transfers between devices  134 us (57%)
  waiting for transfers between devices  62.5 us (26%)
  local copies, waits for them, and re-layouts  15.8 us (7%)
  Pallas kernels  13.1 us (6%)
  other arithmetic  4.59 us (2%)
    ppermute x9, starting transfers between devices, swap(): return lax.ppermute(x, axis, [(0, 1), (1, 0)])  58.7 us
    ppermute x14, starting transfers between devices, shift(): return lax.ppermute(x, axis, [(i, (i + by) % size) for i in range(size)])  50.5 us
    ppermute x14, waiting for transfers between devices, shift(): return lax.ppermute(x, axis, [(i, (i + by) % size) for i in range(size)])  26.6 us
    ppermute x9, waiting for transfers between devices, swap(): return lax.ppermute(x, axis, [(0, 1), (1, 0)])  23.9 us
    unnamed x40, local copies, waits for them, and re-layouts  14.8 us
    pallas_call x7, Pallas kernels, call(): pl.pallas_call(kernel, out_shape=out, in_specs=[VMEM] * len(args), out_sp...  13.1 us
    ppermute x1, waiting for transfers between devices, local(): lax.ppermute(x, AXES, panel_perm(1))  8.86 us
    ppermute x1, starting transfers between devices, local(): lax.ppermute(x, AXES, panel_perm(1))  7.86 us
  transfers between devices with their start and end apart: 29, of which 17 were waited for; matrix products, arithmetic and copies ran while one was open for 2% of the time, Pallas kernels for 2%

profile of v2, /device:TPU:1, one launch (start us, length us, event | category | flops | bytes accessed | tf_op | source)
XLA Modules:
  0.0 231.2 jit_solution(2067930067033518196)
XLA Ops:
  3.7 8.8 %collective-permute-start.3 = (bf16[512,896]{1,0:T(8,128)(2,1)S(1)}, bf16[512,896]{1,0:T(8,128)(2,1)S(1)}, u32[]{:S(2)}, u32[]{:S(2)}) collective-permute-start(bf16[512,896]{1,0:T(8,128)(2,1)S(1)} %shard_map.85.refs_9_), channel_id=1, source_target_pairs={{0,1},{1,0},{2,3},{3,2},{4,5},{5,4},{6,7},{7,6},{8,9},{9,8},{10,11... | collective-permute-start | bytes 2752520 | tf_op jit(solution)/shard_map/ppermute | solution.py:67
  13.1 7.9 %collective-permute-start.1 = (bf16[592,128]{1,0:T(8,128)(2,1)S(1)}, bf16[592,128]{1,0:T(8,128)(2,1)S(1)}, u32[]{:S(2)}, u32[]{:S(2)}) collective-permute-start(bf16[592,128]{1,0:T(8,128)(2,1)S(1)} %pad_maximum_fusion.2), channel_id=1, source_target_pairs={{0,256},{1,257},{2,384},{3,385},{4,320},{5,321},{6,448},{7,449},{8... | collective-permute-start | bytes 454664 | tf_op jit(solution)/shard_map/ppermute | solution.py:259
  21.7 8.9 %collective-permute-done.1 = bf16[592,128]{1,0:T(8,128)(2,1)S(1)} collective-permute-done((bf16[592,128]{1,0:T(8,128)(2,1)S(1)}, bf16[592,128]{1,0:T(8,128)(2,1)S(1)}, u32[]{:S(2)}, u32[]{:S(2)}) %collective-permute-start.1) | collective-permute-done | bytes 151584 | tf_op jit(solution)/shard_map/ppermute | solution.py:259
  32.5 7.7 %collective-permute-start.5 = (bf16[2,592,128]{2,1,0:T(8,128)(2,1)S(1)}, bf16[2,592,128]{2,1,0:T(8,128)(2,1)S(1)}, u32[]{:S(2)}, u32[]{:S(2)}) collective-permute-start(bf16[2,592,128]{2,1,0:T(8,128)(2,1)S(1)} %pad_maximum_fusion.refs_0_), channel_id=1, source_target_pairs={{0,112},{16,0},{32,16},{48,32},{64,48},{80,64},{96,80},{112,96},{1... | collective-permute-start | bytes 909320 | tf_op jit(solution)/shard_map/ppermute | solution.py:71
  40.2 4.3 %collective-permute-done.4.refs_1_ = bf16[2,592,128]{2,1,0:T(8,128)(2,1)S(1)} collective-permute-done((bf16[2,592,128]{2,1,0:T(8,128)(2,1)S(1)}, bf16[2,592,128]{2,1,0:T(8,128)(2,1)S(1)}, u32[]{:S(2)}, u32[]{:S(2)}) %collective-permute-start.4) | collective-permute-done | bytes 303136 | tf_op jit(solution)/shard_map/ppermute | solution.py:71
  45.4 9.9 %collective-permute-start.12 = (bf16[512,896]{1,0:T(8,128)(2,1)S(1)}, bf16[512,896]{1,0:T(8,128)(2,1)S(1)}, u32[]{:S(2)}, u32[]{:S(2)}) collective-permute-start(bf16[512,896]{1,0:T(8,128)(2,1)S(1)} %shard_map.85.refs_9_), channel_id=1, source_target_pairs={{0,128},{128,0},{1,129},{129,1},{2,130},{130,2},{3,131},{131,3},{4... | collective-permute-start | bytes 2752520 | tf_op jit(solution)/shard_map/ppermute | solution.py:67
  57.3 5.3 %collective-permute-start.7 = (bf16[2,592,128]{2,1,0:T(8,128)(2,1)S(1)}, bf16[2,592,128]{2,1,0:T(8,128)(2,1)S(1)}, u32[]{:S(2)}, u32[]{:S(2)}) collective-permute-start(bf16[2,592,128]{2,1,0:T(8,128)(2,1)S(1)} %collective-permute-done.5.refs_2_), channel_id=1, source_target_pairs={{0,112},{16,0},{32,16},{48,32},{64,48},{80,64},{96,80},{112,96},{1... | collective-permute-start | bytes 909320 | tf_op jit(solution)/shard_map/ppermute | solution.py:71
  66.8 4.6 %collective-permute-start.9 = (bf16[2,592,128]{2,1,0:T(8,128)(2,1)S(1)}, bf16[2,592,128]{2,1,0:T(8,128)(2,1)S(1)}, u32[]{:S(2)}, u32[]{:S(2)}) collective-permute-start(bf16[2,592,128]{2,1,0:T(8,128)(2,1)S(1)} %collective-permute-done.7.refs_4_), channel_id=1, source_target_pairs={{0,112},{16,0},{32,16},{48,32},{64,48},{80,64},{96,80},{112,96},{1... | collective-permute-start | bytes 909320 | tf_op jit(solution)/shard_map/ppermute | solution.py:71
  75.1 7.1 %collective-permute-start.13 = (bf16[512,896]{1,0:T(8,128)(2,1)S(1)}, bf16[512,896]{1,0:T(8,128)(2,1)S(1)}, u32[]{:S(2)}, u32[]{:S(2)}) collective-permute-start(bf16[512,896]{1,0:T(8,128)(2,1)S(1)} %collective-permute-done.12.refs_11_), channel_id=1, source_target_pairs={{0,1},{1,0},{2,3},{3,2},{4,5},{5,4},{6,7},{7,6},{8,9},{9,8},{10,11... | collective-permute-start | bytes 2752520 | tf_op jit(solution)/shard_map/ppermute | solution.py:67
  82.3 2.8 %collective-permute-start.10 = (bf16[592,128]{1,0:T(8,128)(2,1)S(1)}, bf16[592,128]{1,0:T(8,128)(2,1)S(1)}, u32[]{:S(2)}, u32[]{:S(2)}) collective-permute-start(bf16[592,128]{1,0:T(8,128)(2,1)S(1)} %slice_bitcast_fusion.2), channel_id=1, source_target_pairs={{0,16},{16,32},{32,48},{48,64},{64,80},{80,96},{96,112},{112,0},{1... | collective-permute-start | bytes 454664 | tf_op jit(solution)/shard_map/ppermute | solution.py:71
  85.1 4.4 %collective-permute-start.11 = (bf16[592,128]{1,0:T(8,128)(2,1)S(1)}, bf16[592,128]{1,0:T(8,128)(2,1)S(1)}, u32[]{:S(2)}, u32[]{:S(2)}) collective-permute-start(bf16[592,128]{1,0:T(8,128)(2,1)S(1)} %slice_bitcast_fusion.1), channel_id=1, source_target_pairs={{0,112},{16,0},{32,16},{48,32},{64,48},{80,64},{96,80},{112,96},{1... | collective-permute-start | bytes 454664 | tf_op jit(solution)/shard_map/ppermute | solution.py:71
  93.8 3.8 %shard_map.86 = (bf16[8,2,592,128]{3,2,1,0:T(8,128)(2,1)S(1)}, f32[2,592,128]{2,1,0:T(8,128)S(1)}, bf16[4,2,592,128]{3,2,1,0:T(8,128)(2,1)}) custom-call(bf16[2,592,128]{2,1,0:T(8,128)(2,1)S(1)} %pad_maximum_fusion.refs_0_, bf16[2,592,128]{2,1,0:T(8,128)(2,1)S(1)} %collective-permute-done.4.refs_1_, bf16[2,592,128]{2,1,0:T(8,128)(2,1)S(1)} %collective-permute-done.5.refs_2_, ...), custom_call_target="tpu_custom_call" | custom-call | flops 1738539008 | bytes 10338304 | tf_op jit(solution)/shard_map/pallas_call | solution.py:84
  99.0 7.8 %all-to-all-start = ((bf16[4,2,592,128]{3,2,1,0:T(8,128)(2,1)}), bf16[4,2,592,128]{3,2,1,0:T(8,128)(2,1)S(1)}, u32[]{:S(2)}, u32[]{:S(2)}) async-start(bf16[4,2,592,128]{3,2,1,0:T(8,128)(2,1)} %get-tuple-element.39), calls=%async_computation | async-start | bytes 2424832 | tf_op jit(solution)/shard_map/all_to_all | solution.py:282
  106.8 8.1 %collective-permute-start.15 = (bf16[592,128]{1,0:T(8,128)(2,1)S(1)}, bf16[592,128]{1,0:T(8,128)(2,1)S(1)}, u32[]{:S(2)}, u32[]{:S(2)}) collective-permute-start(bf16[592,128]{1,0:T(8,128)(2,1)S(1)} %collective-permute-done.2), channel_id=1, source_target_pairs={{0,2},{2,0},{1,3},{3,1},{4,6},{6,4},{5,7},{7,5},{8,10},{10,8},{9,1... | collective-permute-start | bytes 454664 | tf_op jit(solution)/shard_map/ppermute | solution.py:67
  115.0 6.5 %collective-permute-done.15 = bf16[592,128]{1,0:T(8,128)(2,1)S(1)} collective-permute-done((bf16[592,128]{1,0:T(8,128)(2,1)S(1)}, bf16[592,128]{1,0:T(8,128)(2,1)S(1)}, u32[]{:S(2)}, u32[]{:S(2)}) %collective-permute-start.15) | collective-permute-done | bytes 151584 | tf_op jit(solution)/shard_map/ppermute | solution.py:67
  125.2 3.7 %collective-permute-start.17 = (bf16[2,592,128]{2,1,0:T(8,128)(2,1)S(1)}, bf16[2,592,128]{2,1,0:T(8,128)(2,1)S(1)}, u32[]{:S(2)}, u32[]{:S(2)}) collective-permute-start(bf16[2,592,128]{2,1,0:T(8,128)(2,1)S(1)} %pad_maximum_fusion.1.c0), channel_id=1, source_target_pairs={{0,8},{4,12},{8,0},{12,4},{1,9},{5,13},{9,1},{13,5},{2,10},{6,14},... | collective-permute-start | bytes 909320 | tf_op jit(solution)/shard_map/ppermute | solution.py:71
  128.9 2.5 %collective-permute-start.18 = (bf16[2,592,128]{2,1,0:T(8,128)(2,1)S(1)}, bf16[2,592,128]{2,1,0:T(8,128)(2,1)S(1)}, u32[]{:S(2)}, u32[]{:S(2)}) collective-permute-start(bf16[2,592,128]{2,1,0:T(8,128)(2,1)S(1)} %pad_maximum_fusion.1.c0), channel_id=1, source_target_pairs={{0,12},{4,0},{8,4},{12,8},{1,13},{5,1},{9,5},{13,9},{2,14},{6,2},{... | collective-permute-start | bytes 909320 | tf_op jit(solution)/shard_map/ppermute | solution.py:71
  131.5 8.2 %collective-permute-start.14 = (bf16[1024,128]{1,0:T(8,128)(2,1)S(1)}, bf16[1024,128]{1,0:T(8,128)(2,1)S(1)}, u32[]{:S(2)}, u32[]{:S(2)}) collective-permute-start(bf16[1024,128]{1,0:T(8,128)(2,1)S(1)} %get-tuple-element.41), channel_id=1, source_target_pairs={{0,2},{2,0},{1,3},{3,1},{4,6},{6,4},{5,7},{7,5},{8,10},{10,8},{9,1... | collective-permute-start | bytes 786440 | tf_op jit(solution)/shard_map/ppermute | solution.py:67
  139.6 8.1 %collective-permute-done.14.got = bf16[1024,128]{1,0:T(8,128)(2,1)S(1)} collective-permute-done((bf16[1024,128]{1,0:T(8,128)(2,1)S(1)}, bf16[1024,128]{1,0:T(8,128)(2,1)S(1)}, u32[]{:S(2)}, u32[]{:S(2)}) %collective-permute-start.14) | collective-permute-done | bytes 262176 | tf_op jit(solution)/shard_map/ppermute | solution.py:67
  151.5 4.0 %shard_map.89 = (f32[160,320]{1,0:T(8,128)S(1)}, f32[432,864]{1,0:T(8,128)S(1)}, f32[512,896]{1,0:T(8,128)S(1)}, bf16[2,512,896]{2,1,0:T(8,128)(2,1)}) custom-call(bf16[8,2,592,128]{3,2,1,0:T(8,128)(2,1)S(1)} %copy-done.19, bf16[2,592,128]{2,1,0:T(8,128)(2,1)S(1)} %copy-done.3, bf16[2,592,128]{2,1,0:T(8,128)(2,1)S(1)} %collective-permute-done.16.c1, ...), custom_call_target="tpu_custom_call" | custom-call | flops 1738539008 | bytes 10702848 | tf_op jit(solution)/shard_map/pallas_call | solution.py:84
  157.4 6.7 %collective-permute-start.19 = (bf16[2,512,896]{2,1,0:T(8,128)(2,1)}, bf16[2,512,896]{2,1,0:T(8,128)(2,1)S(1)}, u32[]{:S(2)}, u32[]{:S(2)}) collective-permute-start(bf16[2,512,896]{2,1,0:T(8,128)(2,1)} %get-tuple-element.49), channel_id=1, source_target_pairs={{0,1},{1,0},{2,3},{3,2},{4,5},{5,4},{6,7},{7,6},{8,9},{9,8},{10,11... | collective-permute-start | bytes 5505032 | tf_op jit(solution)/shard_map/ppermute | solution.py:67
  164.1 2.8 %collective-permute-start.22 = (bf16[2,432,128]{2,1,0:T(8,128)(2,1)S(1)}, bf16[2,432,128]{2,1,0:T(8,128)(2,1)S(1)}, u32[]{:S(2)}, u32[]{:S(2)}) collective-permute-start(bf16[2,432,128]{2,1,0:T(8,128)(2,1)S(1)} %get-tuple-element.53.right), channel_id=1, source_target_pairs={{0,4},{4,8},{8,12},{12,0},{1,5},{5,9},{9,13},{13,1},{2,6},{6,10},{... | collective-permute-start | bytes 663560 | tf_op jit(solution)/shard_map/ppermute | solution.py:71
  166.9 3.2 %collective-permute-start.23 = (bf16[2,432,128]{2,1,0:T(8,128)(2,1)S(1)}, bf16[2,432,128]{2,1,0:T(8,128)(2,1)S(1)}, u32[]{:S(2)}, u32[]{:S(2)}) collective-permute-start(bf16[2,432,128]{2,1,0:T(8,128)(2,1)S(1)} %get-tuple-element.53.right), channel_id=1, source_target_pairs={{0,8},{4,12},{8,0},{12,4},{1,9},{5,13},{9,1},{13,5},{2,10},{6,14},... | collective-permute-start | bytes 663560 | tf_op jit(solution)/shard_map/ppermute | solution.py:71
  170.8 8.2 %collective-permute-done.22.r1 = bf16[2,432,128]{2,1,0:T(8,128)(2,1)S(1)} collective-permute-done((bf16[2,432,128]{2,1,0:T(8,128)(2,1)S(1)}, bf16[2,432,128]{2,1,0:T(8,128)(2,1)S(1)}, u32[]{:S(2)}, u32[]{:S(2)}) %collective-permute-start.22) | collective-permute-done | bytes 221216 | tf_op jit(solution)/shard_map/ppermute | solution.py:71
  181.3 7.2 %all-to-all-start.1 = ((bf16[16,160,128]{2,1,0:T(8,128)(2,1)}), bf16[16,160,128]{2,1,0:T(8,128)(2,1)}, u32[]{:S(2)}, u32[]{:S(2)}) async-start(bf16[16,160,128]{2,1,0:T(8,128)(2,1)} %broadcast_in_dim.3), calls=%async_computation.1 | async-start | bytes 1310720 | tf_op jit(solution)/shard_map/all_to_all | solution.py:306
  188.6 2.7 %fusion = bf16[512,896]{1,0:T(8,128)(2,1)} fusion(f32[512,896]{1,0:T(8,128)} %copy-done, bf16[2,512,896]{2,1,0:T(8,128)(2,1)S(1)} %collective-permute-done.19.got), kind=kLoop, calls=%fused_computation.1 | loop fusion | flops 1376256 | bytes 3670016 | tf_op jit(solution)/shard_map/convert_element_type | solution.py:305
  191.3 3.2 %collective-permute-start.20 = (bf16[512,896]{1,0:T(8,128)(2,1)}, bf16[512,896]{1,0:T(8,128)(2,1)}, u32[]{:S(2)}, u32[]{:S(2)}) collective-permute-start(bf16[512,896]{1,0:T(8,128)(2,1)} %fusion), channel_id=1, source_target_pairs={{0,128},{128,0},{1,129},{129,1},{2,130},{130,2},{3,131},{131,3},{4... | collective-permute-start | bytes 2752520 | tf_op jit(solution)/shard_map/ppermute | solution.py:67
  194.4 5.4 %collective-permute-start.24 = (bf16[2,432,128]{2,1,0:T(8,128)(2,1)S(1)}, bf16[2,432,128]{2,1,0:T(8,128)(2,1)S(1)}, u32[]{:S(2)}, u32[]{:S(2)}) collective-permute-start(bf16[2,432,128]{2,1,0:T(8,128)(2,1)S(1)} %copy-done.10), channel_id=1, source_target_pairs={{0,12},{4,0},{8,4},{12,8},{1,13},{5,1},{9,5},{13,9},{2,14},{6,2},{... | collective-permute-start | bytes 663560 | tf_op jit(solution)/shard_map/ppermute | solution.py:71
  199.9 2.9 %collective-permute-done.24.r3 = bf16[2,432,128]{2,1,0:T(8,128)(2,1)S(1)} collective-permute-done((bf16[2,432,128]{2,1,0:T(8,128)(2,1)S(1)}, bf16[2,432,128]{2,1,0:T(8,128)(2,1)S(1)}, u32[]{:S(2)}, u32[]{:S(2)}) %collective-permute-start.24) | collective-permute-done | bytes 221216 | tf_op jit(solution)/shard_map/ppermute | solution.py:71
  211.6 4.8 %collective-permute-start.25 = (bf16[2,320,432]{2,1,0:T(8,128)(2,1)S(1)}, bf16[2,320,432]{2,1,0:T(8,128)(2,1)S(1)}, u32[]{:S(2)}, u32[]{:S(2)}) collective-permute-start(bf16[2,320,432]{2,1,0:T(8,128)(2,1)S(1)} %get-tuple-element.56), channel_id=1, source_target_pairs={{0,1},{1,0},{2,3},{3,2},{4,5},{5,4},{6,7},{7,6},{8,9},{9,8},{10,11... | collective-permute-start | bytes 1658888 | tf_op jit(solution)/shard_map/ppermute | solution.py:67
  222.5 2.6 %shard_map.90 = (f32[160,320]{1,0:T(8,128)}, f32[432,864]{1,0:T(8,128)}) custom-call(f32[160,320]{1,0:T(8,128)S(1)} %copy-done.5, f32[432,864]{1,0:T(8,128)S(1)} %get-tuple-element.48.g_own, bf16[2,512,896]{2,1,0:T(8,128)(2,1)S(1)} %collective-permute-done.19.got, bf16[512,896]{1,0:T(8,128)(2,1)} %collective-permute-done.20.last), custom_call_target="tpu_custom_call" | custom-call | bytes 6148096 | tf_op jit(solution)/shard_map/pallas_call | solution.py:84
  225.1 5.3 %collective-permute-done.26 = bf16[320,432]{1,0:T(8,128)(2,1)S(1)} collective-permute-done((bf16[320,432]{1,0:T(8,128)(2,1)S(1)}, bf16[320,432]{1,0:T(8,128)(2,1)S(1)}, u32[]{:S(2)}, u32[]{:S(2)}) %collective-permute-start.26) | collective-permute-done | bytes 276512 | tf_op jit(solution)/shard_map/ppermute | solution.py:67
  (82 shorter events, 50.8 us)
Async XLA Ops:
  3.7 26.9 %collective-permute-start.3 = (bf16[512,896]{1,0:T(8,128)(2,1)S(1)}, bf16[512,896]{1,0:T(8,128)(2,1)S(1)}, u32[]{:S(2)}, u32[]{:S(2)}) collective-permute-start(bf16[512,896]{1,0:T(8,128)(2,1)S(1)} %shard_map.85.refs_9_), channel_id=1, source_target_pairs={{0,1},{1,0},{2,3},{3,2},{4,5},{5,4},{6,7},{7,6},{8,9},{9,8},{10,11... | collective-permute-start | bytes 2752520 | tf_op jit(solution)/shard_map/ppermute | solution.py:67
  12.5 9.2 %collective-permute-start = (bf16[592,128]{1,0:T(8,128)(2,1)S(1)}, bf16[592,128]{1,0:T(8,128)(2,1)S(1)}, u32[]{:S(2)}, u32[]{:S(2)}) collective-permute-start(bf16[592,128]{1,0:T(8,128)(2,1)S(1)} %pad_maximum_fusion.2), channel_id=1, source_target_pairs={{0,0},{1,1},{2,128},{3,129},{4,64},{5,65},{6,192},{7,193},{8,256},... | collective-permute-start | bytes 454664 | tf_op jit(solution)/shard_map/ppermute | solution.py:258
  13.1 17.4 %collective-permute-start.1 = (bf16[592,128]{1,0:T(8,128)(2,1)S(1)}, bf16[592,128]{1,0:T(8,128)(2,1)S(1)}, u32[]{:S(2)}, u32[]{:S(2)}) collective-permute-start(bf16[592,128]{1,0:T(8,128)(2,1)S(1)} %pad_maximum_fusion.2), channel_id=1, source_target_pairs={{0,256},{1,257},{2,384},{3,385},{4,320},{5,321},{6,448},{7,449},{8... | collective-permute-start | bytes 454664 | tf_op jit(solution)/shard_map/ppermute | solution.py:259
  21.0 9.6 %collective-permute-start.2 = (bf16[592,128]{1,0:T(8,128)(2,1)S(1)}, bf16[592,128]{1,0:T(8,128)(2,1)S(1)}, u32[]{:S(2)}, u32[]{:S(2)}) collective-permute-start(bf16[592,128]{1,0:T(8,128)(2,1)S(1)} %pad_maximum_fusion.2), channel_id=1, source_target_pairs={{0,0},{1,1},{2,128},{3,129},{4,4},{5,5},{6,132},{7,133},{8,8},{9,9... | collective-permute-start | bytes 454664 | tf_op jit(solution)/shard_map/ppermute | solution.py:260
  30.6 13.9 %collective-permute-start.4 = (bf16[2,592,128]{2,1,0:T(8,128)(2,1)S(1)}, bf16[2,592,128]{2,1,0:T(8,128)(2,1)S(1)}, u32[]{:S(2)}, u32[]{:S(2)}) collective-permute-start(bf16[2,592,128]{2,1,0:T(8,128)(2,1)S(1)} %pad_maximum_fusion.refs_0_), channel_id=1, source_target_pairs={{0,16},{16,32},{32,48},{48,64},{64,80},{80,96},{96,112},{112,0},{1... | collective-permute-start | bytes 909320 | tf_op jit(solution)/shard_map/ppermute | solution.py:71
  32.5 12.9 %collective-permute-start.5 = (bf16[2,592,128]{2,1,0:T(8,128)(2,1)S(1)}, bf16[2,592,128]{2,1,0:T(8,128)(2,1)S(1)}, u32[]{:S(2)}, u32[]{:S(2)}) collective-permute-start(bf16[2,592,128]{2,1,0:T(8,128)(2,1)S(1)} %pad_maximum_fusion.refs_0_), channel_id=1, source_target_pairs={{0,112},{16,0},{32,16},{48,32},{64,48},{80,64},{96,80},{112,96},{1... | collective-permute-start | bytes 909320 | tf_op jit(solution)/shard_map/ppermute | solution.py:71
  45.4 29.7 %collective-permute-start.12 = (bf16[512,896]{1,0:T(8,128)(2,1)S(1)}, bf16[512,896]{1,0:T(8,128)(2,1)S(1)}, u32[]{:S(2)}, u32[]{:S(2)}) collective-permute-start(bf16[512,896]{1,0:T(8,128)(2,1)S(1)} %shard_map.85.refs_9_), channel_id=1, source_target_pairs={{0,128},{128,0},{1,129},{129,1},{2,130},{130,2},{3,131},{131,3},{4... | collective-permute-start | bytes 2752520 | tf_op jit(solution)/shard_map/ppermute | solution.py:67
  55.4 9.5 %collective-permute-start.6 = (bf16[2,592,128]{2,1,0:T(8,128)(2,1)S(1)}, bf16[2,592,128]{2,1,0:T(8,128)(2,1)S(1)}, u32[]{:S(2)}, u32[]{:S(2)}) collective-permute-start(bf16[2,592,128]{2,1,0:T(8,128)(2,1)S(1)} %collective-permute-done.4.refs_1_), channel_id=1, source_target_pairs={{0,16},{16,32},{32,48},{48,64},{64,80},{80,96},{96,112},{112,0},{1... | collective-permute-start | bytes 909320 | tf_op jit(solution)/shard_map/ppermute | solution.py:71
  57.3 9.5 %collective-permute-start.7 = (bf16[2,592,128]{2,1,0:T(8,128)(2,1)S(1)}, bf16[2,592,128]{2,1,0:T(8,128)(2,1)S(1)}, u32[]{:S(2)}, u32[]{:S(2)}) collective-permute-start(bf16[2,592,128]{2,1,0:T(8,128)(2,1)S(1)} %collective-permute-done.5.refs_2_), channel_id=1, source_target_pairs={{0,112},{16,0},{32,16},{48,32},{64,48},{80,64},{96,80},{112,96},{1... | collective-permute-start | bytes 909320 | tf_op jit(solution)/shard_map/ppermute | solution.py:71
  64.9 8.8 %collective-permute-start.8 = (bf16[2,592,128]{2,1,0:T(8,128)(2,1)S(1)}, bf16[2,592,128]{2,1,0:T(8,128)(2,1)S(1)}, u32[]{:S(2)}, u32[]{:S(2)}) collective-permute-start(bf16[2,592,128]{2,1,0:T(8,128)(2,1)S(1)} %collective-permute-done.6.refs_3_), channel_id=1, source_target_pairs={{0,16},{16,32},{32,48},{48,64},{64,80},{80,96},{96,112},{112,0},{1... | collective-permute-start | bytes 909320 | tf_op jit(solution)/shard_map/ppermute | solution.py:71
  66.8 8.3 %collective-permute-start.9 = (bf16[2,592,128]{2,1,0:T(8,128)(2,1)S(1)}, bf16[2,592,128]{2,1,0:T(8,128)(2,1)S(1)}, u32[]{:S(2)}, u32[]{:S(2)}) collective-permute-start(bf16[2,592,128]{2,1,0:T(8,128)(2,1)S(1)} %collective-permute-done.7.refs_4_), channel_id=1, source_target_pairs={{0,112},{16,0},{32,16},{48,32},{64,48},{80,64},{96,80},{112,96},{1... | collective-permute-start | bytes 909320 | tf_op jit(solution)/shard_map/ppermute | solution.py:71
  75.1 18.7 %collective-permute-start.13 = (bf16[512,896]{1,0:T(8,128)(2,1)S(1)}, bf16[512,896]{1,0:T(8,128)(2,1)S(1)}, u32[]{:S(2)}, u32[]{:S(2)}) collective-permute-start(bf16[512,896]{1,0:T(8,128)(2,1)S(1)} %collective-permute-done.12.refs_11_), channel_id=1, source_target_pairs={{0,1},{1,0},{2,3},{3,2},{4,5},{5,4},{6,7},{7,6},{8,9},{9,8},{10,11... | collective-permute-start | bytes 2752520 | tf_op jit(solution)/shard_map/ppermute | solution.py:67
  82.3 9.6 %collective-permute-start.10 = (bf16[592,128]{1,0:T(8,128)(2,1)S(1)}, bf16[592,128]{1,0:T(8,128)(2,1)S(1)}, u32[]{:S(2)}, u32[]{:S(2)}) collective-permute-start(bf16[592,128]{1,0:T(8,128)(2,1)S(1)} %slice_bitcast_fusion.2), channel_id=1, source_target_pairs={{0,16},{16,32},{32,48},{48,64},{64,80},{80,96},{96,112},{112,0},{1... | collective-permute-start | bytes 454664 | tf_op jit(solution)/shard_map/ppermute | solution.py:71
  85.1 8.7 %collective-permute-start.11 = (bf16[592,128]{1,0:T(8,128)(2,1)S(1)}, bf16[592,128]{1,0:T(8,128)(2,1)S(1)}, u32[]{:S(2)}, u32[]{:S(2)}) collective-permute-start(bf16[592,128]{1,0:T(8,128)(2,1)S(1)} %slice_bitcast_fusion.1), channel_id=1, source_target_pairs={{0,112},{16,0},{32,16},{48,32},{64,48},{80,64},{96,80},{112,96},{1... | collective-permute-start | bytes 454664 | tf_op jit(solution)/shard_map/ppermute | solution.py:71
  99.0 23.6 %all-to-all-start = ((bf16[4,2,592,128]{3,2,1,0:T(8,128)(2,1)}), bf16[4,2,592,128]{3,2,1,0:T(8,128)(2,1)S(1)}, u32[]{:S(2)}, u32[]{:S(2)}) async-start(bf16[4,2,592,128]{3,2,1,0:T(8,128)(2,1)} %get-tuple-element.39), calls=%async_computation | async-start | bytes 2424832 | tf_op jit(solution)/shard_map/all_to_all | solution.py:282
  106.8 14.6 %collective-permute-start.15 = (bf16[592,128]{1,0:T(8,128)(2,1)S(1)}, bf16[592,128]{1,0:T(8,128)(2,1)S(1)}, u32[]{:S(2)}, u32[]{:S(2)}) collective-permute-start(bf16[592,128]{1,0:T(8,128)(2,1)S(1)} %collective-permute-done.2), channel_id=1, source_target_pairs={{0,2},{2,0},{1,3},{3,1},{4,6},{6,4},{5,7},{7,5},{8,10},{10,8},{9,1... | collective-permute-start | bytes 454664 | tf_op jit(solution)/shard_map/ppermute | solution.py:67
  121.4 26.4 %copy-start.2 = (bf16[2,592,128]{2,1,0:T(8,128)(2,1)}, bf16[2,592,128]{2,1,0:T(8,128)(2,1)S(1)}, u32[]{:S(2)}) copy-start(bf16[2,592,128]{2,1,0:T(8,128)(2,1)S(1)} %pad_maximum_fusion.1.c0) | copy-start | bytes 909316
  122.6 25.2 %copy-start.7 = (f32[864,432]{0,1:T(8,128)S(1)}, f32[864,432]{0,1:T(8,128)}, u32[]{:S(2)}) copy-start(f32[864,432]{0,1:T(8,128)} %param.9) | copy-start | bytes 4478980
  122.9 24.9 %collective-permute-start.16 = (bf16[2,592,128]{2,1,0:T(8,128)(2,1)S(1)}, bf16[2,592,128]{2,1,0:T(8,128)(2,1)S(1)}, u32[]{:S(2)}, u32[]{:S(2)}) collective-permute-start(bf16[2,592,128]{2,1,0:T(8,128)(2,1)S(1)} %pad_maximum_fusion.1.c0), channel_id=1, source_target_pairs={{0,4},{4,8},{8,12},{12,0},{1,5},{5,9},{9,13},{13,1},{2,6},{6,10},{... | collective-permute-start | bytes 909320 | tf_op jit(solution)/shard_map/ppermute | solution.py:71
  125.2 22.6 %collective-permute-start.17 = (bf16[2,592,128]{2,1,0:T(8,128)(2,1)S(1)}, bf16[2,592,128]{2,1,0:T(8,128)(2,1)S(1)}, u32[]{:S(2)}, u32[]{:S(2)}) collective-permute-start(bf16[2,592,128]{2,1,0:T(8,128)(2,1)S(1)} %pad_maximum_fusion.1.c0), channel_id=1, source_target_pairs={{0,8},{4,12},{8,0},{12,4},{1,9},{5,13},{9,1},{13,5},{2,10},{6,14},... | collective-permute-start | bytes 909320 | tf_op jit(solution)/shard_map/ppermute | solution.py:71
  128.9 18.9 %collective-permute-start.18 = (bf16[2,592,128]{2,1,0:T(8,128)(2,1)S(1)}, bf16[2,592,128]{2,1,0:T(8,128)(2,1)S(1)}, u32[]{:S(2)}, u32[]{:S(2)}) collective-permute-start(bf16[2,592,128]{2,1,0:T(8,128)(2,1)S(1)} %pad_maximum_fusion.1.c0), channel_id=1, source_target_pairs={{0,12},{4,0},{8,4},{12,8},{1,13},{5,1},{9,5},{13,9},{2,14},{6,2},{... | collective-permute-start | bytes 909320 | tf_op jit(solution)/shard_map/ppermute | solution.py:71
  131.5 16.3 %collective-permute-start.14 = (bf16[1024,128]{1,0:T(8,128)(2,1)S(1)}, bf16[1024,128]{1,0:T(8,128)(2,1)S(1)}, u32[]{:S(2)}, u32[]{:S(2)}) collective-permute-start(bf16[1024,128]{1,0:T(8,128)(2,1)S(1)} %get-tuple-element.41), channel_id=1, source_target_pairs={{0,2},{2,0},{1,3},{3,1},{4,6},{6,4},{5,7},{7,5},{8,10},{10,8},{9,1... | collective-permute-start | bytes 786440 | tf_op jit(solution)/shard_map/ppermute | solution.py:67
  147.8 19.1 %copy-start.9 = (bf16[2,432,128]{2,1,0:T(8,128)(2,1)}, bf16[2,432,128]{2,1,0:T(8,128)(2,1)S(1)}, u32[]{:S(2)}) copy-start(bf16[2,432,128]{2,1,0:T(8,128)(2,1)S(1)} %get-tuple-element.53.right) | copy-start | bytes 663556
  157.4 31.2 %collective-permute-start.19 = (bf16[2,512,896]{2,1,0:T(8,128)(2,1)}, bf16[2,512,896]{2,1,0:T(8,128)(2,1)S(1)}, u32[]{:S(2)}, u32[]{:S(2)}) collective-permute-start(bf16[2,512,896]{2,1,0:T(8,128)(2,1)} %get-tuple-element.49), channel_id=1, source_target_pairs={{0,1},{1,0},{2,3},{3,2},{4,5},{5,4},{6,7},{7,6},{8,9},{9,8},{10,11... | collective-permute-start | bytes 5505032 | tf_op jit(solution)/shard_map/ppermute | solution.py:67
  164.1 14.9 %collective-permute-start.22 = (bf16[2,432,128]{2,1,0:T(8,128)(2,1)S(1)}, bf16[2,432,128]{2,1,0:T(8,128)(2,1)S(1)}, u32[]{:S(2)}, u32[]{:S(2)}) collective-permute-start(bf16[2,432,128]{2,1,0:T(8,128)(2,1)S(1)} %get-tuple-element.53.right), channel_id=1, source_target_pairs={{0,4},{4,8},{8,12},{12,0},{1,5},{5,9},{9,13},{13,1},{2,6},{6,10},{... | collective-permute-start | bytes 663560 | tf_op jit(solution)/shard_map/ppermute | solution.py:71
  166.9 12.8 %collective-permute-start.23 = (bf16[2,432,128]{2,1,0:T(8,128)(2,1)S(1)}, bf16[2,432,128]{2,1,0:T(8,128)(2,1)S(1)}, u32[]{:S(2)}, u32[]{:S(2)}) collective-permute-start(bf16[2,432,128]{2,1,0:T(8,128)(2,1)S(1)} %get-tuple-element.53.right), channel_id=1, source_target_pairs={{0,8},{4,12},{8,0},{12,4},{1,9},{5,13},{9,1},{13,5},{2,10},{6,14},... | collective-permute-start | bytes 663560 | tf_op jit(solution)/shard_map/ppermute | solution.py:71
  170.1 0.7 collective-permute-start.21
  181.3 24.2 %all-to-all-start.1 = ((bf16[16,160,128]{2,1,0:T(8,128)(2,1)}), bf16[16,160,128]{2,1,0:T(8,128)(2,1)}, u32[]{:S(2)}, u32[]{:S(2)}) async-start(bf16[16,160,128]{2,1,0:T(8,128)(2,1)} %broadcast_in_dim.3), calls=%async_computation.1 | async-start | bytes 1310720 | tf_op jit(solution)/shard_map/all_to_all | solution.py:306
  191.3 29.2 %collective-permute-start.20 = (bf16[512,896]{1,0:T(8,128)(2,1)}, bf16[512,896]{1,0:T(8,128)(2,1)}, u32[]{:S(2)}, u32[]{:S(2)}) collective-permute-start(bf16[512,896]{1,0:T(8,128)(2,1)} %fusion), channel_id=1, source_target_pairs={{0,128},{128,0},{1,129},{129,1},{2,130},{130,2},{3,131},{131,3},{4... | collective-permute-start | bytes 2752520 | tf_op jit(solution)/shard_map/ppermute | solution.py:67
  194.4 8.3 %collective-permute-start.24 = (bf16[2,432,128]{2,1,0:T(8,128)(2,1)S(1)}, bf16[2,432,128]{2,1,0:T(8,128)(2,1)S(1)}, u32[]{:S(2)}, u32[]{:S(2)}) collective-permute-start(bf16[2,432,128]{2,1,0:T(8,128)(2,1)S(1)} %copy-done.10), channel_id=1, source_target_pairs={{0,12},{4,0},{8,4},{12,8},{1,13},{5,1},{9,5},{13,9},{2,14},{6,2},{... | collective-permute-start | bytes 663560 | tf_op jit(solution)/shard_map/ppermute | solution.py:71
  211.6 6.5 %collective-permute-start.25 = (bf16[2,320,432]{2,1,0:T(8,128)(2,1)S(1)}, bf16[2,320,432]{2,1,0:T(8,128)(2,1)S(1)}, u32[]{:S(2)}, u32[]{:S(2)}) collective-permute-start(bf16[2,320,432]{2,1,0:T(8,128)(2,1)S(1)} %get-tuple-element.56), channel_id=1, source_target_pairs={{0,1},{1,0},{2,3},{3,2},{4,5},{5,4},{6,7},{7,6},{8,9},{9,8},{10,11... | collective-permute-start | bytes 1658888 | tf_op jit(solution)/shard_map/ppermute | solution.py:67
  220.5 9.8 %collective-permute-start.26 = (bf16[320,432]{1,0:T(8,128)(2,1)S(1)}, bf16[320,432]{1,0:T(8,128)(2,1)S(1)}, u32[]{:S(2)}, u32[]{:S(2)}) collective-permute-start(bf16[320,432]{1,0:T(8,128)(2,1)S(1)} %fusion.1), channel_id=1, source_target_pairs={{0,128},{128,0},{1,129},{129,1},{2,130},{130,2},{3,131},{131,3},{4... | collective-permute-start | bytes 829448 | tf_op jit(solution)/shard_map/ppermute | solution.py:67
  (17 other events, 33.9 us)

commit v3 on v2

--- a/solution.py
+++ b/solution.py
@@ -87,7 +87,7 @@
         in_specs=[VMEM] * len(args),
         out_specs=jax.tree.map(lambda _: VMEM, out),
         scratch_shapes=list(scratch),
-        compiler_params=pltpu.CompilerParams(vmem_limit_bytes=16 * 1024 * 1024),
+        compiler_params=pltpu.CompilerParams(vmem_limit_bytes=8 * 1024 * 1024),
         cost_estimate=pl.CostEstimate(flops=flops, bytes_accessed=size, transcendentals=0),
     )(*args)
 
@@ -115,7 +115,7 @@
 
 def sides_kernel(da, dg, h, *refs):
     ring, inverses = refs[: RING + 1], refs[RING + 1 : RING + 5]
-    rows, own, send, acc = refs[RING + 5 :]
+    rows, own, s1, s2, s3, acc = refs[RING + 5 :]
     core, zg, p, y = (lax.axis_index(a) for a in ("core", "zg", "p", "y"))
     group = lax.axis_index("xh")
     x = 2 * group + lax.axis_index("xl")
@@ -152,17 +152,14 @@
                 for xh in range(2):
                     acc[2 * xh + xl, lax.bitwise_xor(p, q), lo:hi, :] = total[:, xh * n : (xh + 1) * n]
     own[...] = acc[x]
-    send[...] = acc[...].astype(send.dtype)
-
-
-def first_sum_kernel(da, own, got, keep, send):
+    for ahead, ref in enumerate((s1, s2, s3)):
+        ref[...] = acc[lax.rem(x + ahead + 1, 4)].astype(ref.dtype)
+
+
+def first_sum_kernel(da, own, r1, r2, r3, keep, send):
     w = lax.axis_index("w")
-    x = 2 * lax.axis_index("xh") + lax.axis_index("xl")
     dg = own.shape[1] - da
-    total = own[...]
-    for i in range(1, 4):
-        total = total + got[lax.rem(x + i, 4)].astype(f32)
-    keep[...] = total
+    keep[...] = ((own[...] + r1[...].astype(f32)) + r2[...].astype(f32)) + r3[...].astype(f32)
     for t in range(2):
         send[t * dg : (t + 1) * dg, :] = keep[t, da:, :].astype(send.dtype)
     send[2 * dg :, :] = keep[1 - w, :da, :].astype(send.dtype)
@@ -220,7 +217,7 @@
 
 
 def product_kernel(h, scale, left, right, r1, r2, r3, own, keep, send, held):
-    core, p, group = lax.axis_index("core"), lax.axis_index("p"), lax.axis_index("xh")
+    core, p, group = (lax.axis_index(a) for a in ("core", "p", "xh"))
     x = 2 * group + lax.axis_index("xl")
     n = left.shape[1]
     for behind, ref in enumerate((right, r1, r2, r3)):
@@ -262,31 +259,33 @@
         )
     )
     u = jnp.stack([first, second])
+    inverse_z = swap(after(inverse, u), "p")
     up, down = [u], [u]
-    for _ in range(3):
+    for stage in range(3):
+        if stage == 2:
+            col = jnp.stack([col, swap(col, "w")])
+            up[2], down[2], col = lax.optimization_barrier((up[2], down[2], col))
         up.append(shift(up[-1], "y", RING, 1))
         down.append(shift(down[-1], "y", RING, -1))
+    cols = [shift(col, X, 4, i + 1) for i in range(3)]
+    halves = lax.optimization_barrier((up[3][0], down[3][1], *cols))
+    cols = list(halves[2:])
     ring = [u, up[1], down[1], up[2], down[2], up[3], down[3]]
-    ring += [shift(up[3][0], "y", RING, 1), shift(down[3][1], "y", RING, -1)]
-
-    inverse_z = swap(after(inverse, up[1], down[1]), "p")
-    inverse_zc = swap(after(inverse_z, up[3], down[3]), "core")
-
-    rows, own, send = call(
+    ring += [shift(halves[0], "y", RING, 1), shift(halves[1], "y", RING, -1)]
+    inverse_zc = swap(inverse_z, "core")
+
+    rows, own, *ahead = call(
         functools.partial(sides_kernel, da, dg, h),
-        (shape((RING, *pair), bf16), shape(pair, f32), shape((4, *pair), bf16)),
+        (shape((RING, *pair), bf16), shape(pair, f32)) + (shape(pair, bf16),) * 3,
         work, *ring, inverse, inverse_c, inverse_z, inverse_zc,
         scratch=[pltpu.VMEM((4, *pair), f32)],
     )
-    col = jnp.stack([col, swap(after(col, send), "w")])
-    got = lax.all_to_all(send, X, 0, 0, tiled=True)
+    got = [shift(part, X, 4, i + 1) for i, part in enumerate(ahead)]
     keep, send = call(
         functools.partial(first_sum_kernel, da),
         (shape(pair, f32), shape((2 * dg + da, block), bf16)),
-        0, own, got,
-    )
-    col = after(col, send)
-    cols = [shift(col, X, 4, i + 1) for i in range(3)]
+        0, own, *got,
+    )
     left, right = call(
         functools.partial(second_sum_kernel, da),
         (shape((da, block), bf16), shape((2, dg, block), bf16)),
@@ -295,29 +294,30 @@
     i_own, g_own, f_keep, f_send = call(
         functools.partial(factor_kernel, da, dg, h, (1.0 - decay_rate) / tokens),
         (shape((da, da * h), f32), shape((dg, dg * h), f32), shape(pack, f32), shape((2, *pack), bf16)),
-        work, after(rows, left), col, *cols, input_prior.T, gradient_prior.T,
+        work, rows, col, *cols, input_prior.T, gradient_prior.T,
         scratch=[pltpu.VMEM((4, *pair), bf16)],
     )
     piece = lax.ppermute(left, AXES, piece_perm())
     rights = [shift(right, X, 4, i + 1) for i in range(3)]
 
-    f_got = swap(f_send, "core")
-    f_mid = (f_keep + f_got[1].astype(f32)).astype(bf16)
-    lefts = lax.all_to_all(jnp.broadcast_to(after(piece, *rights[:2]), (16, *piece.shape)), ("zg", "y"), 0, 0, tiled=True)
+    f_got = swap(after(f_send, send), "core")
+    f_mid = after((f_keep + f_got[1].astype(f32)).astype(bf16), left)
     f_last = swap(f_mid, "p")
+    pieces = jnp.broadcast_to(after(piece, *rights, f_last), (16, *piece.shape))
+    lefts = lax.all_to_all(pieces, ("zg", "y"), 0, 0, tiled=True)
+
     input_factor, gradient_factor = call(
         functools.partial(factor_sum_kernel, da, dg, h),
         (shape((da, da * h), f32), shape((dg, dg * h), f32)),
-        0, i_own, g_own, f_got, f_last,
-    )
-
+        0, after(i_own, lefts), g_own, f_got, f_last,
+    )
     p_own, p_keep, p_send = call(
         functools.partial(product_kernel, h, 1.0 / tokens),
         (shape((da * h, dg), f32), shape((da * h, dg), f32), shape((2, da * h, dg), bf16)),
         2 * tokens * h * da * dg, lefts, right, *rights,
         scratch=[pltpu.VMEM((4, 2, dg, block), bf16)],
     )
-    p_got = after(swap(p_send, "core"), f_last)
+    p_got = swap(p_send, "core")
     p_last = swap((p_keep + p_got[1].astype(f32)).astype(bf16), "p")
     preconditioned = (p_own + p_got[0].astype(f32) + p_last.astype(f32)).astype(bf16)
     return input_factor.T, gradient_factor.T, preconditioned

time: 236 us -> 239 us (1.013); the launches traced: 231 us -> 238 us
  blocking collectives: 0 us -> 27 us
  local copies, waits for them, and re-layouts: 15.8 us -> 2.15 us
  waiting for transfers between devices: 62.5 us -> 69.5 us
  starting transfers between devices: 134 us -> 128 us
  Pallas kernels: 13.1 us -> 8.44 us
  other arithmetic: 4.59 us -> 2.12 us
    all_to_all x0 -> x1, blocking collectives: none -> 27 us  [local(): lefts = lax.all_to_all(pieces, ('zg', 'y'), 0, 0, tiled=True)]
    ppermute x14 -> x17, starting transfers between devices: 50.5 us -> 65.8 us  [shift(): return lax.ppermute(x, axis, [(i, (i + by) % size) for i in range(size)])]
    all_to_all x2 -> x0, starting transfers between devices: 15.1 us -> none  [the longest x1 7.82 us: local(): got = lax.all_to_all(send, X, 0, 0, tiled=True)]
    unnamed x40 -> x8, local copies, waits for them, and re-layouts: 14.8 us -> 2.04 us
    ppermute x9, waiting for transfers between devices: 23.9 us -> 31.4 us  [swap(): return lax.ppermute(x, axis, [(0, 1), (1, 0)])]
    ppermute x1, starting transfers between devices: 7.86 us -> 1.92 us  [local(): lax.ppermute(x, AXES, panel_perm(1))]
    ppermute x14 -> x17, waiting for transfers between devices: 26.6 us -> 31.7 us  [shift(): return lax.ppermute(x, axis, [(i, (i + by) % size) for i in range(size)])]
    pallas_call x7, Pallas kernels: 13.1 us -> 8.44 us  [call(): pl.pallas_call(kernel, out_shape=out, in_specs=[VMEM] * len(args), out_sp...]
  transfers between devices with their start and end apart: 29 -> 30, of which waited for: 17 -> 17; matrix products, arithmetic and copies ran while one was open for 2% -> 0% of each run, Pallas kernels for 2% -> 2%
where the time goes in v3:
time: 239 us; the launch traced here: 238 us
  starting transfers between devices  128 us (54%)
  waiting for transfers between devices  69.5 us (29%)
  blocking collectives  27 us (11%)
  Pallas kernels  8.44 us (4%)
    ppermute x17, starting transfers between devices, shift(): return lax.ppermute(x, axis, [(i, (i + by) % size) for i in range(size)])  65.8 us
    ppermute x9, starting transfers between devices, swap(): return lax.ppermute(x, axis, [(0, 1), (1, 0)])  58.3 us
    ppermute x17, waiting for transfers between devices, shift(): return lax.ppermute(x, axis, [(i, (i + by) % size) for i in range(size)])  31.7 us
    ppermute x9, waiting for transfers between devices, swap(): return lax.ppermute(x, axis, [(0, 1), (1, 0)])  31.4 us
    all_to_all x1, blocking collectives, local(): lefts = lax.all_to_all(pieces, ('zg', 'y'), 0, 0, tiled=True)  27 us
    pallas_call x7, Pallas kernels, call(): pl.pallas_call(kernel, out_shape=out, in_specs=[VMEM] * len(args), out_sp...  8.44 us
    ppermute x1, waiting for transfers between devices, local(): lax.ppermute(x, AXES, panel_perm(1))  6.34 us
  transfers between devices with their start and end apart: 30, of which 17 were waited for; matrix products, arithmetic and copies ran while one was open for 0% of the time, Pallas kernels for 2%

profile of v3, /device:TPU:1, one launch (start us, length us, event | category | flops | bytes accessed | tf_op | source)
XLA Modules:
  0.0 238.4 jit_solution(2648341172013203911)
XLA Ops:
  3.7 8.8 %collective-permute-start.3 = (bf16[512,896]{1,0:T(8,128)(2,1)S(1)}, bf16[512,896]{1,0:T(8,128)(2,1)S(1)}, u32[]{:S(2)}, u32[]{:S(2)}) collective-permute-start(bf16[512,896]{1,0:T(8,128)(2,1)S(1)} %shard_map.85.refs_9_), channel_id=1, source_target_pairs={{0,1},{1,0},{2,3},{3,2},{4,5},{5,4},{6,7},{7,6},{8,9},{9,8},{10,11... | collective-permute-start | bytes 2752520 | tf_op jit(solution)/shard_map/ppermute | solution.py:67
  15.8 6.3 %collective-permute-done.1 = bf16[592,128]{1,0:T(8,128)(2,1)S(1)} collective-permute-done((bf16[592,128]{1,0:T(8,128)(2,1)S(1)}, bf16[592,128]{1,0:T(8,128)(2,1)S(1)}, u32[]{:S(2)}, u32[]{:S(2)}) %collective-permute-start.1) | collective-permute-done | bytes 151584 | tf_op jit(solution)/shard_map/ppermute | solution.py:256
  22.1 17.9 %collective-permute-start.16 = (bf16[512,896]{1,0:T(8,128)(2,1)S(1)}, bf16[512,896]{1,0:T(8,128)(2,1)S(1)}, u32[]{:S(2)}, u32[]{:S(2)}) collective-permute-start(bf16[512,896]{1,0:T(8,128)(2,1)S(1)} %shard_map.85.refs_9_), channel_id=1, source_target_pairs={{0,128},{128,0},{1,129},{129,1},{2,130},{130,2},{3,131},{131,3},{4... | collective-permute-start | bytes 2752520 | tf_op jit(solution)/shard_map/ppermute | solution.py:67
  40.1 10.2 %collective-permute-start.5 = (bf16[2,592,128]{2,1,0:T(8,128)(2,1)S(1)}, bf16[2,592,128]{2,1,0:T(8,128)(2,1)S(1)}, u32[]{:S(2)}, u32[]{:S(2)}) collective-permute-start(bf16[2,592,128]{2,1,0:T(8,128)(2,1)S(1)} %pad_maximum_fusion.refs_0_), channel_id=1, source_target_pairs={{0,112},{16,0},{32,16},{48,32},{64,48},{80,64},{96,80},{112,96},{1... | collective-permute-start | bytes 909320 | tf_op jit(solution)/shard_map/ppermute | solution.py:71
  50.3 1.9 collective-permute-start.4
  52.3 2.7 %collective-permute-done.5.refs_2_ = bf16[2,592,128]{2,1,0:T(8,128)(2,1)S(1)} collective-permute-done((bf16[2,592,128]{2,1,0:T(8,128)(2,1)S(1)}, bf16[2,592,128]{2,1,0:T(8,128)(2,1)S(1)}, u32[]{:S(2)}, u32[]{:S(2)}) %collective-permute-start.5) | collective-permute-done | bytes 303136 | tf_op jit(solution)/shard_map/ppermute | solution.py:71
  54.9 7.6 %collective-permute-start.7 = (bf16[2,592,128]{2,1,0:T(8,128)(2,1)S(1)}, bf16[2,592,128]{2,1,0:T(8,128)(2,1)S(1)}, u32[]{:S(2)}, u32[]{:S(2)}) collective-permute-start(bf16[2,592,128]{2,1,0:T(8,128)(2,1)S(1)} %collective-permute-done.5.refs_2_), channel_id=1, source_target_pairs={{0,112},{16,0},{32,16},{48,32},{64,48},{80,64},{96,80},{112,96},{1... | collective-permute-start | bytes 909320 | tf_op jit(solution)/shard_map/ppermute | solution.py:71
  67.1 8.0 %collective-permute-done.8 = bf16[592,128]{1,0:T(8,128)(2,1)S(1)} collective-permute-done((bf16[592,128]{1,0:T(8,128)(2,1)S(1)}, bf16[592,128]{1,0:T(8,128)(2,1)S(1)}, u32[]{:S(2)}, u32[]{:S(2)}) %collective-permute-start.8) | collective-permute-done | bytes 151584 | tf_op jit(solution)/shard_map/ppermute | solution.py:67
  77.1 7.2 %collective-permute-start.17 = (bf16[512,896]{1,0:T(8,128)(2,1)S(1)}, bf16[512,896]{1,0:T(8,128)(2,1)S(1)}, u32[]{:S(2)}, u32[]{:S(2)}) collective-permute-start(bf16[512,896]{1,0:T(8,128)(2,1)S(1)} %collective-permute-done.16.refs_11_), channel_id=1, source_target_pairs={{0,1},{1,0},{2,3},{3,2},{4,5},{5,4},{6,7},{7,6},{8,9},{9,8},{10,11... | collective-permute-start | bytes 2752520 | tf_op jit(solution)/shard_map/ppermute | solution.py:67
  84.3 5.4 %collective-permute-start.10 = (bf16[2,592,128]{2,1,0:T(8,128)(2,1)S(1)}, bf16[2,592,128]{2,1,0:T(8,128)(2,1)S(1)}, u32[]{:S(2)}, u32[]{:S(2)}) collective-permute-start(bf16[2,592,128]{2,1,0:T(8,128)(2,1)S(1)} %collective-permute-done.7.refs_4_), channel_id=1, source_target_pairs={{0,112},{16,0},{32,16},{48,32},{64,48},{80,64},{96,80},{112,96},{1... | collective-permute-start | bytes 909320 | tf_op jit(solution)/shard_map/ppermute | solution.py:71
  89.8 2.4 %collective-permute-start.13 = (bf16[2,592,128]{2,1,0:T(8,128)(2,1)S(1)}, bf16[2,592,128]{2,1,0:T(8,128)(2,1)S(1)}, u32[]{:S(2)}, u32[]{:S(2)}) collective-permute-start(bf16[2,592,128]{2,1,0:T(8,128)(2,1)S(1)} %pad_maximum_fusion.1.c0), channel_id=1, source_target_pairs={{0,12},{4,0},{8,4},{12,8},{1,13},{5,1},{9,5},{13,9},{2,14},{6,2},{... | collective-permute-start | bytes 909320 | tf_op jit(solution)/shard_map/ppermute | solution.py:71
  92.2 5.1 %collective-permute-start.12 = (bf16[2,592,128]{2,1,0:T(8,128)(2,1)S(1)}, bf16[2,592,128]{2,1,0:T(8,128)(2,1)S(1)}, u32[]{:S(2)}, u32[]{:S(2)}) collective-permute-start(bf16[2,592,128]{2,1,0:T(8,128)(2,1)S(1)} %pad_maximum_fusion.1.c0), channel_id=1, source_target_pairs={{0,8},{4,12},{8,0},{12,4},{1,9},{5,13},{9,1},{13,5},{2,10},{6,14},... | collective-permute-start | bytes 909320 | tf_op jit(solution)/shard_map/ppermute | solution.py:71
  101.0 3.4 %collective-permute-done.12.c2 = bf16[2,592,128]{2,1,0:T(8,128)(2,1)S(1)} collective-permute-done((bf16[2,592,128]{2,1,0:T(8,128)(2,1)S(1)}, bf16[2,592,128]{2,1,0:T(8,128)(2,1)S(1)}, u32[]{:S(2)}, u32[]{:S(2)}) %collective-permute-start.12) | collective-permute-done | bytes 303136 | tf_op jit(solution)/shard_map/ppermute | solution.py:71
  104.3 7.1 %collective-permute-done.11.c1 = bf16[2,592,128]{2,1,0:T(8,128)(2,1)S(1)} collective-permute-done((bf16[2,592,128]{2,1,0:T(8,128)(2,1)S(1)}, bf16[2,592,128]{2,1,0:T(8,128)(2,1)S(1)}, u32[]{:S(2)}, u32[]{:S(2)}) %collective-permute-start.11) | collective-permute-done | bytes 303136 | tf_op jit(solution)/shard_map/ppermute | solution.py:71
  113.4 4.6 %collective-permute-start.15 = (bf16[592,128]{1,0:T(8,128)(2,1)S(1)}, bf16[592,128]{1,0:T(8,128)(2,1)S(1)}, u32[]{:S(2)}, u32[]{:S(2)}) collective-permute-start(bf16[592,128]{1,0:T(8,128)(2,1)S(1)} %slice_bitcast_fusion.3), channel_id=1, source_target_pairs={{0,112},{16,0},{32,16},{48,32},{64,48},{80,64},{96,80},{112,96},{1... | collective-permute-start | bytes 454664 | tf_op jit(solution)/shard_map/ppermute | solution.py:71
  120.4 2.7 %shard_map.86 = (bf16[8,2,592,128]{3,2,1,0:T(8,128)(2,1)S(1)}, f32[2,592,128]{2,1,0:T(8,128)S(1)}, bf16[2,592,128]{2,1,0:T(8,128)(2,1)S(1)}, bf16[2,592,128]{2,1,0:T(8,128)(2,1)S(1)}, bf16[2,592,128]{2,1,0:T(8,128)(2,1)S(1)}) custom-call(bf16[2,592,128]{2,1,0:T(8,128)(2,1)S(1)} %pad_maximum_fusion.refs_0_, ...), custom_call_target="tpu_custom_call" | custom-call | flops 1738539008 | bytes 10035200 | tf_op jit(solution)/shard_map/pallas_call | solution.py:84
  123.2 2.1 collective-permute-start.18
  125.3 4.7 %collective-permute-start.19 = (bf16[2,592,128]{2,1,0:T(8,128)(2,1)S(1)}, bf16[2,592,128]{2,1,0:T(8,128)(2,1)S(1)}, u32[]{:S(2)}, u32[]{:S(2)}) collective-permute-start(bf16[2,592,128]{2,1,0:T(8,128)(2,1)S(1)} %get-tuple-element.57), channel_id=1, source_target_pairs={{0,8},{4,12},{8,0},{12,4},{1,9},{5,13},{9,1},{13,5},{2,10},{6,14},... | collective-permute-start | bytes 909320 | tf_op jit(solution)/shard_map/ppermute | solution.py:71
  130.0 4.0 %collective-permute-start.20 = (bf16[2,592,128]{2,1,0:T(8,128)(2,1)S(1)}, bf16[2,592,128]{2,1,0:T(8,128)(2,1)S(1)}, u32[]{:S(2)}, u32[]{:S(2)}) collective-permute-start(bf16[2,592,128]{2,1,0:T(8,128)(2,1)S(1)} %get-tuple-element.58), channel_id=1, source_target_pairs={{0,12},{4,0},{8,4},{12,8},{1,13},{5,1},{9,5},{13,9},{2,14},{6,2},{... | collective-permute-start | bytes 909320 | tf_op jit(solution)/shard_map/ppermute | solution.py:71
  134.0 2.7 %shard_map.87 = (f32[160,320]{1,0:T(8,128)S(1)}, f32[432,864]{1,0:T(8,128)S(1)}, f32[512,896]{1,0:T(8,128)S(1)}, bf16[2,512,896]{2,1,0:T(8,128)(2,1)S(1)}) custom-call(bf16[8,2,592,128]{3,2,1,0:T(8,128)(2,1)S(1)} %get-tuple-element.50.rows, bf16[2,592,128]{2,1,0:T(8,128)(2,1)S(1)} %pad_maximum_fusion.1.c0, ...), custom_call_target="tpu_custom_call" | custom-call | flops 1738539008 | bytes 10702848 | tf_op jit(solution)/shard_map/pallas_call | solution.py:84
  136.7 3.7 %collective-permute-done.19.r2 = bf16[2,592,128]{2,1,0:T(8,128)(2,1)S(1)} collective-permute-done((bf16[2,592,128]{2,1,0:T(8,128)(2,1)S(1)}, bf16[2,592,128]{2,1,0:T(8,128)(2,1)S(1)}, u32[]{:S(2)}, u32[]{:S(2)}) %collective-permute-start.19) | collective-permute-done | bytes 303136 | tf_op jit(solution)/shard_map/ppermute | solution.py:71
  142.3 4.7 %collective-permute-start.26 = (bf16[2,512,896]{2,1,0:T(8,128)(2,1)S(1)}, bf16[2,512,896]{2,1,0:T(8,128)(2,1)S(1)}, u32[]{:S(2)}, u32[]{:S(2)}) collective-permute-start(bf16[2,512,896]{2,1,0:T(8,128)(2,1)S(1)} %get-tuple-element.65), channel_id=1, source_target_pairs={{0,1},{1,0},{2,3},{3,2},{4,5},{5,4},{6,7},{7,6},{8,9},{9,8},{10,11... | collective-permute-start | bytes 5505032 | tf_op jit(solution)/shard_map/ppermute | solution.py:67
  147.0 4.3 %collective-permute-start.21 = (bf16[1024,128]{1,0:T(8,128)(2,1)S(1)}, bf16[1024,128]{1,0:T(8,128)(2,1)S(1)}, u32[]{:S(2)}, u32[]{:S(2)}) collective-permute-start(bf16[1024,128]{1,0:T(8,128)(2,1)S(1)} %get-tuple-element.60), channel_id=1, source_target_pairs={{0,2},{2,0},{1,3},{3,1},{4,6},{6,4},{5,7},{7,5},{8,10},{10,8},{9,1... | collective-permute-start | bytes 786440 | tf_op jit(solution)/shard_map/ppermute | solution.py:67
  151.3 13.5 %collective-permute-done.21.got = bf16[1024,128]{1,0:T(8,128)(2,1)S(1)} collective-permute-done((bf16[1024,128]{1,0:T(8,128)(2,1)S(1)}, bf16[1024,128]{1,0:T(8,128)(2,1)S(1)}, u32[]{:S(2)}, u32[]{:S(2)}) %collective-permute-start.21) | collective-permute-done | bytes 262176 | tf_op jit(solution)/shard_map/ppermute | solution.py:67
  165.0 4.4 %collective-permute-start.27 = (bf16[512,896]{1,0:T(8,128)(2,1)S(1)}, bf16[512,896]{1,0:T(8,128)(2,1)S(1)}, u32[]{:S(2)}, u32[]{:S(2)}) collective-permute-start(bf16[512,896]{1,0:T(8,128)(2,1)S(1)} %fusion), channel_id=1, source_target_pairs={{0,128},{128,0},{1,129},{129,1},{2,130},{130,2},{3,131},{131,3},{4... | collective-permute-start | bytes 2752520 | tf_op jit(solution)/shard_map/ppermute | solution.py:67
  169.4 4.4 %collective-permute-start.25 = (bf16[2,432,128]{2,1,0:T(8,128)(2,1)S(1)}, bf16[2,432,128]{2,1,0:T(8,128)(2,1)S(1)}, u32[]{:S(2)}, u32[]{:S(2)}) collective-permute-start(bf16[2,432,128]{2,1,0:T(8,128)(2,1)S(1)} %get-tuple-element.62.right), channel_id=1, source_target_pairs={{0,12},{4,0},{8,4},{12,8},{1,13},{5,1},{9,5},{13,9},{2,14},{6,2},{... | collective-permute-start | bytes 663560 | tf_op jit(solution)/shard_map/ppermute | solution.py:71
  173.8 3.8 %collective-permute-start.24 = (bf16[2,432,128]{2,1,0:T(8,128)(2,1)S(1)}, bf16[2,432,128]{2,1,0:T(8,128)(2,1)S(1)}, u32[]{:S(2)}, u32[]{:S(2)}) collective-permute-start(bf16[2,432,128]{2,1,0:T(8,128)(2,1)S(1)} %get-tuple-element.62.right), channel_id=1, source_target_pairs={{0,8},{4,12},{8,0},{12,4},{1,9},{5,13},{9,1},{13,5},{2,10},{6,14},... | collective-permute-start | bytes 663560 | tf_op jit(solution)/shard_map/ppermute | solution.py:71
  180.2 2.5 %collective-permute-done.24.r2 = bf16[2,432,128]{2,1,0:T(8,128)(2,1)S(1)} collective-permute-done((bf16[2,432,128]{2,1,0:T(8,128)(2,1)S(1)}, bf16[2,432,128]{2,1,0:T(8,128)(2,1)S(1)}, u32[]{:S(2)}, u32[]{:S(2)}) %collective-permute-start.24) | collective-permute-done | bytes 221216 | tf_op jit(solution)/shard_map/ppermute | solution.py:71
  182.8 5.8 %collective-permute-done.23.r1 = bf16[2,432,128]{2,1,0:T(8,128)(2,1)S(1)} collective-permute-done((bf16[2,432,128]{2,1,0:T(8,128)(2,1)S(1)}, bf16[2,432,128]{2,1,0:T(8,128)(2,1)S(1)}, u32[]{:S(2)}, u32[]{:S(2)}) %collective-permute-start.23) | collective-permute-done | bytes 221216 | tf_op jit(solution)/shard_map/ppermute | solution.py:71
  189.4 27.0 %all_to_all.5.left = bf16[16,160,128]{2,1,0:T(8,128)(2,1)S(1)} all-to-all(bf16[16,160,128]{2,1,0:T(8,128)(2,1)S(1)} %broadcast_in_dim.3), channel_id=1, replica_groups=mesh['zg'=2,'p'=2,'y'=8,'xh'=2,'xl'=2,'w'=2,'core'=2] {'zg','y'}, dimensions={0} | all-to-all | bytes 1310720 | tf_op jit(solution)/shard_map/all_to_all | solution.py:307
  217.7 7.1 %collective-permute-start.28 = (bf16[2,320,432]{2,1,0:T(8,128)(2,1)S(1)}, bf16[2,320,432]{2,1,0:T(8,128)(2,1)S(1)}, u32[]{:S(2)}, u32[]{:S(2)}) collective-permute-start(bf16[2,320,432]{2,1,0:T(8,128)(2,1)S(1)} %get-tuple-element.73), channel_id=1, source_target_pairs={{0,1},{1,0},{2,3},{3,2},{4,5},{5,4},{6,7},{7,6},{8,9},{9,8},{10,11... | collective-permute-start | bytes 1658888 | tf_op jit(solution)/shard_map/ppermute | solution.py:67
  230.0 7.5 %collective-permute-done.29 = bf16[320,432]{1,0:T(8,128)(2,1)S(1)} collective-permute-done((bf16[320,432]{1,0:T(8,128)(2,1)S(1)}, bf16[320,432]{1,0:T(8,128)(2,1)S(1)}, u32[]{:S(2)}, u32[]{:S(2)}) %collective-permute-start.29) | collective-permute-done | bytes 276512 | tf_op jit(solution)/shard_map/ppermute | solution.py:67
  (53 shorter events, 33.6 us)
Async XLA Ops:
  3.7 18.4 %collective-permute-start.3 = (bf16[512,896]{1,0:T(8,128)(2,1)S(1)}, bf16[512,896]{1,0:T(8,128)(2,1)S(1)}, u32[]{:S(2)}, u32[]{:S(2)}) collective-permute-start(bf16[512,896]{1,0:T(8,128)(2,1)S(1)} %shard_map.85.refs_9_), channel_id=1, source_target_pairs={{0,1},{1,0},{2,3},{3,2},{4,5},{5,4},{6,7},{7,6},{8,9},{9,8},{10,11... | collective-permute-start | bytes 2752520 | tf_op jit(solution)/shard_map/ppermute | solution.py:67
  12.5 3.3 %collective-permute-start.2 = (bf16[592,128]{1,0:T(8,128)(2,1)S(1)}, bf16[592,128]{1,0:T(8,128)(2,1)S(1)}, u32[]{:S(2)}, u32[]{:S(2)}) collective-permute-start(bf16[592,128]{1,0:T(8,128)(2,1)S(1)} %pad_maximum_fusion.2), channel_id=1, source_target_pairs={{0,0},{1,1},{2,128},{3,129},{4,4},{5,5},{6,132},{7,133},{8,8},{9,9... | collective-permute-start | bytes 454664 | tf_op jit(solution)/shard_map/ppermute | solution.py:257
  13.1 9.0 %collective-permute-start.1 = (bf16[592,128]{1,0:T(8,128)(2,1)S(1)}, bf16[592,128]{1,0:T(8,128)(2,1)S(1)}, u32[]{:S(2)}, u32[]{:S(2)}) collective-permute-start(bf16[592,128]{1,0:T(8,128)(2,1)S(1)} %pad_maximum_fusion.2), channel_id=1, source_target_pairs={{0,256},{1,257},{2,384},{3,385},{4,320},{5,321},{6,448},{7,449},{8... | collective-permute-start | bytes 454664 | tf_op jit(solution)/shard_map/ppermute | solution.py:256
  15.1 7.0 %collective-permute-start = (bf16[592,128]{1,0:T(8,128)(2,1)S(1)}, bf16[592,128]{1,0:T(8,128)(2,1)S(1)}, u32[]{:S(2)}, u32[]{:S(2)}) collective-permute-start(bf16[592,128]{1,0:T(8,128)(2,1)S(1)} %pad_maximum_fusion.2), channel_id=1, source_target_pairs={{0,0},{1,1},{2,128},{3,129},{4,64},{5,65},{6,192},{7,193},{8,256},... | collective-permute-start | bytes 454664 | tf_op jit(solution)/shard_map/ppermute | solution.py:255
  22.1 55.0 %collective-permute-start.16 = (bf16[512,896]{1,0:T(8,128)(2,1)S(1)}, bf16[512,896]{1,0:T(8,128)(2,1)S(1)}, u32[]{:S(2)}, u32[]{:S(2)}) collective-permute-start(bf16[512,896]{1,0:T(8,128)(2,1)S(1)} %shard_map.85.refs_9_), channel_id=1, source_target_pairs={{0,128},{128,0},{1,129},{129,1},{2,130},{130,2},{3,131},{131,3},{4... | collective-permute-start | bytes 2752520 | tf_op jit(solution)/shard_map/ppermute | solution.py:67
  40.1 14.8 %collective-permute-start.5 = (bf16[2,592,128]{2,1,0:T(8,128)(2,1)S(1)}, bf16[2,592,128]{2,1,0:T(8,128)(2,1)S(1)}, u32[]{:S(2)}, u32[]{:S(2)}) collective-permute-start(bf16[2,592,128]{2,1,0:T(8,128)(2,1)S(1)} %pad_maximum_fusion.refs_0_), channel_id=1, source_target_pairs={{0,112},{16,0},{32,16},{48,32},{64,48},{80,64},{96,80},{112,96},{1... | collective-permute-start | bytes 909320 | tf_op jit(solution)/shard_map/ppermute | solution.py:71
  50.3 12.9 %collective-permute-start.4 = (bf16[2,592,128]{2,1,0:T(8,128)(2,1)S(1)}, bf16[2,592,128]{2,1,0:T(8,128)(2,1)S(1)}, u32[]{:S(2)}, u32[]{:S(2)}) collective-permute-start(bf16[2,592,128]{2,1,0:T(8,128)(2,1)S(1)} %pad_maximum_fusion.refs_0_), channel_id=1, source_target_pairs={{0,16},{16,32},{32,48},{48,64},{64,80},{80,96},{96,112},{112,0},{1... | collective-permute-start | bytes 909320 | tf_op jit(solution)/shard_map/ppermute | solution.py:71
  54.9 20.2 %collective-permute-start.7 = (bf16[2,592,128]{2,1,0:T(8,128)(2,1)S(1)}, bf16[2,592,128]{2,1,0:T(8,128)(2,1)S(1)}, u32[]{:S(2)}, u32[]{:S(2)}) collective-permute-start(bf16[2,592,128]{2,1,0:T(8,128)(2,1)S(1)} %collective-permute-done.5.refs_2_), channel_id=1, source_target_pairs={{0,112},{16,0},{32,16},{48,32},{64,48},{80,64},{96,80},{112,96},{1... | collective-permute-start | bytes 909320 | tf_op jit(solution)/shard_map/ppermute | solution.py:71
  63.3 11.9 %collective-permute-start.6 = (bf16[2,592,128]{2,1,0:T(8,128)(2,1)S(1)}, bf16[2,592,128]{2,1,0:T(8,128)(2,1)S(1)}, u32[]{:S(2)}, u32[]{:S(2)}) collective-permute-start(bf16[2,592,128]{2,1,0:T(8,128)(2,1)S(1)} %collective-permute-done.4.refs_1_), channel_id=1, source_target_pairs={{0,16},{16,32},{32,48},{48,64},{64,80},{80,96},{96,112},{112,0},{1... | collective-permute-start | bytes 909320 | tf_op jit(solution)/shard_map/ppermute | solution.py:71
  65.2 9.9 %collective-permute-start.8 = (bf16[592,128]{1,0:T(8,128)(2,1)S(1)}, bf16[592,128]{1,0:T(8,128)(2,1)S(1)}, u32[]{:S(2)}, u32[]{:S(2)}) collective-permute-start(bf16[592,128]{1,0:T(8,128)(2,1)S(1)} %collective-permute-done.2), channel_id=1, source_target_pairs={{0,2},{2,0},{1,3},{3,1},{4,6},{6,4},{5,7},{7,5},{8,10},{10,8},{9,1... | collective-permute-start | bytes 454664 | tf_op jit(solution)/shard_map/ppermute | solution.py:67
  75.2 22.2 %collective-permute-start.9 = (bf16[2,592,128]{2,1,0:T(8,128)(2,1)S(1)}, bf16[2,592,128]{2,1,0:T(8,128)(2,1)S(1)}, u32[]{:S(2)}, u32[]{:S(2)}) collective-permute-start(bf16[2,592,128]{2,1,0:T(8,128)(2,1)S(1)} %collective-permute-done.6.refs_3_), channel_id=1, source_target_pairs={{0,16},{16,32},{32,48},{48,64},{64,80},{80,96},{96,112},{112,0},{1... | collective-permute-start | bytes 909320 | tf_op jit(solution)/shard_map/ppermute | solution.py:71
  77.1 43.3 %collective-permute-start.17 = (bf16[512,896]{1,0:T(8,128)(2,1)S(1)}, bf16[512,896]{1,0:T(8,128)(2,1)S(1)}, u32[]{:S(2)}, u32[]{:S(2)}) collective-permute-start(bf16[512,896]{1,0:T(8,128)(2,1)S(1)} %collective-permute-done.16.refs_11_), channel_id=1, source_target_pairs={{0,1},{1,0},{2,3},{3,2},{4,5},{5,4},{6,7},{7,6},{8,9},{9,8},{10,11... | collective-permute-start | bytes 2752520 | tf_op jit(solution)/shard_map/ppermute | solution.py:67
  84.3 15.0 %collective-permute-start.10 = (bf16[2,592,128]{2,1,0:T(8,128)(2,1)S(1)}, bf16[2,592,128]{2,1,0:T(8,128)(2,1)S(1)}, u32[]{:S(2)}, u32[]{:S(2)}) collective-permute-start(bf16[2,592,128]{2,1,0:T(8,128)(2,1)S(1)} %collective-permute-done.7.refs_4_), channel_id=1, source_target_pairs={{0,112},{16,0},{32,16},{48,32},{64,48},{80,64},{96,80},{112,96},{1... | collective-permute-start | bytes 909320 | tf_op jit(solution)/shard_map/ppermute | solution.py:71
  89.8 11.2 %collective-permute-start.13 = (bf16[2,592,128]{2,1,0:T(8,128)(2,1)S(1)}, bf16[2,592,128]{2,1,0:T(8,128)(2,1)S(1)}, u32[]{:S(2)}, u32[]{:S(2)}) collective-permute-start(bf16[2,592,128]{2,1,0:T(8,128)(2,1)S(1)} %pad_maximum_fusion.1.c0), channel_id=1, source_target_pairs={{0,12},{4,0},{8,4},{12,8},{1,13},{5,1},{9,5},{13,9},{2,14},{6,2},{... | collective-permute-start | bytes 909320 | tf_op jit(solution)/shard_map/ppermute | solution.py:71
  92.2 12.1 %collective-permute-start.12 = (bf16[2,592,128]{2,1,0:T(8,128)(2,1)S(1)}, bf16[2,592,128]{2,1,0:T(8,128)(2,1)S(1)}, u32[]{:S(2)}, u32[]{:S(2)}) collective-permute-start(bf16[2,592,128]{2,1,0:T(8,128)(2,1)S(1)} %pad_maximum_fusion.1.c0), channel_id=1, source_target_pairs={{0,8},{4,12},{8,0},{12,4},{1,9},{5,13},{9,1},{13,5},{2,10},{6,14},... | collective-permute-start | bytes 909320 | tf_op jit(solution)/shard_map/ppermute | solution.py:71
  97.4 14.1 %collective-permute-start.11 = (bf16[2,592,128]{2,1,0:T(8,128)(2,1)S(1)}, bf16[2,592,128]{2,1,0:T(8,128)(2,1)S(1)}, u32[]{:S(2)}, u32[]{:S(2)}) collective-permute-start(bf16[2,592,128]{2,1,0:T(8,128)(2,1)S(1)} %pad_maximum_fusion.1.c0), channel_id=1, source_target_pairs={{0,4},{4,8},{8,12},{12,0},{1,5},{5,9},{9,13},{13,1},{2,6},{6,10},{... | collective-permute-start | bytes 909320 | tf_op jit(solution)/shard_map/ppermute | solution.py:71
  99.4 34.6 %copy-start.2 = (f32[864,432]{0,1:T(8,128)S(1)}, f32[864,432]{0,1:T(8,128)}, u32[]{:S(2)}) copy-start(f32[864,432]{0,1:T(8,128)} %param.9) | copy-start | bytes 4478980
  99.4 34.6 %copy-start.3 = (f32[320,160]{0,1:T(8,128)S(1)}, f32[320,160]{0,1:T(8,128)}, u32[]{:S(2)}) copy-start(f32[320,160]{0,1:T(8,128)} %param.8) | copy-start | bytes 614404
  111.5 8.1 %collective-permute-start.14 = (bf16[592,128]{1,0:T(8,128)(2,1)S(1)}, bf16[592,128]{1,0:T(8,128)(2,1)S(1)}, u32[]{:S(2)}, u32[]{:S(2)}) collective-permute-start(bf16[592,128]{1,0:T(8,128)(2,1)S(1)} %slice_bitcast_fusion.4), channel_id=1, source_target_pairs={{0,16},{16,32},{32,48},{48,64},{64,80},{80,96},{96,112},{112,0},{1... | collective-permute-start | bytes 454664 | tf_op jit(solution)/shard_map/ppermute | solution.py:71
  113.4 7.0 %collective-permute-start.15 = (bf16[592,128]{1,0:T(8,128)(2,1)S(1)}, bf16[592,128]{1,0:T(8,128)(2,1)S(1)}, u32[]{:S(2)}, u32[]{:S(2)}) collective-permute-start(bf16[592,128]{1,0:T(8,128)(2,1)S(1)} %slice_bitcast_fusion.3), channel_id=1, source_target_pairs={{0,112},{16,0},{32,16},{48,32},{64,48},{80,64},{96,80},{112,96},{1... | collective-permute-start | bytes 454664 | tf_op jit(solution)/shard_map/ppermute | solution.py:71
  123.2 13.5 %collective-permute-start.18 = (bf16[2,592,128]{2,1,0:T(8,128)(2,1)S(1)}, bf16[2,592,128]{2,1,0:T(8,128)(2,1)S(1)}, u32[]{:S(2)}, u32[]{:S(2)}) collective-permute-start(bf16[2,592,128]{2,1,0:T(8,128)(2,1)S(1)} %get-tuple-element.56), channel_id=1, source_target_pairs={{0,4},{4,8},{8,12},{12,0},{1,5},{5,9},{9,13},{13,1},{2,6},{6,10},{... | collective-permute-start | bytes 909320 | tf_op jit(solution)/shard_map/ppermute | solution.py:71
  125.3 15.0 %collective-permute-start.19 = (bf16[2,592,128]{2,1,0:T(8,128)(2,1)S(1)}, bf16[2,592,128]{2,1,0:T(8,128)(2,1)S(1)}, u32[]{:S(2)}, u32[]{:S(2)}) collective-permute-start(bf16[2,592,128]{2,1,0:T(8,128)(2,1)S(1)} %get-tuple-element.57), channel_id=1, source_target_pairs={{0,8},{4,12},{8,0},{12,4},{1,9},{5,13},{9,1},{13,5},{2,10},{6,14},... | collective-permute-start | bytes 909320 | tf_op jit(solution)/shard_map/ppermute | solution.py:71
  130.0 12.1 %collective-permute-start.20 = (bf16[2,592,128]{2,1,0:T(8,128)(2,1)S(1)}, bf16[2,592,128]{2,1,0:T(8,128)(2,1)S(1)}, u32[]{:S(2)}, u32[]{:S(2)}) collective-permute-start(bf16[2,592,128]{2,1,0:T(8,128)(2,1)S(1)} %get-tuple-element.58), channel_id=1, source_target_pairs={{0,12},{4,0},{8,4},{12,8},{1,13},{5,1},{9,5},{13,9},{2,14},{6,2},{... | collective-permute-start | bytes 909320 | tf_op jit(solution)/shard_map/ppermute | solution.py:71
  142.3 22.5 %collective-permute-start.26 = (bf16[2,512,896]{2,1,0:T(8,128)(2,1)S(1)}, bf16[2,512,896]{2,1,0:T(8,128)(2,1)S(1)}, u32[]{:S(2)}, u32[]{:S(2)}) collective-permute-start(bf16[2,512,896]{2,1,0:T(8,128)(2,1)S(1)} %get-tuple-element.65), channel_id=1, source_target_pairs={{0,1},{1,0},{2,3},{3,2},{4,5},{5,4},{6,7},{7,6},{8,9},{9,8},{10,11... | collective-permute-start | bytes 5505032 | tf_op jit(solution)/shard_map/ppermute | solution.py:67
  147.0 17.7 %collective-permute-start.21 = (bf16[1024,128]{1,0:T(8,128)(2,1)S(1)}, bf16[1024,128]{1,0:T(8,128)(2,1)S(1)}, u32[]{:S(2)}, u32[]{:S(2)}) collective-permute-start(bf16[1024,128]{1,0:T(8,128)(2,1)S(1)} %get-tuple-element.60), channel_id=1, source_target_pairs={{0,2},{2,0},{1,3},{3,1},{4,6},{6,4},{5,7},{7,5},{8,10},{10,8},{9,1... | collective-permute-start | bytes 786440 | tf_op jit(solution)/shard_map/ppermute | solution.py:67
  165.0 24.3 %collective-permute-start.27 = (bf16[512,896]{1,0:T(8,128)(2,1)S(1)}, bf16[512,896]{1,0:T(8,128)(2,1)S(1)}, u32[]{:S(2)}, u32[]{:S(2)}) collective-permute-start(bf16[512,896]{1,0:T(8,128)(2,1)S(1)} %fusion), channel_id=1, source_target_pairs={{0,128},{128,0},{1,129},{129,1},{2,130},{130,2},{3,131},{131,3},{4... | collective-permute-start | bytes 2752520 | tf_op jit(solution)/shard_map/ppermute | solution.py:67
  169.4 10.8 %collective-permute-start.25 = (bf16[2,432,128]{2,1,0:T(8,128)(2,1)S(1)}, bf16[2,432,128]{2,1,0:T(8,128)(2,1)S(1)}, u32[]{:S(2)}, u32[]{:S(2)}) collective-permute-start(bf16[2,432,128]{2,1,0:T(8,128)(2,1)S(1)} %get-tuple-element.62.right), channel_id=1, source_target_pairs={{0,12},{4,0},{8,4},{12,8},{1,13},{5,1},{9,5},{13,9},{2,14},{6,2},{... | collective-permute-start | bytes 663560 | tf_op jit(solution)/shard_map/ppermute | solution.py:71
  173.8 9.0 %collective-permute-start.24 = (bf16[2,432,128]{2,1,0:T(8,128)(2,1)S(1)}, bf16[2,432,128]{2,1,0:T(8,128)(2,1)S(1)}, u32[]{:S(2)}, u32[]{:S(2)}) collective-permute-start(bf16[2,432,128]{2,1,0:T(8,128)(2,1)S(1)} %get-tuple-element.62.right), channel_id=1, source_target_pairs={{0,8},{4,12},{8,0},{12,4},{1,9},{5,13},{9,1},{13,5},{2,10},{6,14},... | collective-permute-start | bytes 663560 | tf_op jit(solution)/shard_map/ppermute | solution.py:71
  177.6 11.0 %collective-permute-start.23 = (bf16[2,432,128]{2,1,0:T(8,128)(2,1)S(1)}, bf16[2,432,128]{2,1,0:T(8,128)(2,1)S(1)}, u32[]{:S(2)}, u32[]{:S(2)}) collective-permute-start(bf16[2,432,128]{2,1,0:T(8,128)(2,1)S(1)} %get-tuple-element.62.right), channel_id=1, source_target_pairs={{0,4},{4,8},{8,12},{12,0},{1,5},{5,9},{9,13},{13,1},{2,6},{6,10},{... | collective-permute-start | bytes 663560 | tf_op jit(solution)/shard_map/ppermute | solution.py:71
  179.5 0.7 collective-permute-start.22
  217.7 8.8 %collective-permute-start.28 = (bf16[2,320,432]{2,1,0:T(8,128)(2,1)S(1)}, bf16[2,320,432]{2,1,0:T(8,128)(2,1)S(1)}, u32[]{:S(2)}, u32[]{:S(2)}) collective-permute-start(bf16[2,320,432]{2,1,0:T(8,128)(2,1)S(1)} %get-tuple-element.73), channel_id=1, source_target_pairs={{0,1},{1,0},{2,3},{3,2},{4,5},{5,4},{6,7},{7,6},{8,9},{9,8},{10,11... | collective-permute-start | bytes 1658888 | tf_op jit(solution)/shard_map/ppermute | solution.py:67
  226.7 10.8 %collective-permute-start.29 = (bf16[320,432]{1,0:T(8,128)(2,1)S(1)}, bf16[320,432]{1,0:T(8,128)(2,1)S(1)}, u32[]{:S(2)}, u32[]{:S(2)}) collective-permute-start(bf16[320,432]{1,0:T(8,128)(2,1)S(1)} %fusion.1), channel_id=1, source_target_pairs={{0,128},{128,0},{1,129},{129,1},{2,130},{130,2},{3,131},{131,3},{4... | collective-permute-start | bytes 829448 | tf_op jit(solution)/shard_map/ppermute | solution.py:67
  (2 other events, 2.0 us)

commit v4 on v3

--- a/solution.py
+++ b/solution.py
@@ -53,11 +53,11 @@
     ]
 
 
-def column_perm():
+def column_perm(flip):
     return [
         (
             device(zg, p, y, xh, xl, w, core),
-            device(zg, w, y, xh, xl, p, core),
+            device(zg, w, y, xh, xl, p ^ flip, core),
         )
         for zg, p, y, xh, xl, w, core in coordinates()
     ]
@@ -250,28 +250,24 @@
 
     x = jnp.concatenate([activations.T, output_grads.T], 0)
     inverse = call(pack_kernel, shape(pack, bf16), 0, after(input_inverse.T, x), gradient_inverse.T)
-    first, second, col, inverse_c = lax.optimization_barrier(
+    near, far = (lax.ppermute(x, AXES, column_perm(j)) for j in range(2))
+    first, second, col, inverse_c, inverse_z = lax.optimization_barrier(
         (
             lax.ppermute(x, AXES, panel_perm(0)),
             lax.ppermute(x, AXES, panel_perm(1)),
-            lax.ppermute(x, AXES, column_perm()),
+            jnp.stack([near, far]),
             swap(inverse, "core"),
-        )
-    )
+            swap(inverse, "p"),
+        )
+    )
+    cols = [shift(col, X, 4, i + 1) for i in range(3)]
     u = jnp.stack([first, second])
-    inverse_z = swap(after(inverse, u), "p")
     up, down = [u], [u]
-    for stage in range(3):
-        if stage == 2:
-            col = jnp.stack([col, swap(col, "w")])
-            up[2], down[2], col = lax.optimization_barrier((up[2], down[2], col))
+    for _ in range(3):
         up.append(shift(up[-1], "y", RING, 1))
         down.append(shift(down[-1], "y", RING, -1))
-    cols = [shift(col, X, 4, i + 1) for i in range(3)]
-    halves = lax.optimization_barrier((up[3][0], down[3][1], *cols))
-    cols = list(halves[2:])
     ring = [u, up[1], down[1], up[2], down[2], up[3], down[3]]
-    ring += [shift(halves[0], "y", RING, 1), shift(halves[1], "y", RING, -1)]
+    ring += [shift(up[3][0], "y", RING, 1), shift(down[3][1], "y", RING, -1)]
     inverse_zc = swap(inverse_z, "core")
 
     rows, own, *ahead = call(

time: 239 us -> 227 us (0.950); the launches traced: 238 us -> 224 us
  waiting for transfers between devices: 69.5 us -> 54.7 us
  starting transfers between devices: 128 us -> 133 us
  blocking collectives: 27 us -> 22.8 us
    ppermute x9 -> x8, waiting for transfers between devices: 31.4 us -> 19 us  [swap(): return lax.ppermute(x, axis, [(0, 1), (1, 0)])]
    ppermute x1, starting transfers between devices: 1.92 us -> 12.1 us  [local(): lax.ppermute(x, AXES, panel_perm(1))]
    ppermute x1 -> x2, starting transfers between devices: 0.67 us -> 9.46 us  [local(): near, far = (lax.ppermute(x, AXES, column_perm(j)) for j in range(2))]
    ppermute x9 -> x8, starting transfers between devices: 58.3 us -> 50.1 us  [swap(): return lax.ppermute(x, axis, [(0, 1), (1, 0)])]
    ppermute x17, starting transfers between devices: 65.8 us -> 59.5 us  [shift(): return lax.ppermute(x, axis, [(i, (i + by) % size) for i in range(size)])]
    all_to_all x1, blocking collectives: 27 us -> 22.8 us  [local(): lefts = lax.all_to_all(pieces, ('zg', 'y'), 0, 0, tiled=True)]
    ppermute x1 -> x2, waiting for transfers between devices: 0.01 us -> 4.18 us  [local(): near, far = (lax.ppermute(x, AXES, column_perm(j)) for j in range(2))]
    ppermute x17, waiting for transfers between devices: 31.7 us -> 28.3 us  [shift(): return lax.ppermute(x, axis, [(i, (i + by) % size) for i in range(size)])]
  transfers between devices with their start and end apart: 30 -> 30, of which waited for: 17 -> 14; matrix products, arithmetic and copies ran while one was open for 0% -> 0% of each run, Pallas kernels for 2% -> 3%
where the time goes in v4:
time: 227 us; the launch traced here: 224 us
  starting transfers between devices  133 us (59%)
  waiting for transfers between devices  54.7 us (24%)
  blocking collectives  22.8 us (10%)
  Pallas kernels  8.47 us (4%)
    ppermute x17, starting transfers between devices, shift(): return lax.ppermute(x, axis, [(i, (i + by) % size) for i in range(size)])  59.5 us
    ppermute x8, starting transfers between devices, swap(): return lax.ppermute(x, axis, [(0, 1), (1, 0)])  50.1 us
    ppermute x17, waiting for transfers between devices, shift(): return lax.ppermute(x, axis, [(i, (i + by) % size) for i in range(size)])  28.3 us
    all_to_all x1, blocking collectives, local(): lefts = lax.all_to_all(pieces, ('zg', 'y'), 0, 0, tiled=True)  22.8 us
    ppermute x8, waiting for transfers between devices, swap(): return lax.ppermute(x, axis, [(0, 1), (1, 0)])  19 us
    ppermute x1, starting transfers between devices, local(): lax.ppermute(x, AXES, panel_perm(1))  12.1 us
    ppermute x2, starting transfers between devices, local(): near, far = (lax.ppermute(x, AXES, column_perm(j)) for j in range(2))  9.46 us
    pallas_call x7, Pallas kernels, call(): pl.pallas_call(kernel, out_shape=out, in_specs=[VMEM] * len(args), out_sp...  8.47 us
  transfers between devices with their start and end apart: 30, of which 14 were waited for; matrix products, arithmetic and copies ran while one was open for 0% of the time, Pallas kernels for 3%

profile of v4, /device:TPU:1, one launch (start us, length us, event | category | flops | bytes accessed | tf_op | source)
XLA Modules:
  0.0 223.8 jit_solution(17773825779303818879)
XLA Ops:
  3.7 8.8 %collective-permute-start.4 = (bf16[512,896]{1,0:T(8,128)(2,1)S(1)}, bf16[512,896]{1,0:T(8,128)(2,1)S(1)}, u32[]{:S(2)}, u32[]{:S(2)}) collective-permute-start(bf16[512,896]{1,0:T(8,128)(2,1)S(1)} %shard_map.85.refs_9_), channel_id=1, source_target_pairs={{0,1},{1,0},{2,3},{3,2},{4,5},{5,4},{6,7},{7,6},{8,9},{9,8},{10,11... | collective-permute-start | bytes 2752520 | tf_op jit(solution)/shard_map/ppermute | solution.py:67
  15.1 8.8 %collective-permute-start.3 = (bf16[592,128]{1,0:T(8,128)(2,1)S(1)}, bf16[592,128]{1,0:T(8,128)(2,1)S(1)}, u32[]{:S(2)}, u32[]{:S(2)}) collective-permute-start(bf16[592,128]{1,0:T(8,128)(2,1)S(1)} %pad_maximum_fusion.2), channel_id=1, source_target_pairs={{0,2},{1,3},{2,130},{3,131},{4,6},{5,7},{6,134},{7,135},{8,10},{9,... | collective-permute-start | bytes 454664 | tf_op jit(solution)/shard_map/ppermute | solution.py:253
  24.6 12.1 %collective-permute-start.1 = (bf16[592,128]{1,0:T(8,128)(2,1)S(1)}, bf16[592,128]{1,0:T(8,128)(2,1)S(1)}, u32[]{:S(2)}, u32[]{:S(2)}) collective-permute-start(bf16[592,128]{1,0:T(8,128)(2,1)S(1)} %pad_maximum_fusion.2), channel_id=1, source_target_pairs={{0,256},{1,257},{2,384},{3,385},{4,320},{5,321},{6,448},{7,449},{8... | collective-permute-start | bytes 454664 | tf_op jit(solution)/shard_map/ppermute | solution.py:257
  36.7 4.2 %collective-permute-done.3 = bf16[592,128]{1,0:T(8,128)(2,1)S(1)} collective-permute-done((bf16[592,128]{1,0:T(8,128)(2,1)S(1)}, bf16[592,128]{1,0:T(8,128)(2,1)S(1)}, u32[]{:S(2)}, u32[]{:S(2)}) %collective-permute-start.3) | collective-permute-done | bytes 151584 | tf_op jit(solution)/shard_map/ppermute | solution.py:253
  40.9 3.2 %collective-permute-done.1 = bf16[592,128]{1,0:T(8,128)(2,1)S(1)} collective-permute-done((bf16[592,128]{1,0:T(8,128)(2,1)S(1)}, bf16[592,128]{1,0:T(8,128)(2,1)S(1)}, u32[]{:S(2)}, u32[]{:S(2)}) %collective-permute-start.1) | collective-permute-done | bytes 151584 | tf_op jit(solution)/shard_map/ppermute | solution.py:257
  46.1 4.6 %collective-permute-start.7 = (bf16[2,592,128]{2,1,0:T(8,128)(2,1)S(1)}, bf16[2,592,128]{2,1,0:T(8,128)(2,1)S(1)}, u32[]{:S(2)}, u32[]{:S(2)}) collective-permute-start(bf16[2,592,128]{2,1,0:T(8,128)(2,1)S(1)} %pad_maximum_fusion.1.refs_0_), channel_id=1, source_target_pairs={{0,112},{16,0},{32,16},{48,32},{64,48},{80,64},{96,80},{112,96},{1... | collective-permute-start | bytes 909320 | tf_op jit(solution)/shard_map/ppermute | solution.py:71
  50.7 5.1 %collective-permute-done.6.refs_1_ = bf16[2,592,128]{2,1,0:T(8,128)(2,1)S(1)} collective-permute-done((bf16[2,592,128]{2,1,0:T(8,128)(2,1)S(1)}, bf16[2,592,128]{2,1,0:T(8,128)(2,1)S(1)}, u32[]{:S(2)}, u32[]{:S(2)}) %collective-permute-start.6) | collective-permute-done | bytes 303136 | tf_op jit(solution)/shard_map/ppermute | solution.py:71
  55.7 2.9 %collective-permute-start.8 = (bf16[2,592,128]{2,1,0:T(8,128)(2,1)S(1)}, bf16[2,592,128]{2,1,0:T(8,128)(2,1)S(1)}, u32[]{:S(2)}, u32[]{:S(2)}) collective-permute-start(bf16[2,592,128]{2,1,0:T(8,128)(2,1)S(1)} %collective-permute-done.6.refs_1_), channel_id=1, source_target_pairs={{0,16},{16,32},{32,48},{48,64},{64,80},{80,96},{96,112},{112,0},{1... | collective-permute-start | bytes 909320 | tf_op jit(solution)/shard_map/ppermute | solution.py:71
  58.7 4.6 %collective-permute-start.9 = (bf16[2,592,128]{2,1,0:T(8,128)(2,1)S(1)}, bf16[2,592,128]{2,1,0:T(8,128)(2,1)S(1)}, u32[]{:S(2)}, u32[]{:S(2)}) collective-permute-start(bf16[2,592,128]{2,1,0:T(8,128)(2,1)S(1)} %collective-permute-done.7.refs_2_), channel_id=1, source_target_pairs={{0,112},{16,0},{32,16},{48,32},{64,48},{80,64},{96,80},{112,96},{1... | collective-permute-start | bytes 909320 | tf_op jit(solution)/shard_map/ppermute | solution.py:71
  63.3 3.5 %collective-permute-done.8.refs_3_ = bf16[2,592,128]{2,1,0:T(8,128)(2,1)S(1)} collective-permute-done((bf16[2,592,128]{2,1,0:T(8,128)(2,1)S(1)}, bf16[2,592,128]{2,1,0:T(8,128)(2,1)S(1)}, u32[]{:S(2)}, u32[]{:S(2)}) %collective-permute-start.8) | collective-permute-done | bytes 303136 | tf_op jit(solution)/shard_map/ppermute | solution.py:71
  68.8 4.5 %collective-permute-start.14 = (bf16[512,896]{1,0:T(8,128)(2,1)S(1)}, bf16[512,896]{1,0:T(8,128)(2,1)S(1)}, u32[]{:S(2)}, u32[]{:S(2)}) collective-permute-start(bf16[512,896]{1,0:T(8,128)(2,1)S(1)} %collective-permute-done.5.refs_11_), channel_id=1, source_target_pairs={{0,1},{1,0},{2,3},{3,2},{4,5},{5,4},{6,7},{7,6},{8,9},{9,8},{10,11... | collective-permute-start | bytes 2752520 | tf_op jit(solution)/shard_map/ppermute | solution.py:67
  73.3 4.9 %collective-permute-start.11 = (bf16[2,592,128]{2,1,0:T(8,128)(2,1)S(1)}, bf16[2,592,128]{2,1,0:T(8,128)(2,1)S(1)}, u32[]{:S(2)}, u32[]{:S(2)}) collective-permute-start(bf16[2,592,128]{2,1,0:T(8,128)(2,1)S(1)} %collective-permute-done.9.refs_4_), channel_id=1, source_target_pairs={{0,112},{16,0},{32,16},{48,32},{64,48},{80,64},{96,80},{112,96},{1... | collective-permute-start | bytes 909320 | tf_op jit(solution)/shard_map/ppermute | solution.py:71
  80.1 4.6 %collective-permute-done.11.refs_6_ = bf16[2,592,128]{2,1,0:T(8,128)(2,1)S(1)} collective-permute-done((bf16[2,592,128]{2,1,0:T(8,128)(2,1)S(1)}, bf16[2,592,128]{2,1,0:T(8,128)(2,1)S(1)}, u32[]{:S(2)}, u32[]{:S(2)}) %collective-permute-start.11) | collective-permute-done | bytes 303136 | tf_op jit(solution)/shard_map/ppermute | solution.py:71
  84.8 5.5 %collective-permute-start.13 = (bf16[592,128]{1,0:T(8,128)(2,1)S(1)}, bf16[592,128]{1,0:T(8,128)(2,1)S(1)}, u32[]{:S(2)}, u32[]{:S(2)}) collective-permute-start(bf16[592,128]{1,0:T(8,128)(2,1)S(1)} %slice_bitcast_fusion.3), channel_id=1, source_target_pairs={{0,112},{16,0},{32,16},{48,32},{64,48},{80,64},{96,80},{112,96},{1... | collective-permute-start | bytes 454664 | tf_op jit(solution)/shard_map/ppermute | solution.py:71
  90.2 4.1 %collective-permute-start.15 = (bf16[2,592,128]{2,1,0:T(8,128)(2,1)S(1)}, bf16[2,592,128]{2,1,0:T(8,128)(2,1)S(1)}, u32[]{:S(2)}, u32[]{:S(2)}) collective-permute-start(bf16[2,592,128]{2,1,0:T(8,128)(2,1)S(1)} %pad_maximum_fusion.c0), channel_id=1, source_target_pairs={{0,4},{4,8},{8,12},{12,0},{1,5},{5,9},{9,13},{13,1},{2,6},{6,10},{... | collective-permute-start | bytes 909320 | tf_op jit(solution)/shard_map/ppermute | solution.py:71
  94.3 6.3 %collective-permute-start.16 = (bf16[2,592,128]{2,1,0:T(8,128)(2,1)S(1)}, bf16[2,592,128]{2,1,0:T(8,128)(2,1)S(1)}, u32[]{:S(2)}, u32[]{:S(2)}) collective-permute-start(bf16[2,592,128]{2,1,0:T(8,128)(2,1)S(1)} %pad_maximum_fusion.c0), channel_id=1, source_target_pairs={{0,8},{4,12},{8,0},{12,4},{1,9},{5,13},{9,1},{13,5},{2,10},{6,14},... | collective-permute-start | bytes 909320 | tf_op jit(solution)/shard_map/ppermute | solution.py:71
  102.6 2.8 %shard_map.86 = (bf16[8,2,592,128]{3,2,1,0:T(8,128)(2,1)S(1)}, f32[2,592,128]{2,1,0:T(8,128)S(1)}, bf16[2,592,128]{2,1,0:T(8,128)(2,1)S(1)}, bf16[2,592,128]{2,1,0:T(8,128)(2,1)S(1)}, bf16[2,592,128]{2,1,0:T(8,128)(2,1)S(1)}) custom-call(bf16[2,592,128]{2,1,0:T(8,128)(2,1)S(1)} %pad_maximum_fusion.1.refs_0_, ...), custom_call_target="tpu_custom_call" | custom-call | flops 1738539008 | bytes 10035200 | tf_op jit(solution)/shard_map/pallas_call | solution.py:84
  105.4 3.4 %collective-permute-start.18 = (bf16[2,592,128]{2,1,0:T(8,128)(2,1)S(1)}, bf16[2,592,128]{2,1,0:T(8,128)(2,1)S(1)}, u32[]{:S(2)}, u32[]{:S(2)}) collective-permute-start(bf16[2,592,128]{2,1,0:T(8,128)(2,1)S(1)} %get-tuple-element.40), channel_id=1, source_target_pairs={{0,4},{4,8},{8,12},{12,0},{1,5},{5,9},{9,13},{13,1},{2,6},{6,10},{... | collective-permute-start | bytes 909320 | tf_op jit(solution)/shard_map/ppermute | solution.py:71
  110.7 4.3 %collective-permute-start.20 = (bf16[2,592,128]{2,1,0:T(8,128)(2,1)S(1)}, bf16[2,592,128]{2,1,0:T(8,128)(2,1)S(1)}, u32[]{:S(2)}, u32[]{:S(2)}) collective-permute-start(bf16[2,592,128]{2,1,0:T(8,128)(2,1)S(1)} %get-tuple-element.42), channel_id=1, source_target_pairs={{0,12},{4,0},{8,4},{12,8},{1,13},{5,1},{9,5},{13,9},{2,14},{6,2},{... | collective-permute-start | bytes 909320 | tf_op jit(solution)/shard_map/ppermute | solution.py:71
  115.1 2.7 %shard_map.87 = (f32[160,320]{1,0:T(8,128)S(1)}, f32[432,864]{1,0:T(8,128)S(1)}, f32[512,896]{1,0:T(8,128)S(1)}, bf16[2,512,896]{2,1,0:T(8,128)(2,1)S(1)}) custom-call(bf16[8,2,592,128]{3,2,1,0:T(8,128)(2,1)S(1)} %get-tuple-element.36.rows, bf16[2,592,128]{2,1,0:T(8,128)(2,1)S(1)} %pad_maximum_fusion.c0, ...), custom_call_target="tpu_custom_call" | custom-call | flops 1738539008 | bytes 10702848 | tf_op jit(solution)/shard_map/pallas_call | solution.py:84
  119.0 5.4 %collective-permute-done.19.r2 = bf16[2,592,128]{2,1,0:T(8,128)(2,1)S(1)} collective-permute-done((bf16[2,592,128]{2,1,0:T(8,128)(2,1)S(1)}, bf16[2,592,128]{2,1,0:T(8,128)(2,1)S(1)}, u32[]{:S(2)}, u32[]{:S(2)}) %collective-permute-start.19) | collective-permute-done | bytes 303136 | tf_op jit(solution)/shard_map/ppermute | solution.py:71
  126.4 3.5 %collective-permute-start.26 = (bf16[2,512,896]{2,1,0:T(8,128)(2,1)S(1)}, bf16[2,512,896]{2,1,0:T(8,128)(2,1)S(1)}, u32[]{:S(2)}, u32[]{:S(2)}) collective-permute-start(bf16[2,512,896]{2,1,0:T(8,128)(2,1)S(1)} %get-tuple-element.49), channel_id=1, source_target_pairs={{0,1},{1,0},{2,3},{3,2},{4,5},{5,4},{6,7},{7,6},{8,9},{9,8},{10,11... | collective-permute-start | bytes 5505032 | tf_op jit(solution)/shard_map/ppermute | solution.py:67
  129.9 9.6 %collective-permute-start.21 = (bf16[1024,128]{1,0:T(8,128)(2,1)S(1)}, bf16[1024,128]{1,0:T(8,128)(2,1)S(1)}, u32[]{:S(2)}, u32[]{:S(2)}) collective-permute-start(bf16[1024,128]{1,0:T(8,128)(2,1)S(1)} %get-tuple-element.44), channel_id=1, source_target_pairs={{0,2},{2,0},{1,3},{3,1},{4,6},{6,4},{5,7},{7,5},{8,10},{10,8},{9,1... | collective-permute-start | bytes 786440 | tf_op jit(solution)/shard_map/ppermute | solution.py:67
  139.5 7.0 %collective-permute-done.21.got = bf16[1024,128]{1,0:T(8,128)(2,1)S(1)} collective-permute-done((bf16[1024,128]{1,0:T(8,128)(2,1)S(1)}, bf16[1024,128]{1,0:T(8,128)(2,1)S(1)}, u32[]{:S(2)}, u32[]{:S(2)}) %collective-permute-start.21) | collective-permute-done | bytes 262176 | tf_op jit(solution)/shard_map/ppermute | solution.py:67
  146.7 12.8 %collective-permute-start.27 = (bf16[512,896]{1,0:T(8,128)(2,1)S(1)}, bf16[512,896]{1,0:T(8,128)(2,1)S(1)}, u32[]{:S(2)}, u32[]{:S(2)}) collective-permute-start(bf16[512,896]{1,0:T(8,128)(2,1)S(1)} %fusion), channel_id=1, source_target_pairs={{0,128},{128,0},{1,129},{129,1},{2,130},{130,2},{3,131},{131,3},{4... | collective-permute-start | bytes 2752520 | tf_op jit(solution)/shard_map/ppermute | solution.py:67
  159.5 2.8 %collective-permute-start.23 = (bf16[2,432,128]{2,1,0:T(8,128)(2,1)S(1)}, bf16[2,432,128]{2,1,0:T(8,128)(2,1)S(1)}, u32[]{:S(2)}, u32[]{:S(2)}) collective-permute-start(bf16[2,432,128]{2,1,0:T(8,128)(2,1)S(1)} %get-tuple-element.46.right), channel_id=1, source_target_pairs={{0,4},{4,8},{8,12},{12,0},{1,5},{5,9},{9,13},{13,1},{2,6},{6,10},{... | collective-permute-start | bytes 663560 | tf_op jit(solution)/shard_map/ppermute | solution.py:71
  162.3 4.5 %collective-permute-start.24 = (bf16[2,432,128]{2,1,0:T(8,128)(2,1)S(1)}, bf16[2,432,128]{2,1,0:T(8,128)(2,1)S(1)}, u32[]{:S(2)}, u32[]{:S(2)}) collective-permute-start(bf16[2,432,128]{2,1,0:T(8,128)(2,1)S(1)} %get-tuple-element.46.right), channel_id=1, source_target_pairs={{0,8},{4,12},{8,0},{12,4},{1,9},{5,13},{9,1},{13,5},{2,10},{6,14},... | collective-permute-start | bytes 663560 | tf_op jit(solution)/shard_map/ppermute | solution.py:71
  169.6 4.9 %collective-permute-done.24.r2 = bf16[2,432,128]{2,1,0:T(8,128)(2,1)S(1)} collective-permute-done((bf16[2,432,128]{2,1,0:T(8,128)(2,1)S(1)}, bf16[2,432,128]{2,1,0:T(8,128)(2,1)S(1)}, u32[]{:S(2)}, u32[]{:S(2)}) %collective-permute-start.24) | collective-permute-done | bytes 221216 | tf_op jit(solution)/shard_map/ppermute | solution.py:71
  176.3 3.6 %collective-permute-done.27.last = bf16[512,896]{1,0:T(8,128)(2,1)S(1)} collective-permute-done((bf16[512,896]{1,0:T(8,128)(2,1)S(1)}, bf16[512,896]{1,0:T(8,128)(2,1)S(1)}, u32[]{:S(2)}, u32[]{:S(2)}) %collective-permute-start.27) | collective-permute-done | bytes 917536 | tf_op jit(solution)/shard_map/ppermute | solution.py:67
  179.9 22.8 %all_to_all.5.left = bf16[16,160,128]{2,1,0:T(8,128)(2,1)S(1)} all-to-all(bf16[16,160,128]{2,1,0:T(8,128)(2,1)S(1)} %broadcast_in_dim.3), channel_id=1, replica_groups=mesh['zg'=2,'p'=2,'y'=8,'xh'=2,'xl'=2,'w'=2,'core'=2] {'zg','y'}, dimensions={0} | all-to-all | bytes 1310720 | tf_op jit(solution)/shard_map/all_to_all | solution.py:303
  203.9 6.4 %collective-permute-start.28 = (bf16[2,320,432]{2,1,0:T(8,128)(2,1)S(1)}, bf16[2,320,432]{2,1,0:T(8,128)(2,1)S(1)}, u32[]{:S(2)}, u32[]{:S(2)}) collective-permute-start(bf16[2,320,432]{2,1,0:T(8,128)(2,1)S(1)} %get-tuple-element.57), channel_id=1, source_target_pairs={{0,1},{1,0},{2,3},{3,2},{4,5},{5,4},{6,7},{7,6},{8,9},{9,8},{10,11... | collective-permute-start | bytes 1658888 | tf_op jit(solution)/shard_map/ppermute | solution.py:67
  216.2 6.7 %collective-permute-done.29 = bf16[320,432]{1,0:T(8,128)(2,1)S(1)} collective-permute-done((bf16[320,432]{1,0:T(8,128)(2,1)S(1)}, bf16[320,432]{1,0:T(8,128)(2,1)S(1)}, u32[]{:S(2)}, u32[]{:S(2)}) %collective-permute-start.29) | collective-permute-done | bytes 276512 | tf_op jit(solution)/shard_map/ppermute | solution.py:67
  (53 shorter events, 32.2 us)
Async XLA Ops:
  3.7 40.5 %collective-permute-start.4 = (bf16[512,896]{1,0:T(8,128)(2,1)S(1)}, bf16[512,896]{1,0:T(8,128)(2,1)S(1)}, u32[]{:S(2)}, u32[]{:S(2)}) collective-permute-start(bf16[512,896]{1,0:T(8,128)(2,1)S(1)} %shard_map.85.refs_9_), channel_id=1, source_target_pairs={{0,1},{1,0},{2,3},{3,2},{4,5},{5,4},{6,7},{7,6},{8,9},{9,8},{10,11... | collective-permute-start | bytes 2752520 | tf_op jit(solution)/shard_map/ppermute | solution.py:67
  12.5 31.7 %collective-permute-start.5 = (bf16[512,896]{1,0:T(8,128)(2,1)S(1)}, bf16[512,896]{1,0:T(8,128)(2,1)S(1)}, u32[]{:S(2)}, u32[]{:S(2)}) collective-permute-start(bf16[512,896]{1,0:T(8,128)(2,1)S(1)} %shard_map.85.refs_9_), channel_id=1, source_target_pairs={{0,128},{128,0},{1,129},{129,1},{2,130},{130,2},{3,131},{131,3},{4... | collective-permute-start | bytes 2752520 | tf_op jit(solution)/shard_map/ppermute | solution.py:67
  14.4 10.2 %collective-permute-start.2 = (bf16[592,128]{1,0:T(8,128)(2,1)S(1)}, bf16[592,128]{1,0:T(8,128)(2,1)S(1)}, u32[]{:S(2)}, u32[]{:S(2)}) collective-permute-start(bf16[592,128]{1,0:T(8,128)(2,1)S(1)} %pad_maximum_fusion.2), channel_id=1, source_target_pairs={{0,0},{1,1},{2,128},{3,129},{4,4},{5,5},{6,132},{7,133},{8,8},{9,9... | collective-permute-start | bytes 454664 | tf_op jit(solution)/shard_map/ppermute | solution.py:253
  15.1 25.8 %collective-permute-start.3 = (bf16[592,128]{1,0:T(8,128)(2,1)S(1)}, bf16[592,128]{1,0:T(8,128)(2,1)S(1)}, u32[]{:S(2)}, u32[]{:S(2)}) collective-permute-start(bf16[592,128]{1,0:T(8,128)(2,1)S(1)} %pad_maximum_fusion.2), channel_id=1, source_target_pairs={{0,2},{1,3},{2,130},{3,131},{4,6},{5,7},{6,134},{7,135},{8,10},{9,... | collective-permute-start | bytes 454664 | tf_op jit(solution)/shard_map/ppermute | solution.py:253
  23.9 17.0 %collective-permute-start = (bf16[592,128]{1,0:T(8,128)(2,1)S(1)}, bf16[592,128]{1,0:T(8,128)(2,1)S(1)}, u32[]{:S(2)}, u32[]{:S(2)}) collective-permute-start(bf16[592,128]{1,0:T(8,128)(2,1)S(1)} %pad_maximum_fusion.2), channel_id=1, source_target_pairs={{0,0},{1,1},{2,128},{3,129},{4,64},{5,65},{6,192},{7,193},{8,256},... | collective-permute-start | bytes 454664 | tf_op jit(solution)/shard_map/ppermute | solution.py:256
  24.6 19.6 %collective-permute-start.1 = (bf16[592,128]{1,0:T(8,128)(2,1)S(1)}, bf16[592,128]{1,0:T(8,128)(2,1)S(1)}, u32[]{:S(2)}, u32[]{:S(2)}) collective-permute-start(bf16[592,128]{1,0:T(8,128)(2,1)S(1)} %pad_maximum_fusion.2), channel_id=1, source_target_pairs={{0,256},{1,257},{2,384},{3,385},{4,320},{5,321},{6,448},{7,449},{8... | collective-permute-start | bytes 454664 | tf_op jit(solution)/shard_map/ppermute | solution.py:257
  44.2 11.6 %collective-permute-start.6 = (bf16[2,592,128]{2,1,0:T(8,128)(2,1)S(1)}, bf16[2,592,128]{2,1,0:T(8,128)(2,1)S(1)}, u32[]{:S(2)}, u32[]{:S(2)}) collective-permute-start(bf16[2,592,128]{2,1,0:T(8,128)(2,1)S(1)} %pad_maximum_fusion.1.refs_0_), channel_id=1, source_target_pairs={{0,16},{16,32},{32,48},{48,64},{64,80},{80,96},{96,112},{112,0},{1... | collective-permute-start | bytes 909320 | tf_op jit(solution)/shard_map/ppermute | solution.py:71
  46.1 12.6 %collective-permute-start.7 = (bf16[2,592,128]{2,1,0:T(8,128)(2,1)S(1)}, bf16[2,592,128]{2,1,0:T(8,128)(2,1)S(1)}, u32[]{:S(2)}, u32[]{:S(2)}) collective-permute-start(bf16[2,592,128]{2,1,0:T(8,128)(2,1)S(1)} %pad_maximum_fusion.1.refs_0_), channel_id=1, source_target_pairs={{0,112},{16,0},{32,16},{48,32},{64,48},{80,64},{96,80},{112,96},{1... | collective-permute-start | bytes 909320 | tf_op jit(solution)/shard_map/ppermute | solution.py:71
  55.7 11.0 %collective-permute-start.8 = (bf16[2,592,128]{2,1,0:T(8,128)(2,1)S(1)}, bf16[2,592,128]{2,1,0:T(8,128)(2,1)S(1)}, u32[]{:S(2)}, u32[]{:S(2)}) collective-permute-start(bf16[2,592,128]{2,1,0:T(8,128)(2,1)S(1)} %collective-permute-done.6.refs_1_), channel_id=1, source_target_pairs={{0,16},{16,32},{32,48},{48,64},{64,80},{80,96},{96,112},{112,0},{1... | collective-permute-start | bytes 909320 | tf_op jit(solution)/shard_map/ppermute | solution.py:71
  58.7 14.6 %collective-permute-start.9 = (bf16[2,592,128]{2,1,0:T(8,128)(2,1)S(1)}, bf16[2,592,128]{2,1,0:T(8,128)(2,1)S(1)}, u32[]{:S(2)}, u32[]{:S(2)}) collective-permute-start(bf16[2,592,128]{2,1,0:T(8,128)(2,1)S(1)} %collective-permute-done.7.refs_2_), channel_id=1, source_target_pairs={{0,112},{16,0},{32,16},{48,32},{64,48},{80,64},{96,80},{112,96},{1... | collective-permute-start | bytes 909320 | tf_op jit(solution)/shard_map/ppermute | solution.py:71
  66.7 11.4 %collective-permute-start.10 = (bf16[2,592,128]{2,1,0:T(8,128)(2,1)S(1)}, bf16[2,592,128]{2,1,0:T(8,128)(2,1)S(1)}, u32[]{:S(2)}, u32[]{:S(2)}) collective-permute-start(bf16[2,592,128]{2,1,0:T(8,128)(2,1)S(1)} %collective-permute-done.8.refs_3_), channel_id=1, source_target_pairs={{0,16},{16,32},{32,48},{48,64},{64,80},{80,96},{96,112},{112,0},{1... | collective-permute-start | bytes 909320 | tf_op jit(solution)/shard_map/ppermute | solution.py:71
  68.8 31.9 %collective-permute-start.14 = (bf16[512,896]{1,0:T(8,128)(2,1)S(1)}, bf16[512,896]{1,0:T(8,128)(2,1)S(1)}, u32[]{:S(2)}, u32[]{:S(2)}) collective-permute-start(bf16[512,896]{1,0:T(8,128)(2,1)S(1)} %collective-permute-done.5.refs_11_), channel_id=1, source_target_pairs={{0,1},{1,0},{2,3},{3,2},{4,5},{5,4},{6,7},{7,6},{8,9},{9,8},{10,11... | collective-permute-start | bytes 2752520 | tf_op jit(solution)/shard_map/ppermute | solution.py:67
  73.3 11.4 %collective-permute-start.11 = (bf16[2,592,128]{2,1,0:T(8,128)(2,1)S(1)}, bf16[2,592,128]{2,1,0:T(8,128)(2,1)S(1)}, u32[]{:S(2)}, u32[]{:S(2)}) collective-permute-start(bf16[2,592,128]{2,1,0:T(8,128)(2,1)S(1)} %collective-permute-done.9.refs_4_), channel_id=1, source_target_pairs={{0,112},{16,0},{32,16},{48,32},{64,48},{80,64},{96,80},{112,96},{1... | collective-permute-start | bytes 909320 | tf_op jit(solution)/shard_map/ppermute | solution.py:71
  78.2 24.4 %collective-permute-start.12 = (bf16[592,128]{1,0:T(8,128)(2,1)S(1)}, bf16[592,128]{1,0:T(8,128)(2,1)S(1)}, u32[]{:S(2)}, u32[]{:S(2)}) collective-permute-start(bf16[592,128]{1,0:T(8,128)(2,1)S(1)} %slice_bitcast_fusion.4), channel_id=1, source_target_pairs={{0,16},{16,32},{32,48},{48,64},{64,80},{80,96},{96,112},{112,0},{1... | collective-permute-start | bytes 454664 | tf_op jit(solution)/shard_map/ppermute | solution.py:71
  84.8 30.3 %copy-start.2 = (f32[864,432]{0,1:T(8,128)S(1)}, f32[864,432]{0,1:T(8,128)}, u32[]{:S(2)}) copy-start(f32[864,432]{0,1:T(8,128)} %param.9) | copy-start | bytes 4478980
  84.8 30.3 %copy-start.3 = (f32[320,160]{0,1:T(8,128)S(1)}, f32[320,160]{0,1:T(8,128)}, u32[]{:S(2)}) copy-start(f32[320,160]{0,1:T(8,128)} %param.8) | copy-start | bytes 614404
  84.8 17.8 %collective-permute-start.13 = (bf16[592,128]{1,0:T(8,128)(2,1)S(1)}, bf16[592,128]{1,0:T(8,128)(2,1)S(1)}, u32[]{:S(2)}, u32[]{:S(2)}) collective-permute-start(bf16[592,128]{1,0:T(8,128)(2,1)S(1)} %slice_bitcast_fusion.3), channel_id=1, source_target_pairs={{0,112},{16,0},{32,16},{48,32},{64,48},{80,64},{96,80},{112,96},{1... | collective-permute-start | bytes 454664 | tf_op jit(solution)/shard_map/ppermute | solution.py:71
  90.2 20.5 %collective-permute-start.15 = (bf16[2,592,128]{2,1,0:T(8,128)(2,1)S(1)}, bf16[2,592,128]{2,1,0:T(8,128)(2,1)S(1)}, u32[]{:S(2)}, u32[]{:S(2)}) collective-permute-start(bf16[2,592,128]{2,1,0:T(8,128)(2,1)S(1)} %pad_maximum_fusion.c0), channel_id=1, source_target_pairs={{0,4},{4,8},{8,12},{12,0},{1,5},{5,9},{9,13},{13,1},{2,6},{6,10},{... | collective-permute-start | bytes 909320 | tf_op jit(solution)/shard_map/ppermute | solution.py:71
  94.3 20.7 %collective-permute-start.16 = (bf16[2,592,128]{2,1,0:T(8,128)(2,1)S(1)}, bf16[2,592,128]{2,1,0:T(8,128)(2,1)S(1)}, u32[]{:S(2)}, u32[]{:S(2)}) collective-permute-start(bf16[2,592,128]{2,1,0:T(8,128)(2,1)S(1)} %pad_maximum_fusion.c0), channel_id=1, source_target_pairs={{0,8},{4,12},{8,0},{12,4},{1,9},{5,13},{9,1},{13,5},{2,10},{6,14},... | collective-permute-start | bytes 909320 | tf_op jit(solution)/shard_map/ppermute | solution.py:71
  100.7 14.3 %collective-permute-start.17 = (bf16[2,592,128]{2,1,0:T(8,128)(2,1)S(1)}, bf16[2,592,128]{2,1,0:T(8,128)(2,1)S(1)}, u32[]{:S(2)}, u32[]{:S(2)}) collective-permute-start(bf16[2,592,128]{2,1,0:T(8,128)(2,1)S(1)} %pad_maximum_fusion.c0), channel_id=1, source_target_pairs={{0,12},{4,0},{8,4},{12,8},{1,13},{5,1},{9,5},{13,9},{2,14},{6,2},{... | collective-permute-start | bytes 909320 | tf_op jit(solution)/shard_map/ppermute | solution.py:71
  105.4 13.6 %collective-permute-start.18 = (bf16[2,592,128]{2,1,0:T(8,128)(2,1)S(1)}, bf16[2,592,128]{2,1,0:T(8,128)(2,1)S(1)}, u32[]{:S(2)}, u32[]{:S(2)}) collective-permute-start(bf16[2,592,128]{2,1,0:T(8,128)(2,1)S(1)} %get-tuple-element.40), channel_id=1, source_target_pairs={{0,4},{4,8},{8,12},{12,0},{1,5},{5,9},{9,13},{13,1},{2,6},{6,10},{... | collective-permute-start | bytes 909320 | tf_op jit(solution)/shard_map/ppermute | solution.py:71
  108.8 15.6 %collective-permute-start.19 = (bf16[2,592,128]{2,1,0:T(8,128)(2,1)S(1)}, bf16[2,592,128]{2,1,0:T(8,128)(2,1)S(1)}, u32[]{:S(2)}, u32[]{:S(2)}) collective-permute-start(bf16[2,592,128]{2,1,0:T(8,128)(2,1)S(1)} %get-tuple-element.41), channel_id=1, source_target_pairs={{0,8},{4,12},{8,0},{12,4},{1,9},{5,13},{9,1},{13,5},{2,10},{6,14},... | collective-permute-start | bytes 909320 | tf_op jit(solution)/shard_map/ppermute | solution.py:71
  110.7 15.5 %collective-permute-start.20 = (bf16[2,592,128]{2,1,0:T(8,128)(2,1)S(1)}, bf16[2,592,128]{2,1,0:T(8,128)(2,1)S(1)}, u32[]{:S(2)}, u32[]{:S(2)}) collective-permute-start(bf16[2,592,128]{2,1,0:T(8,128)(2,1)S(1)} %get-tuple-element.42), channel_id=1, source_target_pairs={{0,12},{4,0},{8,4},{12,8},{1,13},{5,1},{9,5},{13,9},{2,14},{6,2},{... | collective-permute-start | bytes 909320 | tf_op jit(solution)/shard_map/ppermute | solution.py:71
  126.4 20.1 %collective-permute-start.26 = (bf16[2,512,896]{2,1,0:T(8,128)(2,1)S(1)}, bf16[2,512,896]{2,1,0:T(8,128)(2,1)S(1)}, u32[]{:S(2)}, u32[]{:S(2)}) collective-permute-start(bf16[2,512,896]{2,1,0:T(8,128)(2,1)S(1)} %get-tuple-element.49), channel_id=1, source_target_pairs={{0,1},{1,0},{2,3},{3,2},{4,5},{5,4},{6,7},{7,6},{8,9},{9,8},{10,11... | collective-permute-start | bytes 5505032 | tf_op jit(solution)/shard_map/ppermute | solution.py:67
  129.9 16.6 %collective-permute-start.21 = (bf16[1024,128]{1,0:T(8,128)(2,1)S(1)}, bf16[1024,128]{1,0:T(8,128)(2,1)S(1)}, u32[]{:S(2)}, u32[]{:S(2)}) collective-permute-start(bf16[1024,128]{1,0:T(8,128)(2,1)S(1)} %get-tuple-element.44), channel_id=1, source_target_pairs={{0,2},{2,0},{1,3},{3,1},{4,6},{6,4},{5,7},{7,5},{8,10},{10,8},{9,1... | collective-permute-start | bytes 786440 | tf_op jit(solution)/shard_map/ppermute | solution.py:67
  146.7 33.1 %collective-permute-start.27 = (bf16[512,896]{1,0:T(8,128)(2,1)S(1)}, bf16[512,896]{1,0:T(8,128)(2,1)S(1)}, u32[]{:S(2)}, u32[]{:S(2)}) collective-permute-start(bf16[512,896]{1,0:T(8,128)(2,1)S(1)} %fusion), channel_id=1, source_target_pairs={{0,128},{128,0},{1,129},{129,1},{2,130},{130,2},{3,131},{131,3},{4... | collective-permute-start | bytes 2752520 | tf_op jit(solution)/shard_map/ppermute | solution.py:67
  159.5 10.1 %collective-permute-start.23 = (bf16[2,432,128]{2,1,0:T(8,128)(2,1)S(1)}, bf16[2,432,128]{2,1,0:T(8,128)(2,1)S(1)}, u32[]{:S(2)}, u32[]{:S(2)}) collective-permute-start(bf16[2,432,128]{2,1,0:T(8,128)(2,1)S(1)} %get-tuple-element.46.right), channel_id=1, source_target_pairs={{0,4},{4,8},{8,12},{12,0},{1,5},{5,9},{9,13},{13,1},{2,6},{6,10},{... | collective-permute-start | bytes 663560 | tf_op jit(solution)/shard_map/ppermute | solution.py:71
  162.3 12.1 %collective-permute-start.24 = (bf16[2,432,128]{2,1,0:T(8,128)(2,1)S(1)}, bf16[2,432,128]{2,1,0:T(8,128)(2,1)S(1)}, u32[]{:S(2)}, u32[]{:S(2)}) collective-permute-start(bf16[2,432,128]{2,1,0:T(8,128)(2,1)S(1)} %get-tuple-element.46.right), channel_id=1, source_target_pairs={{0,8},{4,12},{8,0},{12,4},{1,9},{5,13},{9,1},{13,5},{2,10},{6,14},... | collective-permute-start | bytes 663560 | tf_op jit(solution)/shard_map/ppermute | solution.py:71
  166.9 9.4 %collective-permute-start.25 = (bf16[2,432,128]{2,1,0:T(8,128)(2,1)S(1)}, bf16[2,432,128]{2,1,0:T(8,128)(2,1)S(1)}, u32[]{:S(2)}, u32[]{:S(2)}) collective-permute-start(bf16[2,432,128]{2,1,0:T(8,128)(2,1)S(1)} %get-tuple-element.46.right), channel_id=1, source_target_pairs={{0,12},{4,0},{8,4},{12,8},{1,13},{5,1},{9,5},{13,9},{2,14},{6,2},{... | collective-permute-start | bytes 663560 | tf_op jit(solution)/shard_map/ppermute | solution.py:71
  168.9 0.7 collective-permute-start.22
  203.9 8.1 %collective-permute-start.28 = (bf16[2,320,432]{2,1,0:T(8,128)(2,1)S(1)}, bf16[2,320,432]{2,1,0:T(8,128)(2,1)S(1)}, u32[]{:S(2)}, u32[]{:S(2)}) collective-permute-start(bf16[2,320,432]{2,1,0:T(8,128)(2,1)S(1)} %get-tuple-element.57), channel_id=1, source_target_pairs={{0,1},{1,0},{2,3},{3,2},{4,5},{5,4},{6,7},{7,6},{8,9},{9,8},{10,11... | collective-permute-start | bytes 1658888 | tf_op jit(solution)/shard_map/ppermute | solution.py:67
  212.1 10.8 %collective-permute-start.29 = (bf16[320,432]{1,0:T(8,128)(2,1)S(1)}, bf16[320,432]{1,0:T(8,128)(2,1)S(1)}, u32[]{:S(2)}, u32[]{:S(2)}) collective-permute-start(bf16[320,432]{1,0:T(8,128)(2,1)S(1)} %fusion.1), channel_id=1, source_target_pairs={{0,128},{128,0},{1,129},{129,1},{2,130},{130,2},{3,131},{131,3},{4... | collective-permute-start | bytes 829448 | tf_op jit(solution)/shard_map/ppermute | solution.py:67
  (2 other events, 2.0 us)

commit v5 on v4

--- a/solution.py
+++ b/solution.py
@@ -53,11 +53,11 @@
     ]
 
 
-def column_perm(flip):
+def column_perm():
     return [
         (
             device(zg, p, y, xh, xl, w, core),
-            device(zg, w, y, xh, xl, p ^ flip, core),
+            device(zg, w, y, xh, xl, p, core),
         )
         for zg, p, y, xh, xl, w, core in coordinates()
     ]
@@ -250,17 +250,15 @@
 
     x = jnp.concatenate([activations.T, output_grads.T], 0)
     inverse = call(pack_kernel, shape(pack, bf16), 0, after(input_inverse.T, x), gradient_inverse.T)
-    near, far = (lax.ppermute(x, AXES, column_perm(j)) for j in range(2))
     first, second, col, inverse_c, inverse_z = lax.optimization_barrier(
         (
             lax.ppermute(x, AXES, panel_perm(0)),
             lax.ppermute(x, AXES, panel_perm(1)),
-            jnp.stack([near, far]),
+            lax.ppermute(x, AXES, column_perm()),
             swap(inverse, "core"),
             swap(inverse, "p"),
         )
     )
-    cols = [shift(col, X, 4, i + 1) for i in range(3)]
     u = jnp.stack([first, second])
     up, down = [u], [u]
     for _ in range(3):
@@ -268,7 +266,10 @@
         down.append(shift(down[-1], "y", RING, -1))
     ring = [u, up[1], down[1], up[2], down[2], up[3], down[3]]
     ring += [shift(up[3][0], "y", RING, 1), shift(down[3][1], "y", RING, -1)]
+
     inverse_zc = swap(inverse_z, "core")
+    col = jnp.stack([col, swap(after(col, up[1], down[1]), "w")])
+    cols = [shift(col, X, 4, i + 1) for i in range(3)]
 
     rows, own, *ahead = call(
         functools.partial(sides_kernel, da, dg, h),
@@ -299,21 +300,21 @@
     f_got = swap(after(f_send, send), "core")
     f_mid = after((f_keep + f_got[1].astype(f32)).astype(bf16), left)
     f_last = swap(f_mid, "p")
-    pieces = jnp.broadcast_to(after(piece, *rights, f_last), (16, *piece.shape))
+    pieces = jnp.broadcast_to(piece, (16, *piece.shape))
     lefts = lax.all_to_all(pieces, ("zg", "y"), 0, 0, tiled=True)
-
     input_factor, gradient_factor = call(
         functools.partial(factor_sum_kernel, da, dg, h),
         (shape((da, da * h), f32), shape((dg, dg * h), f32)),
-        0, after(i_own, lefts), g_own, f_got, f_last,
-    )
+        0, i_own, g_own, f_got, f_last,
+    )
+
     p_own, p_keep, p_send = call(
         functools.partial(product_kernel, h, 1.0 / tokens),
         (shape((da * h, dg), f32), shape((da * h, dg), f32), shape((2, da * h, dg), bf16)),
         2 * tokens * h * da * dg, lefts, right, *rights,
         scratch=[pltpu.VMEM((4, 2, dg, block), bf16)],
     )
-    p_got = swap(p_send, "core")
+    p_got = after(swap(p_send, "core"), f_last)
     p_last = swap((p_keep + p_got[1].astype(f32)).astype(bf16), "p")
     preconditioned = (p_own + p_got[0].astype(f32) + p_last.astype(f32)).astype(bf16)
     return input_factor.T, gradient_factor.T, preconditioned

time: 227 us -> 220 us (0.969)
  blocking collectives: 22.8 us -> 0 us
  local copies, waits for them, and re-layouts: 2.15 us -> 10.7 us
  starting transfers between devices: 133 us -> 137 us
  Pallas kernels: 8.47 us -> 12.1 us
  other arithmetic: 2.12 us -> 4.59 us
    all_to_all x1 -> x0, blocking collectives: 22.8 us -> none  [local(): lefts = lax.all_to_all(pieces, ('zg', 'y'), 0, 0, tiled=True)]
    all_to_all x0 -> x1, starting transfers between devices: none -> 18.9 us  [local(): lefts = lax.all_to_all(pieces, ('zg', 'y'), 0, 0, tiled=True)]
    ppermute x1, waiting for transfers between devices: 3.2 us -> 15.1 us  [local(): lax.ppermute(x, AXES, panel_perm(1))]
    ppermute x2 -> x1, starting transfers between devices: 9.46 us -> 0.67 us  [local(): lax.ppermute(x, AXES, column_perm())]
    ppermute x17, waiting for transfers between devices: 28.3 us -> 20.2 us  [shift(): return lax.ppermute(x, axis, [(i, (i + by) % size) for i in range(size)])]
    ppermute x8 -> x9, starting transfers between devices: 50.1 us -> 42.4 us  [swap(): return lax.ppermute(x, axis, [(0, 1), (1, 0)])]
    unnamed x8 -> x32, local copies, waits for them, and re-layouts: 2.04 us -> 9.75 us
    ppermute x2 -> x1, waiting for transfers between devices: 4.18 us -> 0.01 us  [local(): lax.ppermute(x, AXES, column_perm())]
  transfers between devices with their start and end apart: 30 -> 31, of which waited for: 14 -> 10; matrix products, arithmetic and copies ran while one was open for 0% -> 2% of each run, Pallas kernels for 3% -> 5%
where the time goes in v5:
time: 220 us; the launch traced here: 219 us
  starting transfers between devices  137 us (62%)
  waiting for transfers between devices  53.5 us (24%)
  Pallas kernels  12.1 us (6%)
  local copies, waits for them, and re-layouts  10.7 us (5%)
  other arithmetic  4.59 us (2%)
    ppermute x17, starting transfers between devices, shift(): return lax.ppermute(x, axis, [(i, (i + by) % size) for i in range(size)])  63.3 us
    ppermute x9, starting transfers between devices, swap(): return lax.ppermute(x, axis, [(0, 1), (1, 0)])  42.4 us
    ppermute x17, waiting for transfers between devices, shift(): return lax.ppermute(x, axis, [(i, (i + by) % size) for i in range(size)])  20.2 us
    all_to_all x1, starting transfers between devices, local(): lefts = lax.all_to_all(pieces, ('zg', 'y'), 0, 0, tiled=True)  18.9 us
    ppermute x9, waiting for transfers between devices, swap(): return lax.ppermute(x, axis, [(0, 1), (1, 0)])  18.1 us
    ppermute x1, waiting for transfers between devices, local(): lax.ppermute(x, AXES, panel_perm(1))  15.1 us
    pallas_call x7, Pallas kernels, call(): pl.pallas_call(kernel, out_shape=out, in_specs=[VMEM] * len(args), out_sp...  12.1 us
    ppermute x1, starting transfers between devices, local(): lax.ppermute(x, AXES, panel_perm(1))  9.94 us
  transfers between devices with their start and end apart: 31, of which 10 were waited for; matrix products, arithmetic and copies ran while one was open for 2% of the time, Pallas kernels for 5%

profile of v5, /device:TPU:1, one launch (start us, length us, event | category | flops | bytes accessed | tf_op | source)
XLA Modules:
  0.0 218.6 jit_solution(6832097096043175799)
XLA Ops:
  3.7 8.8 %collective-permute-start.3 = (bf16[512,896]{1,0:T(8,128)(2,1)S(1)}, bf16[512,896]{1,0:T(8,128)(2,1)S(1)}, u32[]{:S(2)}, u32[]{:S(2)}) collective-permute-start(bf16[512,896]{1,0:T(8,128)(2,1)S(1)} %shard_map.85.refs_9_), channel_id=1, source_target_pairs={{0,1},{1,0},{2,3},{3,2},{4,5},{5,4},{6,7},{7,6},{8,9},{9,8},{10,11... | collective-permute-start | bytes 2752520 | tf_op jit(solution)/shard_map/ppermute | solution.py:67
  15.1 9.9 %collective-permute-start.1 = (bf16[592,128]{1,0:T(8,128)(2,1)S(1)}, bf16[592,128]{1,0:T(8,128)(2,1)S(1)}, u32[]{:S(2)}, u32[]{:S(2)}) collective-permute-start(bf16[592,128]{1,0:T(8,128)(2,1)S(1)} %pad_maximum_fusion.2), channel_id=1, source_target_pairs={{0,256},{1,257},{2,384},{3,385},{4,320},{5,321},{6,448},{7,449},{8... | collective-permute-start | bytes 454664 | tf_op jit(solution)/shard_map/ppermute | solution.py:256
  25.7 15.1 %collective-permute-done.1 = bf16[592,128]{1,0:T(8,128)(2,1)S(1)} collective-permute-done((bf16[592,128]{1,0:T(8,128)(2,1)S(1)}, bf16[592,128]{1,0:T(8,128)(2,1)S(1)}, u32[]{:S(2)}, u32[]{:S(2)}) %collective-permute-start.1) | collective-permute-done | bytes 151584 | tf_op jit(solution)/shard_map/ppermute | solution.py:256
  42.8 4.6 %collective-permute-start.6 = (bf16[2,592,128]{2,1,0:T(8,128)(2,1)S(1)}, bf16[2,592,128]{2,1,0:T(8,128)(2,1)S(1)}, u32[]{:S(2)}, u32[]{:S(2)}) collective-permute-start(bf16[2,592,128]{2,1,0:T(8,128)(2,1)S(1)} %pad_maximum_fusion.refs_0_), channel_id=1, source_target_pairs={{0,112},{16,0},{32,16},{48,32},{64,48},{80,64},{96,80},{112,96},{1... | collective-permute-start | bytes 909320 | tf_op jit(solution)/shard_map/ppermute | solution.py:71
  47.4 4.7 %collective-permute-done.5.refs_1_ = bf16[2,592,128]{2,1,0:T(8,128)(2,1)S(1)} collective-permute-done((bf16[2,592,128]{2,1,0:T(8,128)(2,1)S(1)}, bf16[2,592,128]{2,1,0:T(8,128)(2,1)S(1)}, u32[]{:S(2)}, u32[]{:S(2)}) %collective-permute-start.5) | collective-permute-done | bytes 303136 | tf_op jit(solution)/shard_map/ppermute | solution.py:71
  54.1 4.6 %collective-permute-start.8 = (bf16[2,592,128]{2,1,0:T(8,128)(2,1)S(1)}, bf16[2,592,128]{2,1,0:T(8,128)(2,1)S(1)}, u32[]{:S(2)}, u32[]{:S(2)}) collective-permute-start(bf16[2,592,128]{2,1,0:T(8,128)(2,1)S(1)} %collective-permute-done.6.refs_2_), channel_id=1, source_target_pairs={{0,112},{16,0},{32,16},{48,32},{64,48},{80,64},{96,80},{112,96},{1... | collective-permute-start | bytes 909320 | tf_op jit(solution)/shard_map/ppermute | solution.py:71
  58.7 3.8 %collective-permute-done.7.refs_3_ = bf16[2,592,128]{2,1,0:T(8,128)(2,1)S(1)} collective-permute-done((bf16[2,592,128]{2,1,0:T(8,128)(2,1)S(1)}, bf16[2,592,128]{2,1,0:T(8,128)(2,1)S(1)}, u32[]{:S(2)}, u32[]{:S(2)}) %collective-permute-start.7) | collective-permute-done | bytes 303136 | tf_op jit(solution)/shard_map/ppermute | solution.py:71
  64.4 4.3 %collective-permute-start.13 = (bf16[512,896]{1,0:T(8,128)(2,1)S(1)}, bf16[512,896]{1,0:T(8,128)(2,1)S(1)}, u32[]{:S(2)}, u32[]{:S(2)}) collective-permute-start(bf16[512,896]{1,0:T(8,128)(2,1)S(1)} %collective-permute-done.4.refs_11_), channel_id=1, source_target_pairs={{0,1},{1,0},{2,3},{3,2},{4,5},{5,4},{6,7},{7,6},{8,9},{9,8},{10,11... | collective-permute-start | bytes 2752520 | tf_op jit(solution)/shard_map/ppermute | solution.py:67
  68.7 4.9 %collective-permute-start.10 = (bf16[2,592,128]{2,1,0:T(8,128)(2,1)S(1)}, bf16[2,592,128]{2,1,0:T(8,128)(2,1)S(1)}, u32[]{:S(2)}, u32[]{:S(2)}) collective-permute-start(bf16[2,592,128]{2,1,0:T(8,128)(2,1)S(1)} %collective-permute-done.8.refs_4_), channel_id=1, source_target_pairs={{0,112},{16,0},{32,16},{48,32},{64,48},{80,64},{96,80},{112,96},{1... | collective-permute-start | bytes 909320 | tf_op jit(solution)/shard_map/ppermute | solution.py:71
  73.5 9.5 %collective-permute-start.14 = (bf16[592,128]{1,0:T(8,128)(2,1)S(1)}, bf16[592,128]{1,0:T(8,128)(2,1)S(1)}, u32[]{:S(2)}, u32[]{:S(2)}) collective-permute-start(bf16[592,128]{1,0:T(8,128)(2,1)S(1)} %collective-permute-done.2), channel_id=1, source_target_pairs={{0,2},{2,0},{1,3},{3,1},{4,6},{6,4},{5,7},{7,5},{8,10},{10,8},{9,1... | collective-permute-start | bytes 454664 | tf_op jit(solution)/shard_map/ppermute | solution.py:67
  85.0 4.6 %collective-permute-start.12 = (bf16[592,128]{1,0:T(8,128)(2,1)S(1)}, bf16[592,128]{1,0:T(8,128)(2,1)S(1)}, u32[]{:S(2)}, u32[]{:S(2)}) collective-permute-start(bf16[592,128]{1,0:T(8,128)(2,1)S(1)} %slice_bitcast_fusion.1), channel_id=1, source_target_pairs={{0,112},{16,0},{32,16},{48,32},{64,48},{80,64},{96,80},{112,96},{1... | collective-permute-start | bytes 454664 | tf_op jit(solution)/shard_map/ppermute | solution.py:71
  89.7 4.8 %collective-permute-start.15 = (bf16[2,592,128]{2,1,0:T(8,128)(2,1)S(1)}, bf16[2,592,128]{2,1,0:T(8,128)(2,1)S(1)}, u32[]{:S(2)}, u32[]{:S(2)}) collective-permute-start(bf16[2,592,128]{2,1,0:T(8,128)(2,1)S(1)} %pad_maximum_fusion.1.c0), channel_id=1, source_target_pairs={{0,4},{4,8},{8,12},{12,0},{1,5},{5,9},{9,13},{13,1},{2,6},{6,10},{... | collective-permute-start | bytes 909320 | tf_op jit(solution)/shard_map/ppermute | solution.py:71
  94.5 6.4 %collective-permute-start.16 = (bf16[2,592,128]{2,1,0:T(8,128)(2,1)S(1)}, bf16[2,592,128]{2,1,0:T(8,128)(2,1)S(1)}, u32[]{:S(2)}, u32[]{:S(2)}) collective-permute-start(bf16[2,592,128]{2,1,0:T(8,128)(2,1)S(1)} %pad_maximum_fusion.1.c0), channel_id=1, source_target_pairs={{0,8},{4,12},{8,0},{12,4},{1,9},{5,13},{9,1},{13,5},{2,10},{6,14},... | collective-permute-start | bytes 909320 | tf_op jit(solution)/shard_map/ppermute | solution.py:71
  101.0 4.0 %collective-permute-start.17 = (bf16[2,592,128]{2,1,0:T(8,128)(2,1)S(1)}, bf16[2,592,128]{2,1,0:T(8,128)(2,1)S(1)}, u32[]{:S(2)}, u32[]{:S(2)}) collective-permute-start(bf16[2,592,128]{2,1,0:T(8,128)(2,1)S(1)} %pad_maximum_fusion.1.c0), channel_id=1, source_target_pairs={{0,12},{4,0},{8,4},{12,8},{1,13},{5,1},{9,5},{13,9},{2,14},{6,2},{... | collective-permute-start | bytes 909320 | tf_op jit(solution)/shard_map/ppermute | solution.py:71
  105.0 2.8 %shard_map.86 = (bf16[8,2,592,128]{3,2,1,0:T(8,128)(2,1)S(1)}, f32[2,592,128]{2,1,0:T(8,128)S(1)}, bf16[2,592,128]{2,1,0:T(8,128)(2,1)S(1)}, bf16[2,592,128]{2,1,0:T(8,128)(2,1)S(1)}, bf16[2,592,128]{2,1,0:T(8,128)(2,1)S(1)}) custom-call(bf16[2,592,128]{2,1,0:T(8,128)(2,1)S(1)} %pad_maximum_fusion.refs_0_, ...), custom_call_target="tpu_custom_call" | custom-call | flops 1738539008 | bytes 10035200 | tf_op jit(solution)/shard_map/pallas_call | solution.py:84
  109.7 3.1 %collective-permute-start.19 = (bf16[2,592,128]{2,1,0:T(8,128)(2,1)S(1)}, bf16[2,592,128]{2,1,0:T(8,128)(2,1)S(1)}, u32[]{:S(2)}, u32[]{:S(2)}) collective-permute-start(bf16[2,592,128]{2,1,0:T(8,128)(2,1)S(1)} %get-tuple-element.44), channel_id=1, source_target_pairs={{0,8},{4,12},{8,0},{12,4},{1,9},{5,13},{9,1},{13,5},{2,10},{6,14},... | collective-permute-start | bytes 909320 | tf_op jit(solution)/shard_map/ppermute | solution.py:71
  112.8 3.4 %collective-permute-start.20 = (bf16[2,592,128]{2,1,0:T(8,128)(2,1)S(1)}, bf16[2,592,128]{2,1,0:T(8,128)(2,1)S(1)}, u32[]{:S(2)}, u32[]{:S(2)}) collective-permute-start(bf16[2,592,128]{2,1,0:T(8,128)(2,1)S(1)} %get-tuple-element.45), channel_id=1, source_target_pairs={{0,12},{4,0},{8,4},{12,8},{1,13},{5,1},{9,5},{13,9},{2,14},{6,2},{... | collective-permute-start | bytes 909320 | tf_op jit(solution)/shard_map/ppermute | solution.py:71
  116.2 4.0 %shard_map.87 = (f32[160,320]{1,0:T(8,128)S(1)}, f32[432,864]{1,0:T(8,128)S(1)}, f32[512,896]{1,0:T(8,128)S(1)}, bf16[2,512,896]{2,1,0:T(8,128)(2,1)}) custom-call(bf16[8,2,592,128]{3,2,1,0:T(8,128)(2,1)S(1)} %get-tuple-element.36.rows, bf16[2,592,128]{2,1,0:T(8,128)(2,1)S(1)} %pad_maximum_fusion.1.c0, bf16[2,592,128]{2,1,0:T(8,128)(2,1)S(1)} %collective-permute-done.15.c1, ...), custom_call_target="tpu_custom_call" | custom-call | flops 1738539008 | bytes 10702848 | tf_op jit(solution)/shard_map/pallas_call | solution.py:84
  121.5 3.8 %collective-permute-done.19.r2 = bf16[2,592,128]{2,1,0:T(8,128)(2,1)S(1)} collective-permute-done((bf16[2,592,128]{2,1,0:T(8,128)(2,1)S(1)}, bf16[2,592,128]{2,1,0:T(8,128)(2,1)S(1)}, u32[]{:S(2)}, u32[]{:S(2)}) %collective-permute-start.19) | collective-permute-done | bytes 303136 | tf_op jit(solution)/shard_map/ppermute | solution.py:71
  125.3 2.6 %collective-permute-done.20.r3 = bf16[2,592,128]{2,1,0:T(8,128)(2,1)S(1)} collective-permute-done((bf16[2,592,128]{2,1,0:T(8,128)(2,1)S(1)}, bf16[2,592,128]{2,1,0:T(8,128)(2,1)S(1)}, u32[]{:S(2)}, u32[]{:S(2)}) %collective-permute-start.20) | collective-permute-done | bytes 303136 | tf_op jit(solution)/shard_map/ppermute | solution.py:71
  128.2 3.5 %collective-permute-start.21 = (bf16[2,512,896]{2,1,0:T(8,128)(2,1)}, bf16[2,512,896]{2,1,0:T(8,128)(2,1)S(1)}, u32[]{:S(2)}, u32[]{:S(2)}) collective-permute-start(bf16[2,512,896]{2,1,0:T(8,128)(2,1)} %get-tuple-element.47), channel_id=1, source_target_pairs={{0,1},{1,0},{2,3},{3,2},{4,5},{5,4},{6,7},{7,6},{8,9},{9,8},{10,11... | collective-permute-start | bytes 5505032 | tf_op jit(solution)/shard_map/ppermute | solution.py:67
  131.6 4.6 %collective-permute-start.22 = (bf16[1024,128]{1,0:T(8,128)(2,1)S(1)}, bf16[1024,128]{1,0:T(8,128)(2,1)S(1)}, u32[]{:S(2)}, u32[]{:S(2)}) collective-permute-start(bf16[1024,128]{1,0:T(8,128)(2,1)S(1)} %get-tuple-element.46), channel_id=1, source_target_pairs={{0,2},{2,0},{1,3},{3,1},{4,6},{6,4},{5,7},{7,5},{8,10},{10,8},{9,1... | collective-permute-start | bytes 786440 | tf_op jit(solution)/shard_map/ppermute | solution.py:67
  136.2 11.2 %collective-permute-done.22.got = bf16[1024,128]{1,0:T(8,128)(2,1)S(1)} collective-permute-done((bf16[1024,128]{1,0:T(8,128)(2,1)S(1)}, bf16[1024,128]{1,0:T(8,128)(2,1)S(1)}, u32[]{:S(2)}, u32[]{:S(2)}) %collective-permute-start.22) | collective-permute-done | bytes 262176 | tf_op jit(solution)/shard_map/ppermute | solution.py:67
  149.8 18.9 %all-to-all-start = ((bf16[16,160,128]{2,1,0:T(8,128)(2,1)}), bf16[16,160,128]{2,1,0:T(8,128)(2,1)}, u32[]{:S(2)}, u32[]{:S(2)}) async-start(bf16[16,160,128]{2,1,0:T(8,128)(2,1)} %broadcast_in_dim.3), calls=%async_computation | async-start | bytes 1310720 | tf_op jit(solution)/shard_map/all_to_all | solution.py:304
  168.8 2.7 %fusion = bf16[512,896]{1,0:T(8,128)(2,1)} fusion(f32[512,896]{1,0:T(8,128)} %copy-done, bf16[2,512,896]{2,1,0:T(8,128)(2,1)S(1)} %collective-permute-done.21.got), kind=kLoop, calls=%fused_computation.1 | loop fusion | flops 1376256 | bytes 3670016 | tf_op jit(solution)/shard_map/convert_element_type | solution.py:301
  173.9 7.0 %collective-permute-start.25 = (bf16[2,432,128]{2,1,0:T(8,128)(2,1)S(1)}, bf16[2,432,128]{2,1,0:T(8,128)(2,1)S(1)}, u32[]{:S(2)}, u32[]{:S(2)}) collective-permute-start(bf16[2,432,128]{2,1,0:T(8,128)(2,1)S(1)} %copy-done.8), channel_id=1, source_target_pairs={{0,4},{4,8},{8,12},{12,0},{1,5},{5,9},{9,13},{13,1},{2,6},{6,10},{... | collective-permute-start | bytes 663560 | tf_op jit(solution)/shard_map/ppermute | solution.py:71
  180.9 4.6 %collective-permute-start.26 = (bf16[2,432,128]{2,1,0:T(8,128)(2,1)S(1)}, bf16[2,432,128]{2,1,0:T(8,128)(2,1)S(1)}, u32[]{:S(2)}, u32[]{:S(2)}) collective-permute-start(bf16[2,432,128]{2,1,0:T(8,128)(2,1)S(1)} %copy-done.8), channel_id=1, source_target_pairs={{0,8},{4,12},{8,0},{12,4},{1,9},{5,13},{9,1},{13,5},{2,10},{6,14},... | collective-permute-start | bytes 663560 | tf_op jit(solution)/shard_map/ppermute | solution.py:71
  188.1 3.0 %collective-permute-done.26.r2 = bf16[2,432,128]{2,1,0:T(8,128)(2,1)S(1)} collective-permute-done((bf16[2,432,128]{2,1,0:T(8,128)(2,1)S(1)}, bf16[2,432,128]{2,1,0:T(8,128)(2,1)S(1)}, u32[]{:S(2)}, u32[]{:S(2)}) %collective-permute-start.26) | collective-permute-done | bytes 221216 | tf_op jit(solution)/shard_map/ppermute | solution.py:71
  200.8 4.3 %collective-permute-start.28 = (bf16[2,320,432]{2,1,0:T(8,128)(2,1)S(1)}, bf16[2,320,432]{2,1,0:T(8,128)(2,1)S(1)}, u32[]{:S(2)}, u32[]{:S(2)}) collective-permute-start(bf16[2,320,432]{2,1,0:T(8,128)(2,1)S(1)} %get-tuple-element.56), channel_id=1, source_target_pairs={{0,1},{1,0},{2,3},{3,2},{4,5},{5,4},{6,7},{7,6},{8,9},{9,8},{10,11... | collective-permute-start | bytes 1658888 | tf_op jit(solution)/shard_map/ppermute | solution.py:67
  206.9 3.0 %collective-permute-start.29 = (bf16[320,432]{1,0:T(8,128)(2,1)S(1)}, bf16[320,432]{1,0:T(8,128)(2,1)S(1)}, u32[]{:S(2)}, u32[]{:S(2)}) collective-permute-start(bf16[320,432]{1,0:T(8,128)(2,1)S(1)} %fusion.1), channel_id=1, source_target_pairs={{0,128},{128,0},{1,129},{129,1},{2,130},{130,2},{3,131},{131,3},{4... | collective-permute-start | bytes 829448 | tf_op jit(solution)/shard_map/ppermute | solution.py:67
  210.0 2.6 %shard_map.90 = (f32[160,320]{1,0:T(8,128)}, f32[432,864]{1,0:T(8,128)}) custom-call(f32[160,320]{1,0:T(8,128)S(1)} %copy-done.3, f32[432,864]{1,0:T(8,128)S(1)} %get-tuple-element.40.g_own, bf16[2,512,896]{2,1,0:T(8,128)(2,1)S(1)} %collective-permute-done.21.got, bf16[512,896]{1,0:T(8,128)(2,1)} %collective-permute-done.23.last), custom_call_target="tpu_custom_call" | custom-call | bytes 6148096 | tf_op jit(solution)/shard_map/pallas_call | solution.py:84
  212.6 5.1 %collective-permute-done.29 = bf16[320,432]{1,0:T(8,128)(2,1)S(1)} collective-permute-done((bf16[320,432]{1,0:T(8,128)(2,1)S(1)}, bf16[320,432]{1,0:T(8,128)(2,1)S(1)}, u32[]{:S(2)}, u32[]{:S(2)}) %collective-permute-start.29) | collective-permute-done | bytes 276512 | tf_op jit(solution)/shard_map/ppermute | solution.py:67
  (78 shorter events, 37.2 us)
Async XLA Ops:
  3.7 37.2 %collective-permute-start.3 = (bf16[512,896]{1,0:T(8,128)(2,1)S(1)}, bf16[512,896]{1,0:T(8,128)(2,1)S(1)}, u32[]{:S(2)}, u32[]{:S(2)}) collective-permute-start(bf16[512,896]{1,0:T(8,128)(2,1)S(1)} %shard_map.85.refs_9_), channel_id=1, source_target_pairs={{0,1},{1,0},{2,3},{3,2},{4,5},{5,4},{6,7},{7,6},{8,9},{9,8},{10,11... | collective-permute-start | bytes 2752520 | tf_op jit(solution)/shard_map/ppermute | solution.py:67
  12.5 28.4 %collective-permute-start.4 = (bf16[512,896]{1,0:T(8,128)(2,1)S(1)}, bf16[512,896]{1,0:T(8,128)(2,1)S(1)}, u32[]{:S(2)}, u32[]{:S(2)}) collective-permute-start(bf16[512,896]{1,0:T(8,128)(2,1)S(1)} %shard_map.85.refs_9_), channel_id=1, source_target_pairs={{0,128},{128,0},{1,129},{129,1},{2,130},{130,2},{3,131},{131,3},{4... | collective-permute-start | bytes 2752520 | tf_op jit(solution)/shard_map/ppermute | solution.py:67
  14.4 11.3 %collective-permute-start = (bf16[592,128]{1,0:T(8,128)(2,1)S(1)}, bf16[592,128]{1,0:T(8,128)(2,1)S(1)}, u32[]{:S(2)}, u32[]{:S(2)}) collective-permute-start(bf16[592,128]{1,0:T(8,128)(2,1)S(1)} %pad_maximum_fusion.2), channel_id=1, source_target_pairs={{0,0},{1,1},{2,128},{3,129},{4,64},{5,65},{6,192},{7,193},{8,256},... | collective-permute-start | bytes 454664 | tf_op jit(solution)/shard_map/ppermute | solution.py:255
  15.1 25.8 %collective-permute-start.1 = (bf16[592,128]{1,0:T(8,128)(2,1)S(1)}, bf16[592,128]{1,0:T(8,128)(2,1)S(1)}, u32[]{:S(2)}, u32[]{:S(2)}) collective-permute-start(bf16[592,128]{1,0:T(8,128)(2,1)S(1)} %pad_maximum_fusion.2), channel_id=1, source_target_pairs={{0,256},{1,257},{2,384},{3,385},{4,320},{5,321},{6,448},{7,449},{8... | collective-permute-start | bytes 454664 | tf_op jit(solution)/shard_map/ppermute | solution.py:256
  25.0 15.8 %collective-permute-start.2 = (bf16[592,128]{1,0:T(8,128)(2,1)S(1)}, bf16[592,128]{1,0:T(8,128)(2,1)S(1)}, u32[]{:S(2)}, u32[]{:S(2)}) collective-permute-start(bf16[592,128]{1,0:T(8,128)(2,1)S(1)} %pad_maximum_fusion.2), channel_id=1, source_target_pairs={{0,0},{1,1},{2,128},{3,129},{4,4},{5,5},{6,132},{7,133},{8,8},{9,9... | collective-permute-start | bytes 454664 | tf_op jit(solution)/shard_map/ppermute | solution.py:257
  40.9 11.2 %collective-permute-start.5 = (bf16[2,592,128]{2,1,0:T(8,128)(2,1)S(1)}, bf16[2,592,128]{2,1,0:T(8,128)(2,1)S(1)}, u32[]{:S(2)}, u32[]{:S(2)}) collective-permute-start(bf16[2,592,128]{2,1,0:T(8,128)(2,1)S(1)} %pad_maximum_fusion.refs_0_), channel_id=1, source_target_pairs={{0,16},{16,32},{32,48},{48,64},{64,80},{80,96},{96,112},{112,0},{1... | collective-permute-start | bytes 909320 | tf_op jit(solution)/shard_map/ppermute | solution.py:71
  42.8 11.2 %collective-permute-start.6 = (bf16[2,592,128]{2,1,0:T(8,128)(2,1)S(1)}, bf16[2,592,128]{2,1,0:T(8,128)(2,1)S(1)}, u32[]{:S(2)}, u32[]{:S(2)}) collective-permute-start(bf16[2,592,128]{2,1,0:T(8,128)(2,1)S(1)} %pad_maximum_fusion.refs_0_), channel_id=1, source_target_pairs={{0,112},{16,0},{32,16},{48,32},{64,48},{80,64},{96,80},{112,96},{1... | collective-permute-start | bytes 909320 | tf_op jit(solution)/shard_map/ppermute | solution.py:71
  52.1 10.3 %collective-permute-start.7 = (bf16[2,592,128]{2,1,0:T(8,128)(2,1)S(1)}, bf16[2,592,128]{2,1,0:T(8,128)(2,1)S(1)}, u32[]{:S(2)}, u32[]{:S(2)}) collective-permute-start(bf16[2,592,128]{2,1,0:T(8,128)(2,1)S(1)} %collective-permute-done.5.refs_1_), channel_id=1, source_target_pairs={{0,16},{16,32},{32,48},{48,64},{64,80},{80,96},{96,112},{112,0},{1... | collective-permute-start | bytes 909320 | tf_op jit(solution)/shard_map/ppermute | solution.py:71
  54.1 14.6 %collective-permute-start.8 = (bf16[2,592,128]{2,1,0:T(8,128)(2,1)S(1)}, bf16[2,592,128]{2,1,0:T(8,128)(2,1)S(1)}, u32[]{:S(2)}, u32[]{:S(2)}) collective-permute-start(bf16[2,592,128]{2,1,0:T(8,128)(2,1)S(1)} %collective-permute-done.6.refs_2_), channel_id=1, source_target_pairs={{0,112},{16,0},{32,16},{48,32},{64,48},{80,64},{96,80},{112,96},{1... | collective-permute-start | bytes 909320 | tf_op jit(solution)/shard_map/ppermute | solution.py:71
  62.5 20.6 %collective-permute-start.9 = (bf16[2,592,128]{2,1,0:T(8,128)(2,1)S(1)}, bf16[2,592,128]{2,1,0:T(8,128)(2,1)S(1)}, u32[]{:S(2)}, u32[]{:S(2)}) collective-permute-start(bf16[2,592,128]{2,1,0:T(8,128)(2,1)S(1)} %collective-permute-done.7.refs_3_), channel_id=1, source_target_pairs={{0,16},{16,32},{32,48},{48,64},{64,80},{80,96},{96,112},{112,0},{1... | collective-permute-start | bytes 909320 | tf_op jit(solution)/shard_map/ppermute | solution.py:71
  64.4 36.6 %collective-permute-start.13 = (bf16[512,896]{1,0:T(8,128)(2,1)S(1)}, bf16[512,896]{1,0:T(8,128)(2,1)S(1)}, u32[]{:S(2)}, u32[]{:S(2)}) collective-permute-start(bf16[512,896]{1,0:T(8,128)(2,1)S(1)} %collective-permute-done.4.refs_11_), channel_id=1, source_target_pairs={{0,1},{1,0},{2,3},{3,2},{4,5},{5,4},{6,7},{7,6},{8,9},{9,8},{10,11... | collective-permute-start | bytes 2752520 | tf_op jit(solution)/shard_map/ppermute | solution.py:67
  68.7 16.3 %collective-permute-start.10 = (bf16[2,592,128]{2,1,0:T(8,128)(2,1)S(1)}, bf16[2,592,128]{2,1,0:T(8,128)(2,1)S(1)}, u32[]{:S(2)}, u32[]{:S(2)}) collective-permute-start(bf16[2,592,128]{2,1,0:T(8,128)(2,1)S(1)} %collective-permute-done.8.refs_4_), channel_id=1, source_target_pairs={{0,112},{16,0},{32,16},{48,32},{64,48},{80,64},{96,80},{112,96},{1... | collective-permute-start | bytes 909320 | tf_op jit(solution)/shard_map/ppermute | solution.py:71
  73.5 16.1 %collective-permute-start.14 = (bf16[592,128]{1,0:T(8,128)(2,1)S(1)}, bf16[592,128]{1,0:T(8,128)(2,1)S(1)}, u32[]{:S(2)}, u32[]{:S(2)}) collective-permute-start(bf16[592,128]{1,0:T(8,128)(2,1)S(1)} %collective-permute-done.2), channel_id=1, source_target_pairs={{0,2},{2,0},{1,3},{3,1},{4,6},{6,4},{5,7},{7,5},{8,10},{10,8},{9,1... | collective-permute-start | bytes 454664 | tf_op jit(solution)/shard_map/ppermute | solution.py:67
  83.1 21.9 %collective-permute-start.11 = (bf16[592,128]{1,0:T(8,128)(2,1)S(1)}, bf16[592,128]{1,0:T(8,128)(2,1)S(1)}, u32[]{:S(2)}, u32[]{:S(2)}) collective-permute-start(bf16[592,128]{1,0:T(8,128)(2,1)S(1)} %slice_bitcast_fusion.2), channel_id=1, source_target_pairs={{0,16},{16,32},{32,48},{48,64},{64,80},{80,96},{96,112},{112,0},{1... | collective-permute-start | bytes 454664 | tf_op jit(solution)/shard_map/ppermute | solution.py:71
  85.0 19.9 %collective-permute-start.12 = (bf16[592,128]{1,0:T(8,128)(2,1)S(1)}, bf16[592,128]{1,0:T(8,128)(2,1)S(1)}, u32[]{:S(2)}, u32[]{:S(2)}) collective-permute-start(bf16[592,128]{1,0:T(8,128)(2,1)S(1)} %slice_bitcast_fusion.1), channel_id=1, source_target_pairs={{0,112},{16,0},{32,16},{48,32},{64,48},{80,64},{96,80},{112,96},{1... | collective-permute-start | bytes 454664 | tf_op jit(solution)/shard_map/ppermute | solution.py:71
  89.7 26.6 %copy-start.5 = (f32[864,432]{0,1:T(8,128)S(1)}, f32[864,432]{0,1:T(8,128)}, u32[]{:S(2)}) copy-start(f32[864,432]{0,1:T(8,128)} %param.9) | copy-start | bytes 4478980
  89.7 23.1 %collective-permute-start.15 = (bf16[2,592,128]{2,1,0:T(8,128)(2,1)S(1)}, bf16[2,592,128]{2,1,0:T(8,128)(2,1)S(1)}, u32[]{:S(2)}, u32[]{:S(2)}) collective-permute-start(bf16[2,592,128]{2,1,0:T(8,128)(2,1)S(1)} %pad_maximum_fusion.1.c0), channel_id=1, source_target_pairs={{0,4},{4,8},{8,12},{12,0},{1,5},{5,9},{9,13},{13,1},{2,6},{6,10},{... | collective-permute-start | bytes 909320 | tf_op jit(solution)/shard_map/ppermute | solution.py:71
  94.5 21.7 %collective-permute-start.16 = (bf16[2,592,128]{2,1,0:T(8,128)(2,1)S(1)}, bf16[2,592,128]{2,1,0:T(8,128)(2,1)S(1)}, u32[]{:S(2)}, u32[]{:S(2)}) collective-permute-start(bf16[2,592,128]{2,1,0:T(8,128)(2,1)S(1)} %pad_maximum_fusion.1.c0), channel_id=1, source_target_pairs={{0,8},{4,12},{8,0},{12,4},{1,9},{5,13},{9,1},{13,5},{2,10},{6,14},... | collective-permute-start | bytes 909320 | tf_op jit(solution)/shard_map/ppermute | solution.py:71
  101.0 15.2 %collective-permute-start.17 = (bf16[2,592,128]{2,1,0:T(8,128)(2,1)S(1)}, bf16[2,592,128]{2,1,0:T(8,128)(2,1)S(1)}, u32[]{:S(2)}, u32[]{:S(2)}) collective-permute-start(bf16[2,592,128]{2,1,0:T(8,128)(2,1)S(1)} %pad_maximum_fusion.1.c0), channel_id=1, source_target_pairs={{0,12},{4,0},{8,4},{12,8},{1,13},{5,1},{9,5},{13,9},{2,14},{6,2},{... | collective-permute-start | bytes 909320 | tf_op jit(solution)/shard_map/ppermute | solution.py:71
  107.7 13.7 %collective-permute-start.18 = (bf16[2,592,128]{2,1,0:T(8,128)(2,1)S(1)}, bf16[2,592,128]{2,1,0:T(8,128)(2,1)S(1)}, u32[]{:S(2)}, u32[]{:S(2)}) collective-permute-start(bf16[2,592,128]{2,1,0:T(8,128)(2,1)S(1)} %get-tuple-element.43), channel_id=1, source_target_pairs={{0,4},{4,8},{8,12},{12,0},{1,5},{5,9},{9,13},{13,1},{2,6},{6,10},{... | collective-permute-start | bytes 909320 | tf_op jit(solution)/shard_map/ppermute | solution.py:71
  109.7 15.6 %collective-permute-start.19 = (bf16[2,592,128]{2,1,0:T(8,128)(2,1)S(1)}, bf16[2,592,128]{2,1,0:T(8,128)(2,1)S(1)}, u32[]{:S(2)}, u32[]{:S(2)}) collective-permute-start(bf16[2,592,128]{2,1,0:T(8,128)(2,1)S(1)} %get-tuple-element.44), channel_id=1, source_target_pairs={{0,8},{4,12},{8,0},{12,4},{1,9},{5,13},{9,1},{13,5},{2,10},{6,14},... | collective-permute-start | bytes 909320 | tf_op jit(solution)/shard_map/ppermute | solution.py:71
  112.8 15.1 %collective-permute-start.20 = (bf16[2,592,128]{2,1,0:T(8,128)(2,1)S(1)}, bf16[2,592,128]{2,1,0:T(8,128)(2,1)S(1)}, u32[]{:S(2)}, u32[]{:S(2)}) collective-permute-start(bf16[2,592,128]{2,1,0:T(8,128)(2,1)S(1)} %get-tuple-element.45), channel_id=1, source_target_pairs={{0,12},{4,0},{8,4},{12,8},{1,13},{5,1},{9,5},{13,9},{2,14},{6,2},{... | collective-permute-start | bytes 909320 | tf_op jit(solution)/shard_map/ppermute | solution.py:71
  128.2 40.6 %collective-permute-start.21 = (bf16[2,512,896]{2,1,0:T(8,128)(2,1)}, bf16[2,512,896]{2,1,0:T(8,128)(2,1)S(1)}, u32[]{:S(2)}, u32[]{:S(2)}) collective-permute-start(bf16[2,512,896]{2,1,0:T(8,128)(2,1)} %get-tuple-element.47), channel_id=1, source_target_pairs={{0,1},{1,0},{2,3},{3,2},{4,5},{5,4},{6,7},{7,6},{8,9},{9,8},{10,11... | collective-permute-start | bytes 5505032 | tf_op jit(solution)/shard_map/ppermute | solution.py:67
  131.6 15.9 %collective-permute-start.22 = (bf16[1024,128]{1,0:T(8,128)(2,1)S(1)}, bf16[1024,128]{1,0:T(8,128)(2,1)S(1)}, u32[]{:S(2)}, u32[]{:S(2)}) collective-permute-start(bf16[1024,128]{1,0:T(8,128)(2,1)S(1)} %get-tuple-element.46), channel_id=1, source_target_pairs={{0,2},{2,0},{1,3},{3,1},{4,6},{6,4},{5,7},{7,5},{8,10},{10,8},{9,1... | collective-permute-start | bytes 786440 | tf_op jit(solution)/shard_map/ppermute | solution.py:67
  148.2 0.7 collective-permute-start.24
  149.8 44.8 %all-to-all-start = ((bf16[16,160,128]{2,1,0:T(8,128)(2,1)}), bf16[16,160,128]{2,1,0:T(8,128)(2,1)}, u32[]{:S(2)}, u32[]{:S(2)}) async-start(bf16[16,160,128]{2,1,0:T(8,128)(2,1)} %broadcast_in_dim.3), calls=%async_computation | async-start | bytes 1310720 | tf_op jit(solution)/shard_map/all_to_all | solution.py:304
  171.4 35.4 %collective-permute-start.23 = (bf16[512,896]{1,0:T(8,128)(2,1)}, bf16[512,896]{1,0:T(8,128)(2,1)}, u32[]{:S(2)}, u32[]{:S(2)}) collective-permute-start(bf16[512,896]{1,0:T(8,128)(2,1)} %fusion), channel_id=1, source_target_pairs={{0,128},{128,0},{1,129},{129,1},{2,130},{130,2},{3,131},{131,3},{4... | collective-permute-start | bytes 2752520 | tf_op jit(solution)/shard_map/ppermute | solution.py:67
  173.9 13.5 %collective-permute-start.25 = (bf16[2,432,128]{2,1,0:T(8,128)(2,1)S(1)}, bf16[2,432,128]{2,1,0:T(8,128)(2,1)S(1)}, u32[]{:S(2)}, u32[]{:S(2)}) collective-permute-start(bf16[2,432,128]{2,1,0:T(8,128)(2,1)S(1)} %copy-done.8), channel_id=1, source_target_pairs={{0,4},{4,8},{8,12},{12,0},{1,5},{5,9},{9,13},{13,1},{2,6},{6,10},{... | collective-permute-start | bytes 663560 | tf_op jit(solution)/shard_map/ppermute | solution.py:71
  180.9 10.2 %collective-permute-start.26 = (bf16[2,432,128]{2,1,0:T(8,128)(2,1)S(1)}, bf16[2,432,128]{2,1,0:T(8,128)(2,1)S(1)}, u32[]{:S(2)}, u32[]{:S(2)}) collective-permute-start(bf16[2,432,128]{2,1,0:T(8,128)(2,1)S(1)} %copy-done.8), channel_id=1, source_target_pairs={{0,8},{4,12},{8,0},{12,4},{1,9},{5,13},{9,1},{13,5},{2,10},{6,14},... | collective-permute-start | bytes 663560 | tf_op jit(solution)/shard_map/ppermute | solution.py:71
  185.5 8.5 %collective-permute-start.27 = (bf16[2,432,128]{2,1,0:T(8,128)(2,1)S(1)}, bf16[2,432,128]{2,1,0:T(8,128)(2,1)S(1)}, u32[]{:S(2)}, u32[]{:S(2)}) collective-permute-start(bf16[2,432,128]{2,1,0:T(8,128)(2,1)S(1)} %copy-done.8), channel_id=1, source_target_pairs={{0,12},{4,0},{8,4},{12,8},{1,13},{5,1},{9,5},{13,9},{2,14},{6,2},{... | collective-permute-start | bytes 663560 | tf_op jit(solution)/shard_map/ppermute | solution.py:71
  200.8 6.0 %collective-permute-start.28 = (bf16[2,320,432]{2,1,0:T(8,128)(2,1)S(1)}, bf16[2,320,432]{2,1,0:T(8,128)(2,1)S(1)}, u32[]{:S(2)}, u32[]{:S(2)}) collective-permute-start(bf16[2,320,432]{2,1,0:T(8,128)(2,1)S(1)} %get-tuple-element.56), channel_id=1, source_target_pairs={{0,1},{1,0},{2,3},{3,2},{4,5},{5,4},{6,7},{7,6},{8,9},{9,8},{10,11... | collective-permute-start | bytes 1658888 | tf_op jit(solution)/shard_map/ppermute | solution.py:67
  206.9 10.8 %collective-permute-start.29 = (bf16[320,432]{1,0:T(8,128)(2,1)S(1)}, bf16[320,432]{1,0:T(8,128)(2,1)S(1)}, u32[]{:S(2)}, u32[]{:S(2)}) collective-permute-start(bf16[320,432]{1,0:T(8,128)(2,1)S(1)} %fusion.1), channel_id=1, source_target_pairs={{0,128},{128,0},{1,129},{129,1},{2,130},{130,2},{3,131},{131,3},{4... | collective-permute-start | bytes 829448 | tf_op jit(solution)/shard_map/ppermute | solution.py:67
  (15 other events, 79.1 us)
